TPU v7x, 32 devices: a whole 2x2x4 slice. The times are simulated.
32 devices in a mesh: freq: 2 (over y), brick: 4 (over z), orb: 4 (over x, core).
Axes of the slice: x: 2, y: 2, z: 4, core: 2. Of those that a mesh axis runs over, the one named last changes fastest.
Arguments:
- orbitals: float32 [16, 24, 8192], P(None, 'brick'), may hold values from -6 to 6
- potential: float32 [24, 8192], P('brick'), may hold values from 0.5 to 2.5
- perturb: float32 [24, 8192], P('brick'), may hold values from 0.1 to 2
- energies: float32 [16], P('orb'), may hold values from -0.4 to 0
- omega: float32 [2], P('freq'), parts along dimension 0, may hold values from 0.05 to 1
Outputs:
- response: float32 [32, 24, 8192], P(('freq', 'orb'), 'brick'), parts along dimension 0
- induced: float32 [48, 8192], P(('freq', 'brick'), 'orb'), parts along dimension 0
There are 2 independent parts, one for each index of `freq`. A program takes and returns all parts, laid end to end along the dimension named above; an argument that names none is the same for every part. Nothing has to cross between parts.
All inputs are finite; a program needn't handle non-finite values.
Results may differ from a plain program's by a relative error of at most 0.00011.
Values sent between devices are 32-bit elements; how exact they have to be, the bound alone decides.
No kernel may reach another device: no remote copies, remote signals or barrier semaphores. Data moves between devices by JAX's collectives and lax.ppermute only.
A program may use at most 128 MiB of HBM per device.

v0:
```python
import functools
import jax
import jax.numpy as jnp
from jax import lax
from jax.experimental import pallas as pl
from jax.experimental.pallas import tpu as pltpu
from jax.sharding import PartitionSpec as P

NY = 32
LANES = 128
SUB = 8

COEFFS = (
    -5369.0 / 1800.0,
    12.0 / 7.0,
    -15.0 / 56.0,
    10.0 / 189.0,
    -1.0 / 112.0,
    2.0 / 825.0,
    -1.0 / 5544.0,
)
SCREEN = 0.25
HIGHEST = lax.Precision.HIGHEST
VMEM_LIMIT = 48 * 1024 * 1024
SMEM = pl.BlockSpec(memory_space=pltpu.SMEM)
VMEM = pl.BlockSpec(memory_space=pltpu.VMEM)
f32 = jnp.float32


def call(kernel, outs, scratch, smem, *args):
    return pl.pallas_call(
        kernel,
        out_shape=[jax.ShapeDtypeStruct(s, f32) for s in outs],
        in_specs=[SMEM] * smem + [VMEM] * (len(args) - smem),
        out_specs=[VMEM] * len(outs),
        scratch_shapes=[pltpu.VMEM(s, f32) for s in scratch],
        compiler_params=pltpu.CompilerParams(vmem_limit_bytes=VMEM_LIMIT),
    )(*args)


def parts_of(array, axis):
    size = lax.axis_size(axis)
    if size > 4:
        return [lax.psum(array, axis)]
    rotated = [
        lax.ppermute(array, axis, [(i, (i + k) % size) for i in range(size)]) for k in range(1, size)
    ]
    return [array] + rotated


def shifted(array, axis, step):
    size = lax.axis_size(axis)
    return lax.ppermute(array, axis, [(i, (i + step) % size) for i in range(size)])


def add_all(refs):
    total = refs[0][...]
    for ref in refs[1:]:
        total = total + ref[...]
    return total


def column(matrix, index):
    lane = lax.broadcasted_iota(jnp.int32, matrix.shape, 1)
    picked = jnp.sum(jnp.where(lane == index, matrix, 0.0), axis=1, keepdims=True)
    return jnp.broadcast_to(picked, (matrix.shape[0], LANES))


def blocks(plane):
    return plane.reshape(-1, NY, LANES)


def gram_kernel(shape, rows_ref, perturb_ref, planes_ref, gram_ref):
    norb, layers, halves = shape
    groups = norb // SUB
    tiles = NY * halves
    step = 16

    def layer(z, total):
        for c0 in range(0, tiles, step):
            pieces = []
            for t in range(groups):
                base = ((z * groups + t) * tiles + c0) * SUB
                pieces.append(
                    jnp.concatenate(
                        [rows_ref[pl.ds(base + c * SUB, SUB), :] for c in range(step)], axis=1
                    )
                )
            field = jnp.concatenate(pieces, axis=0)
            weight = perturb_ref[pl.ds(z, 1), c0 * LANES : (c0 + step) * LANES]
            both = jnp.concatenate([field, field * weight], axis=0)
            high = both.astype(jnp.bfloat16)
            low = (both - high.astype(f32)).astype(jnp.bfloat16)
            left = jnp.concatenate([high, low], axis=0)
            right = jnp.concatenate([high[:norb], low[:norb]], axis=0)
            total = total + lax.dot_general(
                left, right, (((1,), (1,)), ((), ())), preferred_element_type=f32
            )
        for t in range(groups):
            base = (z * groups + t) * tiles * SUB
            for s in range(SUB):
                for h in range(halves):
                    for q in range(NY // SUB):
                        start = base + (q * SUB * halves + h) * SUB + s
                        planes_ref[t * SUB + s, z, h * (NY // SUB) + q] = rows_ref[
                            pl.ds(start, SUB, stride=SUB * halves), :
                        ]
        return total

    total = lax.fori_loop(0, layers, layer, jnp.zeros((4 * norb, 2 * norb), f32))
    total = total[: 2 * norb] + total[2 * norb :]
    gram_ref[...] = total[:, :norb] + total[:, norb:]


def small_matrices(norb, gram_refs, ncell):
    total = add_all(gram_refs)
    overlap, weighted = total[:norb], total[norb:]
    twice = jnp.dot(overlap, weighted, precision=HIGHEST, preferred_element_type=f32) * (1.0 / ncell)
    return overlap, weighted, twice


def combine(layers, group, norb, planes_ref, coef_ref, start, finish):
    def layer(z, carry):
        sums = [start(n, z) for n in range(group)]
        for m in range(norb):
            field = planes_ref[m, z]
            for n in range(group):
                sums[n] = sums[n] + field * coef_ref[pl.ds(n * norb + m, 1), :]
        for n in range(group):
            finish(n, z, sums[n])
        return carry

    lax.fori_loop(0, layers, layer, 0)


def inner_kernel(shape, ncell, planes_ref, perturb_ref, *refs):
    norb, layers, group, parts = shape
    gram_refs, inner_ref, coef_ref = refs[:parts], refs[parts], refs[parts + 1]
    first = lax.axis_index("orb") * group
    overlap, weighted, twice = small_matrices(norb, gram_refs, ncell)
    coefs = (2.0 * weighted - twice) * (1.0 / ncell)
    for n in range(group):
        coef_ref[n * norb : (n + 1) * norb, :] = column(coefs, first + n)

    def start(n, z):
        return -(perturb_ref[z] * planes_ref[first + n, z])

    def finish(n, z, value):
        inner_ref[n, z] = value

    combine(layers, group, norb, planes_ref, coef_ref, start, finish)


def roll_x(halves_list, amount):
    count = len(halves_list)
    lane = lax.broadcasted_iota(jnp.int32, halves_list[0].shape, 1)
    turned = [pltpu.roll(v, amount % LANES, 1) for v in halves_list]
    if amount > 0:
        return [jnp.where(lane >= amount, turned[h], turned[(h - 1) % count]) for h in range(count)]
    return [
        jnp.where(lane < LANES + amount, turned[h], turned[(h + 1) % count]) for h in range(count)
    ]


def roll_y(value, amount):
    return pltpu.roll(value, amount % NY, 0)


def local_kernel(shape, ncell, shift_ref, planes_ref, perturb_ref, potential_ref, inner_ref, *refs):
    norb, layers, group, parts, halves = shape
    gram_refs = refs[:parts]
    source_ref, partial_ref, overlap_ref, along_ref, square_ref, coef_ref = refs[parts:]
    first = lax.axis_index("orb") * group
    overlap, weighted, twice = small_matrices(norb, gram_refs, ncell)
    for m in range(norb):
        overlap_ref[m] = column(overlap, m)
    for n in range(group):
        rows = slice(n * norb, (n + 1) * norb)
        coef_ref[rows, :] = column(weighted * (1.0 / ncell), first + n)
        along_ref[rows, :] = column(twice - weighted, first + n)
    square_ref[...] = jnp.zeros_like(square_ref)

    def start(n, z):
        return -(perturb_ref[z] * planes_ref[first + n, z])

    def finish(n, z, value):
        source_ref[n, z] = value
        square_ref[n] += jnp.sum(value * value, axis=0)

    combine(layers, group, norb, planes_ref, coef_ref, start, finish)

    for n in range(group):
        def layer(z, carry):
            plane = blocks(inner_ref[n, z])
            sheets = [plane[h] for h in range(halves)]
            sums = [(3.0 * COEFFS[0]) * v for v in sheets]
            for k in range(1, 7):
                right, left = roll_x(sheets, k), roll_x(sheets, -k)
                for h in range(halves):
                    around = right[h] + left[h] + roll_y(sheets[h], k) + roll_y(sheets[h], -k)
                    sums[h] = sums[h] + COEFFS[k] * around
            total = jnp.stack(sums).reshape(inner_ref.shape[2:])
            shift = potential_ref[z] + shift_ref[n]
            partial_ref[n, z] = shift * inner_ref[n, z] - 0.5 * total
            return carry

        lax.fori_loop(0, layers, layer, 0)
        for z in range(layers):
            total = None
            for other in range(layers):
                k = abs(other - z)
                if k == 0 or k > 6:
                    continue
                term = (-0.5 * COEFFS[k]) * inner_ref[n, other]
                total = term if total is None else total + term
            if total is not None:
                partial_ref[n, z] += total


def image_kernel(shape, planes_ref, inner_ref, partial_ref, square_ref, before_ref, after_ref, applied_ref, sums_ref, acc_ref):
    norb, layers, group = shape
    acc_ref[...] = jnp.zeros_like(acc_ref)
    for n in range(group):
        for z in range(layers):
            total = partial_ref[n, z]
            for j in range(layers):
                k = z + layers - j
                if k <= 6:
                    total = total + (-0.5 * COEFFS[k]) * before_ref[n, j]
                k = j + layers - z
                if k <= 6:
                    total = total + (-0.5 * COEFFS[k]) * after_ref[n, j]
            applied_ref[n, z] = total

    def layer(z, carry):
        fields = [applied_ref[n, z] for n in range(group)]
        for n in range(group):
            acc_ref[group * norb + n] += jnp.sum(fields[n] * inner_ref[n, z], axis=0)
        for m in range(norb):
            orbital = planes_ref[m, z]
            for n in range(group):
                acc_ref[n * norb + m] += jnp.sum(orbital * fields[n], axis=0)
        return carry

    lax.fori_loop(0, layers, layer, 0)
    count = group * norb + group
    sums_ref[:count, :] = jnp.sum(acc_ref[:count], axis=1)
    sums_ref[count : count + group, :] = jnp.sum(square_ref[...], axis=1)
    if sums_ref.shape[0] > count + group:
        sums_ref[count + group :, :] = jnp.zeros((sums_ref.shape[0] - count - group, LANES), f32)


def spread(value):
    return jnp.broadcast_to(jnp.sum(value, axis=1, keepdims=True), value.shape)


def residual_kernel(shape, ncell, planes_ref, source_ref, applied_ref, overlap_ref, along_ref, *refs):
    norb, layers, group, parts = shape
    sums_refs = refs[:parts]
    ahead_ref, plain_ref, numbers_ref, coef_ref, step_ref = refs[parts:]
    total = spread(add_all(sums_refs))
    count = group * norb
    curve = total[count : count + group]
    norm = total[count + group : count + 2 * group]
    step = norm / curve
    numbers_ref[:group, :] = norm
    numbers_ref[group : 2 * group, :] = curve
    numbers_ref[2 * group : 3 * group, :] = step
    step_ref[...] = step
    for n in range(group):
        rows = slice(n * norb, (n + 1) * norb)
        product = total[rows]
        alpha = step[n : n + 1]
        again = jnp.zeros((norb, LANES), f32)
        for m in range(norb):
            again = again + overlap_ref[m] * product[m : m + 1]
        left = along_ref[rows, :] - alpha * (product - again * (1.0 / ncell))
        plain_ref[rows, :] = alpha * product * (1.0 / ncell)
        coef_ref[rows, :] = (alpha * product - left) * (1.0 / ncell)

    def start(n, z):
        return source_ref[n, z] - step_ref[n : n + 1, :] * applied_ref[n, z]

    def finish(n, z, value):
        ahead_ref[n, z] = value

    combine(layers, group, norb, planes_ref, coef_ref, start, finish)


def second_kernel(shape, shift_ref, planes_ref, potential_ref, source_ref, applied_ref, ahead_ref, plain_ref, numbers_ref, residual_ref, acc_ref):
    norb, layers, group, halves = shape
    acc_ref[...] = jnp.zeros_like(acc_ref)

    def start(n, z):
        alpha = numbers_ref[2 * group + n : 2 * group + n + 1, :]
        return source_ref[n, z] - alpha * applied_ref[n, z]

    def finish(n, z, value):
        residual_ref[n, z] = value
        acc_ref[2 * group + n] += jnp.sum(value * value, axis=0)

    combine(layers, group, norb, planes_ref, plain_ref, start, finish)

    for n in range(group):
        def layer(z, carry):
            whole = ahead_ref[n, z]
            plane = blocks(whole)
            sheets = [plane[h] for h in range(halves)]
            sums = [(-1.5 * COEFFS[0]) * v for v in sheets]
            for k in range(1, 7):
                right = roll_x(sheets, k)
                for h in range(halves):
                    sums[h] = sums[h] - COEFFS[k] * (right[h] + roll_y(sheets[h], k))
            total = jnp.stack(sums).reshape(whole.shape)
            total = total + (potential_ref[z] + shift_ref[n]) * whole
            acc_ref[n] += jnp.sum(whole * total, axis=0)
            acc_ref[group + n] += jnp.sum(whole * applied_ref[n, z], axis=0)
            return carry

        lax.fori_loop(0, layers, layer, 0)
        for z in range(layers - 1):
            total = None
            for other in range(z + 1, min(layers, z + 7)):
                term = -COEFFS[other - z] * ahead_ref[n, other]
                total = term if total is None else total + term
            acc_ref[n] += jnp.sum(ahead_ref[n, z] * total, axis=0)


def pairs_kernel(shape, ahead_ref, after_ref, acc_ref, sums_ref):
    layers, group = shape
    sums_ref[...] = jnp.sum(acc_ref[...], axis=1)
    for n in range(group):
        total = None
        for z in range(layers):
            line = None
            for j in range(layers):
                k = j + layers - z
                if k <= 6:
                    term = -COEFFS[k] * after_ref[n, j]
                    line = term if line is None else line + term
            if line is not None:
                line = line * ahead_ref[n, z]
                total = line if total is None else total + line
        sums_ref[n : n + 1, :] += jnp.sum(jnp.sum(total, axis=0), axis=0, keepdims=True)


def density_kernel(shape, planes_ref, source_ref, residual_ref, numbers_ref, *refs):
    layers, group, parts, halves, members, width, margin = shape
    sums_refs = refs[:parts]
    cuts_ref, scales_ref, ring_ref = refs[parts:]
    first = lax.axis_index("orb")
    total = spread(add_all(sums_refs))
    norm, curve, alpha = (numbers_ref[i * group : (i + 1) * group, :] for i in range(3))
    squares, cross, bend = total[2 * group : 3 * group], total[group : 2 * group], total[:group]
    beta = squares / norm
    bend = bend + 2.0 * beta * cross + beta * beta * curve
    second = squares / bend
    scales_ref[:group, :] = alpha + second * beta
    scales_ref[group : 2 * group, :] = second

    def layer(z, carry):
        total = jnp.zeros(planes_ref.shape[2:], f32)
        for n in range(group):
            field = scales_ref[n : n + 1, :] * source_ref[n, z]
            field = field + scales_ref[group + n : group + n + 1, :] * residual_ref[n, z]
            total = total + field * planes_ref[first * group + n, z]
        total = blocks(4.0 * total)
        for h in range(halves):
            ring_ref[z, h, SUB : SUB + NY, :] = total[h]
            ring_ref[z, h, :SUB, :] = total[h, NY - SUB :]
            ring_ref[z, h, SUB + NY :, :] = total[h, :SUB]
        return carry

    lax.fori_loop(0, layers, layer, 0)
    for k in range(members):
        owner = lax.rem(first + k, members)
        for z in range(layers):
            for h in range(halves):
                cuts_ref[k, z, h] = ring_ref[z, h, pl.ds(owner * width + SUB - margin, width + 2 * margin), :]


def response_kernel(shape, source_ref, residual_ref, scales_ref, response_ref):
    layers, group, halves = shape
    tiles = NY * halves

    def layer(z, carry):
        for n in range(group):
            field = scales_ref[n : n + 1, :] * source_ref[n, z]
            field = field + scales_ref[group + n : group + n + 1, :] * residual_ref[n, z]
            for h in range(halves):
                for q in range(NY // SUB):
                    start = (z * tiles + q * SUB * halves + h) * group + n
                    response_ref[pl.ds(start, SUB, stride=group * halves), :] = field[h * (NY // SUB) + q]
        return carry

    lax.fori_loop(0, layers, layer, 0)


def gather_kernel(cuts_ref, *refs):
    total = cuts_ref[0]
    for ref in refs[:-1]:
        total = total + ref[...]
    refs[-1][...] = total


def jacobi_kernel(shape, dense_ref, before_ref, after_ref, induced_ref):
    layers, halves, width, margin = shape
    scale = 1.0 / (6.0 + SCREEN)
    dense = [[before_ref[j, h] for h in range(halves)] for j in range(2)]
    dense = dense + [[dense_ref[z, h] for h in range(halves)] for z in range(layers)]
    dense = dense + [[after_ref[j, h] for h in range(halves)] for j in range(2)]
    field = [[scale * v for v in sheet] for sheet in dense]
    rows = width + 2 * margin

    def up(value):
        return pltpu.roll(value, 1, 0)

    def down(value):
        return pltpu.roll(value, rows - 1, 0)

    for sweep in range(2):
        fresh = []
        for z in range(1, len(field) - 1):
            right, left = roll_x(field[z], 1), roll_x(field[z], -1)
            sheet = []
            for h in range(halves):
                value = dense[z][h] + field[z - 1][h] + field[z + 1][h] + right[h] + left[h]
                value = value + up(field[z][h]) + down(field[z][h])
                sheet.append(scale * value)
            fresh.append(sheet)
        field, dense = fresh, dense[1:-1]
    for z in range(layers):
        for h in range(halves):
            for y in range(width):
                c = y * halves + h
                induced_ref[z : z + 1, c * LANES : (c + 1) * LANES] = field[z][h][margin + y : margin + y + 1]


def per_device(orbitals, potential, perturb, energies, omega):
    norb, layers, columns = orbitals.shape
    group = energies.shape[0]
    bricks, members = lax.axis_size("brick"), lax.axis_size("orb")
    ncell = layers * bricks * columns
    halves = columns // NY // LANES
    tiles = columns // LANES
    spots = tiles // SUB
    rows = orbitals.transpose(1, 0, 2).reshape(layers, norb // SUB, SUB, tiles, LANES)
    rows = rows.transpose(0, 1, 3, 2, 4).reshape(layers * norb * tiles, LANES)

    def as_planes(array):
        array = array.reshape(layers, NY, halves, LANES).transpose(0, 2, 1, 3)
        return array.reshape(layers, spots, SUB, LANES)

    shift = omega[0] - energies
    own = (group, layers, spots, SUB, LANES)
    flat = (group * norb, LANES)

    planes, gram = call(
        functools.partial(gram_kernel, (norb, layers, halves)),
        [(norb, layers, spots, SUB, LANES), (2 * norb, norb)],
        [],
        0,
        rows,
        perturb,
    )
    grams = parts_of(gram, "brick")
    perturb_planes, potential_planes = as_planes(perturb), as_planes(potential)
    (inner,) = call(
        functools.partial(inner_kernel, (norb, layers, group, len(grams)), ncell),
        [own],
        [flat],
        0,
        planes,
        perturb_planes,
        *grams,
    )
    before, after = shifted(inner, "brick", 1), shifted(inner, "brick", -1)
    source, partial, overlap, along, square = call(
        functools.partial(local_kernel, (norb, layers, group, len(grams), halves), ncell),
        [own, own, (norb, norb, LANES), flat, (group, SUB, LANES)],
        [flat],
        1,
        shift,
        planes,
        perturb_planes,
        potential_planes,
        inner,
        *grams,
    )
    height = -(-(group * norb + 2 * group) // SUB) * SUB
    applied, sums = call(
        functools.partial(image_kernel, (norb, layers, group)),
        [own, (height, LANES)],
        [(group * norb + group, SUB, LANES)],
        0,
        planes,
        inner,
        partial,
        square,
        before,
        after,
    )
    sums = parts_of(sums, "brick")
    ahead, plain, numbers = call(
        functools.partial(residual_kernel, (norb, layers, group, len(sums)), ncell),
        [own, flat, (3 * group, LANES)],
        [flat, (group, LANES)],
        0,
        planes,
        source,
        applied,
        overlap,
        along,
        *sums,
    )
    after = shifted(ahead, "brick", -1)
    residual, acc = call(
        functools.partial(second_kernel, (norb, layers, group, halves)),
        [own, (3 * group, SUB, LANES)],
        [],
        1,
        shift,
        planes,
        potential_planes,
        source,
        applied,
        ahead,
        plain,
        numbers,
    )
    (sums,) = call(
        functools.partial(pairs_kernel, (layers, group)),
        [(3 * group, LANES)],
        [],
        0,
        ahead,
        after,
        acc,
    )
    sums = parts_of(sums, "brick")
    width = NY // members
    margin = 4 if width % SUB == 0 else 2
    cut = (layers, halves, width + 2 * margin, LANES)
    cuts, scales = call(
        functools.partial(density_kernel, (layers, group, len(sums), halves, members, width, margin)),
        [(members,) + cut, (2 * group, LANES)],
        [(layers, halves, NY + 2 * SUB, LANES)],
        0,
        planes,
        source,
        residual,
        numbers,
        *sums,
    )
    others = [shifted(cuts[k], "orb", k) for k in range(1, members)]
    (response,) = call(
        functools.partial(response_kernel, (layers, group, halves)),
        [(layers * tiles * group, LANES)],
        [],
        0,
        source,
        residual,
        scales,
    )
    (dense,) = call(gather_kernel, [cut], [], 0, cuts, *others)
    before = shifted(dense[layers - 2 :], "brick", 1)
    after = shifted(dense[:2], "brick", -1)
    (induced,) = call(
        functools.partial(jacobi_kernel, (layers, halves, width, margin)),
        [(layers, width * halves * LANES)],
        [],
        0,
        dense,
        before,
        after,
    )
    response = response.reshape(layers, tiles, group, LANES).transpose(2, 0, 1, 3)
    return response.reshape(group, layers, columns), induced


def solution(mesh):
    placed = (P(None, "brick", None), P("brick", None), P("brick", None), P("orb"), P("freq"))
    return jax.shard_map(
        per_device,
        mesh=mesh,
        in_specs=placed,
        out_specs=(P(("freq", "orb"), "brick", None), P(("freq", "brick"), "orb")),
        check_vma=False,
    )
```

profile of v0, /device:TPU:0, one launch (start us, length us, event | category | flops | bytes accessed | tf_op | source)
XLA Modules:
  0.0 109.1 jit_solution(10611661461638753084)
XLA Ops:
  0.6 0.0 copy-start.3
  0.6 0.9 copy-done.3
  1.6 0.0 copy-start.4
  1.6 5.4 %shard_map.68 = (f32[16,6,8,8,128]{4,3,2,1,0:T(8,128)S(1)}, f32[32,16]{1,0:T(8,128)S(1)}) custom-call(f32[6144,128]{1,0:T(8,128)} %bitcast.30, f32[6,8192]{1,0:T(8,128)S(1)} %copy-done.3), custom_call_target="tpu_custom_call" | custom-call | tf_op jit(solution)/shard_map/pallas_call | solution.py:31
  7.0 0.0 copy-start
  7.0 0.0 copy-start.5
  7.0 5.1 %collective-permute-start.2 = (f32[32,16]{1,0:T(8,128)S(1)}, f32[32,16]{1,0:T(8,128)S(1)}, u32[]{:S(2)}, u32[]{:S(2)}) collective-permute-start(f32[32,16]{1,0:T(8,128)S(1)} %get-tuple-element.19.refs_0_), channel_id=1, source_target_pairs={{0,12},{4,0},{8,4},{12,8},{1,13},{5,1},{9,5},{13,9},{2,14},{6,2},{... | collective-permute-start | bytes 6152 | tf_op jit(solution)/shard_map/ppermute | solution.py:46
  12.2 0.0 collective-permute-start.1
  12.2 1.0 collective-permute-start
  13.2 0.0 copy-done.4
  13.2 0.9 reshape.30
  14.0 0.9 copy.7
  15.0 0.0 collective-permute-done.2.refs_3_
  15.0 1.8 %collective-permute-done.1.refs_2_ = f32[32,16]{1,0:T(8,128)S(1)} collective-permute-done((f32[32,16]{1,0:T(8,128)S(1)}, f32[32,16]{1,0:T(8,128)S(1)}, u32[]{:S(2)}, u32[]{:S(2)}) %collective-permute-start.1) | collective-permute-done | bytes 2080 | tf_op jit(solution)/shard_map/ppermute | solution.py:46
  16.8 0.9 collective-permute-done.refs_1_
  17.7 2.2 %shard_map.69.inner_ref = f32[4,6,8,8,128]{4,3,2,1,0:T(8,128)} custom-call(f32[16,6,8,8,128]{4,3,2,1,0:T(8,128)S(1)} %get-tuple-element.18.planes_ref, f32[6,8,8,128]{3,2,1,0:T(8,128)S(1)} %bitcast.28, f32[32,16]{1,0:T(8,128)S(1)} %get-tuple-element.19.refs_0_, f32[32,16]{1,0:T(8,128)S(1)} %collective-permute-done.refs_1_, ...), custom_call_target="tpu_custom_call" | custom-call | tf_op jit(solution)/shard_map/pallas_call | solution.py:31
  19.9 0.6 collective-permute-start.4
  20.4 1.5 %collective-permute-start.3 = (f32[4,6,8,8,128]{4,3,2,1,0:T(8,128)}, f32[4,6,8,8,128]{4,3,2,1,0:T(8,128)}, u32[]{:S(2)}, u32[]{:S(2)}) collective-permute-start(f32[4,6,8,8,128]{4,3,2,1,0:T(8,128)} %shard_map.69.inner_ref), channel_id=1, source_target_pairs={{0,4},{4,8},{8,12},{12,0},{1,5},{5,9},{9,13},{13,1},{2,6},{6,10},{... | collective-permute-start | bytes 2359304 | tf_op jit(solution)/shard_map/ppermute | solution.py:53
  22.6 1.8 %reshape.32 = f32[6,32,2,128]{3,2,1,0:T(2,128)} reshape(f32[6,8192]{1,0:T(8,128)} %param.6) | data formatting | bytes 393216 | tf_op jit(solution)/shard_map/reshape | solution.py:451
  24.4 0.9 copy.8
  25.3 0.0 copy-done.5
  25.3 7.0 %shard_map.70 = (f32[4,6,8,8,128]{4,3,2,1,0:T(8,128)S(1)}, f32[4,6,8,8,128]{4,3,2,1,0:T(8,128)S(1)}, f32[16,16,128]{2,1,0:T(8,128)S(1)}, f32[64,128]{1,0:T(8,128)S(1)}, f32[4,8,128]{2,1,0:T(8,128)S(1)}) custom-call(f32[4]{0:T(128)S(1)} %broadcast_subtract_fusion.shift_ref, f32[16,6,8,8,128]{4,3,2,1,0:T(8,128)S(1)} %get-tuple-element.18.planes_ref, ...), custom_call_target="tpu_custom_call" | custom-call | tf_op jit(solution)/shard_map/pallas_call | solution.py:31
  32.3 0.0 copy-done
  32.4 8.0 %collective-permute-done.4.after_ref = f32[4,6,8,8,128]{4,3,2,1,0:T(8,128)} collective-permute-done((f32[4,6,8,8,128]{4,3,2,1,0:T(8,128)}, f32[4,6,8,8,128]{4,3,2,1,0:T(8,128)}, u32[]{:S(2)}, u32[]{:S(2)}) %collective-permute-start.4) | collective-permute-done | bytes 786464 | tf_op jit(solution)/shard_map/ppermute | solution.py:53
  40.4 14.9 %collective-permute-done.3.before_ref = f32[4,6,8,8,128]{4,3,2,1,0:T(8,128)} collective-permute-done((f32[4,6,8,8,128]{4,3,2,1,0:T(8,128)}, f32[4,6,8,8,128]{4,3,2,1,0:T(8,128)}, u32[]{:S(2)}, u32[]{:S(2)}) %collective-permute-start.3) | collective-permute-done | bytes 786464 | tf_op jit(solution)/shard_map/ppermute | solution.py:53
  55.3 0.0 copy-start.1
  55.3 4.2 %shard_map.71 = (f32[4,6,8,8,128]{4,3,2,1,0:T(8,128)S(1)}, f32[72,128]{1,0:T(8,128)S(1)}) custom-call(f32[16,6,8,8,128]{4,3,2,1,0:T(8,128)} %copy-done, f32[4,6,8,8,128]{4,3,2,1,0:T(8,128)} %shard_map.69.inner_ref, f32[4,6,8,8,128]{4,3,2,1,0:T(8,128)S(1)} %get-tuple-element.21.partial_ref, f32[4,8,128]{2,1,0:T(8,128)S(1)} %get-tuple-element.22.square_ref, ...), custom_call_target="tpu_custom_call" | custom-call | tf_op jit(solution)/shard_map/pallas_call | solution.py:31
  59.5 1.8 %collective-permute-start.7 = (f32[72,128]{1,0:T(8,128)S(1)}, f32[72,128]{1,0:T(8,128)S(1)}, u32[]{:S(2)}, u32[]{:S(2)}) collective-permute-start(f32[72,128]{1,0:T(8,128)S(1)} %get-tuple-element.26.refs_0_), channel_id=1, source_target_pairs={{0,12},{4,0},{8,4},{12,8},{1,13},{5,1},{9,5},{13,9},{2,14},{6,2},{... | collective-permute-start | bytes 110600 | tf_op jit(solution)/shard_map/ppermute | solution.py:46
  61.3 0.3 collective-permute-start.6
  61.6 1.1 collective-permute-start.5
  62.7 0.8 collective-permute-done.7.refs_3_
  63.5 2.8 %collective-permute-done.6.refs_2_ = f32[72,128]{1,0:T(8,128)S(1)} collective-permute-done((f32[72,128]{1,0:T(8,128)S(1)}, f32[72,128]{1,0:T(8,128)S(1)}, u32[]{:S(2)}, u32[]{:S(2)}) %collective-permute-start.6) | collective-permute-done | bytes 36896 | tf_op jit(solution)/shard_map/ppermute | solution.py:46
  66.3 1.1 %collective-permute-done.5.refs_1_ = f32[72,128]{1,0:T(8,128)S(1)} collective-permute-done((f32[72,128]{1,0:T(8,128)S(1)}, f32[72,128]{1,0:T(8,128)S(1)}, u32[]{:S(2)}, u32[]{:S(2)}) %collective-permute-start.5) | collective-permute-done | bytes 36896 | tf_op jit(solution)/shard_map/ppermute | solution.py:46
  67.4 0.0 copy-done.1
  67.4 1.2 %shard_map.72 = (f32[4,6,8,8,128]{4,3,2,1,0:T(8,128)S(1)}, f32[64,128]{1,0:T(8,128)S(1)}, f32[12,128]{1,0:T(8,128)S(1)}) custom-call(f32[16,6,8,8,128]{4,3,2,1,0:T(8,128)S(1)} %copy-done.1, f32[4,6,8,8,128]{4,3,2,1,0:T(8,128)S(1)} %get-tuple-element.20.source_ref, f32[4,6,8,8,128]{4,3,2,1,0:T(8,128)S(1)} %get-tuple-element.23.applied_ref, ...), custom_call_target="tpu_custom_call" | custom-call | tf_op jit(solution)/shard_map/pallas_call | solution.py:31
  68.6 0.9 collective-permute-start.8
  69.5 0.0 copy-start.2
  69.5 6.6 %shard_map.73 = (f32[4,6,8,8,128]{4,3,2,1,0:T(8,128)S(1)}, f32[12,8,128]{2,1,0:T(8,128)S(1)}) custom-call(f32[4]{0:T(128)S(1)} %broadcast_subtract_fusion.shift_ref, f32[16,6,8,8,128]{4,3,2,1,0:T(8,128)} %copy-done, f32[6,8,8,128]{3,2,1,0:T(8,128)S(1)} %bitcast.27, f32[4,6,8,8,128]{4,3,2,1,0:T(8,128)S(1)} %get-tuple-element.20.source_ref, ...), custom_call_target="tpu_custom_call" | custom-call | tf_op jit(solution)/shard_map/pallas_call | solution.py:31
  76.1 9.6 %collective-permute-done.8.after_ref = f32[4,6,8,8,128]{4,3,2,1,0:T(8,128)S(1)} collective-permute-done((f32[4,6,8,8,128]{4,3,2,1,0:T(8,128)S(1)}, f32[4,6,8,8,128]{4,3,2,1,0:T(8,128)S(1)}, u32[]{:S(2)}, u32[]{:S(2)}) %collective-permute-start.8) | collective-permute-done | bytes 786464 | tf_op jit(solution)/shard_map/ppermute | solution.py:53
  85.7 0.2 shard_map.74.refs_0_
  86.0 2.8 %collective-permute-start.11 = (f32[12,128]{1,0:T(8,128)S(1)}, f32[12,128]{1,0:T(8,128)S(1)}, u32[]{:S(2)}, u32[]{:S(2)}) collective-permute-start(f32[12,128]{1,0:T(8,128)S(1)} %shard_map.74.refs_0_), channel_id=1, source_target_pairs={{0,12},{4,0},{8,4},{12,8},{1,13},{5,1},{9,5},{13,9},{2,14},{6,2},{... | collective-permute-start | bytes 18440 | tf_op jit(solution)/shard_map/ppermute | solution.py:46
  88.8 0.0 collective-permute-start.10
  88.8 1.0 collective-permute-start.9
  89.8 0.4 collective-permute-done.11.refs_3_
  90.2 3.2 %collective-permute-done.10.refs_2_ = f32[12,128]{1,0:T(8,128)S(1)} collective-permute-done((f32[12,128]{1,0:T(8,128)S(1)}, f32[12,128]{1,0:T(8,128)S(1)}, u32[]{:S(2)}, u32[]{:S(2)}) %collective-permute-start.10) | collective-permute-done | bytes 6176 | tf_op jit(solution)/shard_map/ppermute | solution.py:46
  93.4 0.9 collective-permute-done.9.refs_1_
  94.3 0.0 copy-done.2
  94.3 0.3 shard_map.75
  94.6 0.1 collective-permute-start.14
  94.7 1.6 %collective-permute-start.13 = (f32[6,2,16,128]{3,2,1,0:T(8,128)S(1)}, f32[6,2,16,128]{3,2,1,0:T(8,128)S(1)}, u32[]{:S(2)}, u32[]{:S(2)}) collective-permute-start(f32[6,2,16,128]{3,2,1,0:T(8,128)S(1)} %get-tuple-element.35), channel_id=1, source_target_pairs={{0,2},{1,3},{2,0},{3,1},{4,6},{5,7},{6,4},{7,5},{8,10},{9,11},{10,... | collective-permute-start | bytes 294920 | tf_op jit(solution)/shard_map/ppermute | solution.py:53
  96.2 0.2 collective-permute-start.12
  96.4 0.5 collective-permute-done.14.refs_2_
  96.9 4.9 %collective-permute-done.13.refs_1_ = f32[6,2,16,128]{3,2,1,0:T(8,128)S(1)} collective-permute-done((f32[6,2,16,128]{3,2,1,0:T(8,128)S(1)}, f32[6,2,16,128]{3,2,1,0:T(8,128)S(1)}, u32[]{:S(2)}, u32[]{:S(2)}) %collective-permute-start.13) | collective-permute-done | bytes 98336 | tf_op jit(solution)/shard_map/ppermute | solution.py:53
  101.8 0.1 collective-permute-done.12.refs_0_
  101.9 0.6 collective-permute-start.16
  102.6 1.5 %collective-permute-start.15 = (f32[2,2,16,128]{3,2,1,0:T(8,128)S(1)}, f32[2,2,16,128]{3,2,1,0:T(8,128)S(1)}, u32[]{:S(2)}, u32[]{:S(2)}) collective-permute-start(f32[2,2,16,128]{3,2,1,0:T(8,128)S(1)} %get-tuple-element.38), channel_id=1, source_target_pairs={{0,4},{4,8},{8,12},{12,0},{1,5},{5,9},{9,13},{13,1},{2,6},{6,10},{... | collective-permute-start | bytes 98312 | tf_op jit(solution)/shard_map/ppermute | solution.py:53
  104.0 1.1 shard_map.76
  105.1 0.8 collective-permute-done.16.after_ref
  105.9 2.4 %collective-permute-done.15.before_ref = f32[2,2,16,128]{3,2,1,0:T(8,128)S(1)} collective-permute-done((f32[2,2,16,128]{3,2,1,0:T(8,128)S(1)}, f32[2,2,16,128]{3,2,1,0:T(8,128)S(1)}, u32[]{:S(2)}, u32[]{:S(2)}) %collective-permute-start.15) | collective-permute-done | bytes 32800 | tf_op jit(solution)/shard_map/ppermute | solution.py:53
  108.3 0.9 shard_map.78
  (4 shorter events, 0.1 us)
Async XLA Ops:
  0.6 1.0 copy-start.3
  1.6 11.6 %copy-start.4 = (f32[6,8192]{1,0:T(8,128)S(1)}, f32[6,8192]{1,0:T(8,128)}, u32[]{:S(2)}) copy-start(f32[6,8192]{1,0:T(8,128)} %perturb_ref.1) | copy-start | bytes 589828
  7.0 25.3 %copy-start = (f32[16,6,8,8,128]{4,3,2,1,0:T(8,128)}, f32[16,6,8,8,128]{4,3,2,1,0:T(8,128)S(1)}, u32[]{:S(2)}) copy-start(f32[16,6,8,8,128]{4,3,2,1,0:T(8,128)S(1)} %get-tuple-element.18.planes_ref) | copy-start | bytes 9437188
  7.0 18.3 %copy-start.5 = (f32[4]{0:T(128)S(1)}, f32[4]{0:T(128)}, u32[]{:S(2)}) copy-start(f32[4]{0:T(128)} %param.8) | copy-start | bytes 52
  7.0 7.9 %collective-permute-start.2 = (f32[32,16]{1,0:T(8,128)S(1)}, f32[32,16]{1,0:T(8,128)S(1)}, u32[]{:S(2)}, u32[]{:S(2)}) collective-permute-start(f32[32,16]{1,0:T(8,128)S(1)} %get-tuple-element.19.refs_0_), channel_id=1, source_target_pairs={{0,12},{4,0},{8,4},{12,8},{1,13},{5,1},{9,5},{13,9},{2,14},{6,2},{... | collective-permute-start | bytes 6152 | tf_op jit(solution)/shard_map/ppermute | solution.py:46
  12.2 4.6 %collective-permute-start.1 = (f32[32,16]{1,0:T(8,128)S(1)}, f32[32,16]{1,0:T(8,128)S(1)}, u32[]{:S(2)}, u32[]{:S(2)}) collective-permute-start(f32[32,16]{1,0:T(8,128)S(1)} %get-tuple-element.19.refs_0_), channel_id=1, source_target_pairs={{0,8},{4,12},{8,0},{12,4},{1,9},{5,13},{9,1},{13,5},{2,10},{6,14},... | collective-permute-start | bytes 6152 | tf_op jit(solution)/shard_map/ppermute | solution.py:46
  12.2 5.5 %collective-permute-start = (f32[32,16]{1,0:T(8,128)S(1)}, f32[32,16]{1,0:T(8,128)S(1)}, u32[]{:S(2)}, u32[]{:S(2)}) collective-permute-start(f32[32,16]{1,0:T(8,128)S(1)} %get-tuple-element.19.refs_0_), channel_id=1, source_target_pairs={{0,4},{4,8},{8,12},{12,0},{1,5},{5,9},{9,13},{13,1},{2,6},{6,10},{... | collective-permute-start | bytes 6152 | tf_op jit(solution)/shard_map/ppermute | solution.py:46
  19.9 20.5 %collective-permute-start.4 = (f32[4,6,8,8,128]{4,3,2,1,0:T(8,128)}, f32[4,6,8,8,128]{4,3,2,1,0:T(8,128)}, u32[]{:S(2)}, u32[]{:S(2)}) collective-permute-start(f32[4,6,8,8,128]{4,3,2,1,0:T(8,128)} %shard_map.69.inner_ref), channel_id=1, source_target_pairs={{0,12},{4,0},{8,4},{12,8},{1,13},{5,1},{9,5},{13,9},{2,14},{6,2},{... | collective-permute-start | bytes 2359304 | tf_op jit(solution)/shard_map/ppermute | solution.py:53
  20.4 34.9 %collective-permute-start.3 = (f32[4,6,8,8,128]{4,3,2,1,0:T(8,128)}, f32[4,6,8,8,128]{4,3,2,1,0:T(8,128)}, u32[]{:S(2)}, u32[]{:S(2)}) collective-permute-start(f32[4,6,8,8,128]{4,3,2,1,0:T(8,128)} %shard_map.69.inner_ref), channel_id=1, source_target_pairs={{0,4},{4,8},{8,12},{12,0},{1,5},{5,9},{9,13},{13,1},{2,6},{6,10},{... | collective-permute-start | bytes 2359304 | tf_op jit(solution)/shard_map/ppermute | solution.py:53
  55.3 12.1 %copy-start.1 = (f32[16,6,8,8,128]{4,3,2,1,0:T(8,128)S(1)}, f32[16,6,8,8,128]{4,3,2,1,0:T(8,128)}, u32[]{:S(2)}) copy-start(f32[16,6,8,8,128]{4,3,2,1,0:T(8,128)} %copy-done) | copy-start | bytes 9437188
  59.5 4.0 %collective-permute-start.7 = (f32[72,128]{1,0:T(8,128)S(1)}, f32[72,128]{1,0:T(8,128)S(1)}, u32[]{:S(2)}, u32[]{:S(2)}) collective-permute-start(f32[72,128]{1,0:T(8,128)S(1)} %get-tuple-element.26.refs_0_), channel_id=1, source_target_pairs={{0,12},{4,0},{8,4},{12,8},{1,13},{5,1},{9,5},{13,9},{2,14},{6,2},{... | collective-permute-start | bytes 110600 | tf_op jit(solution)/shard_map/ppermute | solution.py:46
  61.3 5.0 %collective-permute-start.6 = (f32[72,128]{1,0:T(8,128)S(1)}, f32[72,128]{1,0:T(8,128)S(1)}, u32[]{:S(2)}, u32[]{:S(2)}) collective-permute-start(f32[72,128]{1,0:T(8,128)S(1)} %get-tuple-element.26.refs_0_), channel_id=1, source_target_pairs={{0,8},{4,12},{8,0},{12,4},{1,9},{5,13},{9,1},{13,5},{2,10},{6,14},... | collective-permute-start | bytes 110600 | tf_op jit(solution)/shard_map/ppermute | solution.py:46
  61.6 5.8 %collective-permute-start.5 = (f32[72,128]{1,0:T(8,128)S(1)}, f32[72,128]{1,0:T(8,128)S(1)}, u32[]{:S(2)}, u32[]{:S(2)}) collective-permute-start(f32[72,128]{1,0:T(8,128)S(1)} %get-tuple-element.26.refs_0_), channel_id=1, source_target_pairs={{0,4},{4,8},{8,12},{12,0},{1,5},{5,9},{9,13},{13,1},{2,6},{6,10},{... | collective-permute-start | bytes 110600 | tf_op jit(solution)/shard_map/ppermute | solution.py:46
  68.6 17.1 %collective-permute-start.8 = (f32[4,6,8,8,128]{4,3,2,1,0:T(8,128)S(1)}, f32[4,6,8,8,128]{4,3,2,1,0:T(8,128)S(1)}, u32[]{:S(2)}, u32[]{:S(2)}) collective-permute-start(f32[4,6,8,8,128]{4,3,2,1,0:T(8,128)S(1)} %get-tuple-element.27.ahead_ref), channel_id=1, source_target_pairs={{0,12},{4,0},{8,4},{12,8},{1,13},{5,1},{9,5},{13,9},{2,14},{6,2},{... | collective-permute-start | bytes 2359304 | tf_op jit(solution)/shard_map/ppermute | solution.py:53
  69.5 24.8 %copy-start.2 = (f32[16,6,8,8,128]{4,3,2,1,0:T(8,128)S(1)}, f32[16,6,8,8,128]{4,3,2,1,0:T(8,128)}, u32[]{:S(2)}) copy-start(f32[16,6,8,8,128]{4,3,2,1,0:T(8,128)} %copy-done) | copy-start | bytes 9437188
  86.0 4.2 %collective-permute-start.11 = (f32[12,128]{1,0:T(8,128)S(1)}, f32[12,128]{1,0:T(8,128)S(1)}, u32[]{:S(2)}, u32[]{:S(2)}) collective-permute-start(f32[12,128]{1,0:T(8,128)S(1)} %shard_map.74.refs_0_), channel_id=1, source_target_pairs={{0,12},{4,0},{8,4},{12,8},{1,13},{5,1},{9,5},{13,9},{2,14},{6,2},{... | collective-permute-start | bytes 18440 | tf_op jit(solution)/shard_map/ppermute | solution.py:46
  88.8 4.5 %collective-permute-start.10 = (f32[12,128]{1,0:T(8,128)S(1)}, f32[12,128]{1,0:T(8,128)S(1)}, u32[]{:S(2)}, u32[]{:S(2)}) collective-permute-start(f32[12,128]{1,0:T(8,128)S(1)} %shard_map.74.refs_0_), channel_id=1, source_target_pairs={{0,8},{4,12},{8,0},{12,4},{1,9},{5,13},{9,1},{13,5},{2,10},{6,14},... | collective-permute-start | bytes 18440 | tf_op jit(solution)/shard_map/ppermute | solution.py:46
  88.8 5.4 %collective-permute-start.9 = (f32[12,128]{1,0:T(8,128)S(1)}, f32[12,128]{1,0:T(8,128)S(1)}, u32[]{:S(2)}, u32[]{:S(2)}) collective-permute-start(f32[12,128]{1,0:T(8,128)S(1)} %shard_map.74.refs_0_), channel_id=1, source_target_pairs={{0,4},{4,8},{8,12},{12,0},{1,5},{5,9},{9,13},{13,1},{2,6},{6,10},{... | collective-permute-start | bytes 18440 | tf_op jit(solution)/shard_map/ppermute | solution.py:46
  94.6 2.3 %collective-permute-start.14 = (f32[6,2,16,128]{3,2,1,0:T(8,128)S(1)}, f32[6,2,16,128]{3,2,1,0:T(8,128)S(1)}, u32[]{:S(2)}, u32[]{:S(2)}) collective-permute-start(f32[6,2,16,128]{3,2,1,0:T(8,128)S(1)} %get-tuple-element.34), channel_id=1, source_target_pairs={{0,3},{1,0},{2,1},{3,2},{4,7},{5,4},{6,5},{7,6},{8,11},{9,8},{10,9... | collective-permute-start | bytes 294920 | tf_op jit(solution)/shard_map/ppermute | solution.py:53
  94.7 7.1 %collective-permute-start.13 = (f32[6,2,16,128]{3,2,1,0:T(8,128)S(1)}, f32[6,2,16,128]{3,2,1,0:T(8,128)S(1)}, u32[]{:S(2)}, u32[]{:S(2)}) collective-permute-start(f32[6,2,16,128]{3,2,1,0:T(8,128)S(1)} %get-tuple-element.35), channel_id=1, source_target_pairs={{0,2},{1,3},{2,0},{3,1},{4,6},{5,7},{6,4},{7,5},{8,10},{9,11},{10,... | collective-permute-start | bytes 294920 | tf_op jit(solution)/shard_map/ppermute | solution.py:53
  96.2 5.7 %collective-permute-start.12 = (f32[6,2,16,128]{3,2,1,0:T(8,128)S(1)}, f32[6,2,16,128]{3,2,1,0:T(8,128)S(1)}, u32[]{:S(2)}, u32[]{:S(2)}) collective-permute-start(f32[6,2,16,128]{3,2,1,0:T(8,128)S(1)} %get-tuple-element.36), channel_id=1, source_target_pairs={{0,1},{1,2},{2,3},{3,0},{4,5},{5,6},{6,7},{7,4},{8,9},{9,10},{10,1... | collective-permute-start | bytes 294920 | tf_op jit(solution)/shard_map/ppermute | solution.py:53
  101.9 4.0 %collective-permute-start.16 = (f32[2,2,16,128]{3,2,1,0:T(8,128)S(1)}, f32[2,2,16,128]{3,2,1,0:T(8,128)S(1)}, u32[]{:S(2)}, u32[]{:S(2)}) collective-permute-start(f32[2,2,16,128]{3,2,1,0:T(8,128)S(1)} %get-tuple-element.37), channel_id=1, source_target_pairs={{0,12},{4,0},{8,4},{12,8},{1,13},{5,1},{9,5},{13,9},{2,14},{6,2},{... | collective-permute-start | bytes 98312 | tf_op jit(solution)/shard_map/ppermute | solution.py:53
  102.6 5.7 %collective-permute-start.15 = (f32[2,2,16,128]{3,2,1,0:T(8,128)S(1)}, f32[2,2,16,128]{3,2,1,0:T(8,128)S(1)}, u32[]{:S(2)}, u32[]{:S(2)}) collective-permute-start(f32[2,2,16,128]{3,2,1,0:T(8,128)S(1)} %get-tuple-element.38), channel_id=1, source_target_pairs={{0,4},{4,8},{8,12},{12,0},{1,5},{5,9},{9,13},{13,1},{2,6},{6,10},{... | collective-permute-start | bytes 98312 | tf_op jit(solution)/shard_map/ppermute | solution.py:53
where the time goes:
time: 109 us
  waiting for transfers between devices  53.1 us (49%)
  Pallas kernels  29.1 us (27%)
  starting transfers between devices  19.9 us (18%)
  local copies, waits for them, and re-layouts  5.54 us (5%)
  between operations  1.42 us (1%)
    ppermute x8, waiting for transfers between devices, shifted(): lax.ppermute(array, axis, [(i, (i + step) % size) for i in range(size)])  41.3 us
    pallas_call x11, Pallas kernels, call(): pl.pallas_call(kernel, out_shape=[jax.ShapeDtypeStruct(s, f32) for s in o...  29.1 us
    ppermute x9, starting transfers between devices, parts_of(): lax.ppermute(array, axis, [(i, (i + k) % size) for i in range(size)])  13.2 us
    ppermute x9, waiting for transfers between devices, parts_of(): lax.ppermute(array, axis, [(i, (i + k) % size) for i in range(size)])  11.8 us
    ppermute x8, starting transfers between devices, shifted(): lax.ppermute(array, axis, [(i, (i + step) % size) for i in range(size)])  6.77 us
    reshape x4, local copies, waits for them, and re-layouts, as_planes(): array = array.reshape(layers, NY, halves, LANES).transpose(0, 2, 1, 3)  4.54 us
  transfers between devices with their start and end apart: 17, of which 16 were waited for; matrix products, arithmetic and copies ran while one was open for 4% of the time, Pallas kernels for 13%

commit v1 on v0

--- a/solution.py
+++ b/solution.py
@@ -21,31 +21,30 @@
 )
 SCREEN = 0.25
 HIGHEST = lax.Precision.HIGHEST
-VMEM_LIMIT = 48 * 1024 * 1024
+VMEM_LIMIT = 16 * 1024 * 1024
 SMEM = pl.BlockSpec(memory_space=pltpu.SMEM)
 VMEM = pl.BlockSpec(memory_space=pltpu.VMEM)
+HBM = pl.BlockSpec(memory_space=pltpu.HBM)
 f32 = jnp.float32
 
 
-def call(kernel, outs, scratch, smem, *args):
+def call(kernel, outs, scratch, smem, *args, far=0):
     return pl.pallas_call(
         kernel,
         out_shape=[jax.ShapeDtypeStruct(s, f32) for s in outs],
-        in_specs=[SMEM] * smem + [VMEM] * (len(args) - smem),
+        in_specs=[SMEM] * smem + [HBM] * far + [VMEM] * (len(args) - smem - far),
         out_specs=[VMEM] * len(outs),
-        scratch_shapes=[pltpu.VMEM(s, f32) for s in scratch],
+        scratch_shapes=[pltpu.VMEM(s, f32) if isinstance(s, tuple) else s for s in scratch],
         compiler_params=pltpu.CompilerParams(vmem_limit_bytes=VMEM_LIMIT),
     )(*args)
 
 
 def parts_of(array, axis):
     size = lax.axis_size(axis)
-    if size > 4:
+    if size > 4 or size & (size - 1):
         return [lax.psum(array, axis)]
-    rotated = [
-        lax.ppermute(array, axis, [(i, (i + k) % size) for i in range(size)]) for k in range(1, size)
-    ]
-    return [array] + rotated
+    others = [lax.ppermute(array, axis, [(i, i ^ k) for i in range(size)]) for k in range(1, size)]
+    return [array] + others
 
 
 def shifted(array, axis, step):
@@ -60,39 +59,63 @@
     return total
 
 
-def column(matrix, index):
-    lane = lax.broadcasted_iota(jnp.int32, matrix.shape, 1)
-    picked = jnp.sum(jnp.where(lane == index, matrix, 0.0), axis=1, keepdims=True)
-    return jnp.broadcast_to(picked, (matrix.shape[0], LANES))
+def rows_to_lanes(matrix):
+    count = matrix.shape[0]
+    lane = lax.broadcasted_iota(jnp.int32, (count, LANES), 1)
+    row = lax.broadcasted_iota(jnp.int32, (count, LANES), 0)
+    value = jnp.broadcast_to(jnp.sum(matrix, axis=1, keepdims=True), (count, LANES))
+    line = jnp.sum(jnp.where(lane == row, value, 0.0), axis=0, keepdims=True)
+    return jnp.broadcast_to(line, (SUB, LANES))
+
+
+def lanes_to_rows(line, count):
+    wide = line.shape[1]
+    lane = lax.broadcasted_iota(jnp.int32, (count, wide), 1)
+    row = lax.broadcasted_iota(jnp.int32, (count, wide), 0)
+    picked = jnp.where(lane == row, jnp.broadcast_to(line, (count, wide)), 0.0)
+    return jnp.broadcast_to(jnp.sum(picked, axis=1, keepdims=True), (count, LANES))
 
 
 def blocks(plane):
     return plane.reshape(-1, NY, LANES)
 
 
-def gram_kernel(shape, rows_ref, perturb_ref, planes_ref, gram_ref):
-    norb, layers, halves = shape
+def gram_kernel(shape, far_rows_ref, far_perturb_ref, planes_ref, gram_ref, rows_ref, perturb_ref, row_sems, perturb_sem):
+    norb, layers, halves, group = shape
     groups = norb // SUB
     tiles = NY * halves
     step = 16
+    size = norb * tiles
+    own = lax.axis_index("orb") * group // SUB
+
+    def fetch(z):
+        piece = pl.ds(z * size, size)
+        return pltpu.make_async_copy(far_rows_ref.at[piece], rows_ref.at[piece], row_sems.at[z])
+
+    weights = pltpu.make_async_copy(far_perturb_ref, perturb_ref, perturb_sem)
+    fetch(0).start()
+    weights.start()
+    for z in range(1, layers):
+        fetch(z).start()
+    weights.wait()
+
+    def tile_row(z, t, c0):
+        base = ((z * groups + t) * tiles + c0) * SUB
+        return jnp.concatenate([rows_ref[pl.ds(base + c * SUB, SUB), :] for c in range(step)], axis=1)
+
+    def rounded(value):
+        return value.astype(jnp.bfloat16).astype(f32)
 
     def layer(z, total):
+        fetch(z).wait()
         for c0 in range(0, tiles, step):
-            pieces = []
-            for t in range(groups):
-                base = ((z * groups + t) * tiles + c0) * SUB
-                pieces.append(
-                    jnp.concatenate(
-                        [rows_ref[pl.ds(base + c * SUB, SUB), :] for c in range(step)], axis=1
-                    )
-                )
-            field = jnp.concatenate(pieces, axis=0)
-            weight = perturb_ref[pl.ds(z, 1), c0 * LANES : (c0 + step) * LANES]
-            both = jnp.concatenate([field, field * weight], axis=0)
-            high = both.astype(jnp.bfloat16)
-            low = (both - high.astype(f32)).astype(jnp.bfloat16)
-            left = jnp.concatenate([high, low], axis=0)
-            right = jnp.concatenate([high[:norb], low[:norb]], axis=0)
+            field = jnp.concatenate([tile_row(z, t, c0) for t in range(groups)], axis=0)
+            weighted = perturb_ref[pl.ds(z, 1), c0 * LANES : (c0 + step) * LANES] * tile_row(z, own, c0)
+            rest = (field - rounded(field)).astype(jnp.bfloat16)
+            field = field.astype(jnp.bfloat16)
+            pair = jnp.concatenate([weighted, weighted - rounded(weighted)], axis=0).astype(jnp.bfloat16)
+            left = jnp.concatenate([field, rest, pair], axis=0)
+            right = jnp.concatenate([field, rest], axis=0)
             total = total + lax.dot_general(
                 left, right, (((1,), (1,)), ((), ())), preferred_element_type=f32
             )
@@ -107,16 +130,24 @@
                         ]
         return total
 
-    total = lax.fori_loop(0, layers, layer, jnp.zeros((4 * norb, 2 * norb), f32))
-    total = total[: 2 * norb] + total[2 * norb :]
-    gram_ref[...] = total[:, :norb] + total[:, norb:]
-
-
-def small_matrices(norb, gram_refs, ncell):
+    total = lax.fori_loop(0, layers, layer, jnp.zeros((2 * norb + 2 * SUB, 2 * norb), f32))
+    total = total[:, :norb] + total[:, norb:]
+    gram_ref[:norb, :] = total[:norb] + total[norb : 2 * norb]
+    gram_ref[norb:, :] = total[2 * norb : 2 * norb + SUB] + total[2 * norb + SUB :]
+
+
+def small_matrices(shape, ncell, gram_refs, lines_ref):
+    norb, group = shape
     total = add_all(gram_refs)
-    overlap, weighted = total[:norb], total[norb:]
-    twice = jnp.dot(overlap, weighted, precision=HIGHEST, preferred_element_type=f32) * (1.0 / ncell)
-    return overlap, weighted, twice
+    overlap = total[:norb]
+    lines_ref[...] = total[norb:]
+    start = lax.rem(lax.axis_index("orb") * group, SUB)
+    rows = []
+    for n in range(group):
+        line = lines_ref[pl.ds(start + n, 1), :]
+        again = jnp.sum(lanes_to_rows(line, norb)[:, :norb] * overlap, axis=0, keepdims=True)
+        rows.append((line, again * (1.0 / ncell)))
+    return overlap, rows
 
 
 def combine(layers, group, norb, planes_ref, coef_ref, start, finish):
@@ -134,19 +165,25 @@
 
 
 def inner_kernel(shape, ncell, planes_ref, perturb_ref, *refs):
-    norb, layers, group, parts = shape
-    gram_refs, inner_ref, coef_ref = refs[:parts], refs[parts], refs[parts + 1]
+    norb, layers, group, parts, share = shape
+    gram_refs = refs[:parts]
+    inner_ref, rest_ref = refs[parts : parts + 2]
+    coef_ref, lines_ref = refs[-2:]
     first = lax.axis_index("orb") * group
-    overlap, weighted, twice = small_matrices(norb, gram_refs, ncell)
-    coefs = (2.0 * weighted - twice) * (1.0 / ncell)
-    for n in range(group):
-        coef_ref[n * norb : (n + 1) * norb, :] = column(coefs, first + n)
+    overlap, rows = small_matrices((norb, group), ncell, gram_refs, lines_ref)
+    for n, (line, again) in enumerate(rows):
+        coefs = (2.0 * line - again) * (1.0 / ncell)
+        coef_ref[n * norb : (n + 1) * norb, :] = lanes_to_rows(coefs, norb)
+    place = lax.axis_index("freq") * share
 
     def start(n, z):
         return -(perturb_ref[z] * planes_ref[first + n, z])
 
     def finish(n, z, value):
         inner_ref[n, z] = value
+        rest_ref[n, z] = value[2 * share :]
+        if share:
+            refs[parts + 2][n, z] = inner_ref[n, z, pl.ds(place, share)]
 
     combine(layers, group, norb, planes_ref, coef_ref, start, finish)
 
@@ -169,15 +206,15 @@
 def local_kernel(shape, ncell, shift_ref, planes_ref, perturb_ref, potential_ref, inner_ref, *refs):
     norb, layers, group, parts, halves = shape
     gram_refs = refs[:parts]
-    source_ref, partial_ref, overlap_ref, along_ref, square_ref, coef_ref = refs[parts:]
+    source_ref, partial_ref, overlap_ref, along_ref, square_ref, coef_ref, lines_ref = refs[parts:]
     first = lax.axis_index("orb") * group
-    overlap, weighted, twice = small_matrices(norb, gram_refs, ncell)
+    overlap, rows = small_matrices((norb, group), ncell, gram_refs, lines_ref)
     for m in range(norb):
-        overlap_ref[m] = column(overlap, m)
-    for n in range(group):
-        rows = slice(n * norb, (n + 1) * norb)
-        coef_ref[rows, :] = column(weighted * (1.0 / ncell), first + n)
-        along_ref[rows, :] = column(twice - weighted, first + n)
+        overlap_ref[m] = jnp.broadcast_to(overlap[:, m : m + 1], (norb, LANES))
+    for n, (line, again) in enumerate(rows):
+        place = slice(n * norb, (n + 1) * norb)
+        coef_ref[place, :] = lanes_to_rows(line * (1.0 / ncell), norb)
+        along_ref[place, :] = lanes_to_rows(again - line, norb)
     square_ref[...] = jnp.zeros_like(square_ref)
 
     def start(n, z):
@@ -217,20 +254,37 @@
                 partial_ref[n, z] += total
 
 
-def image_kernel(shape, planes_ref, inner_ref, partial_ref, square_ref, before_ref, after_ref, applied_ref, sums_ref, acc_ref):
-    norb, layers, group = shape
+def halo_sum(layers, n, z, before_ref, after_ref):
+    total = None
+    for j in range(layers):
+        for k, ref in ((z + layers - j, before_ref), (j + layers - z, after_ref)):
+            if k <= 6:
+                term = (-0.5 * COEFFS[k]) * ref[n, j]
+                total = term if total is None else total + term
+    return total
+
+
+def halo_kernel(shape, before_ref, after_ref, halo_ref):
+    layers, group = shape
+    for n in range(group):
+        for z in range(layers):
+            halo_ref[n, z] = halo_sum(layers, n, z, before_ref, after_ref)
+
+
+def image_kernel(shape, planes_ref, inner_ref, partial_ref, square_ref, before_ref, after_ref, *refs):
+    norb, layers, group, share = shape
+    applied_ref, sums_ref, acc_ref = refs[-3:]
+    place = lax.axis_index("freq") * share
     acc_ref[...] = jnp.zeros_like(acc_ref)
     for n in range(group):
         for z in range(layers):
-            total = partial_ref[n, z]
-            for j in range(layers):
-                k = z + layers - j
-                if k <= 6:
-                    total = total + (-0.5 * COEFFS[k]) * before_ref[n, j]
-                k = j + layers - z
-                if k <= 6:
-                    total = total + (-0.5 * COEFFS[k]) * after_ref[n, j]
-            applied_ref[n, z] = total
+            applied_ref[n, z, 2 * share :] = partial_ref[n, z, 2 * share :] + halo_sum(
+                layers, n, z, before_ref, after_ref
+            )
+            if share:
+                mine, other = pl.ds(place, share), pl.ds(share - place, share)
+                applied_ref[n, z, mine] = partial_ref[n, z, mine] + refs[0][n, z]
+                applied_ref[n, z, other] = partial_ref[n, z, other] + refs[1][n, z]
 
     def layer(z, carry):
         fields = [applied_ref[n, z] for n in range(group)]
@@ -243,23 +297,16 @@
         return carry
 
     lax.fori_loop(0, layers, layer, 0)
-    count = group * norb + group
-    sums_ref[:count, :] = jnp.sum(acc_ref[:count], axis=1)
-    sums_ref[count : count + group, :] = jnp.sum(square_ref[...], axis=1)
-    if sums_ref.shape[0] > count + group:
-        sums_ref[count + group :, :] = jnp.zeros((sums_ref.shape[0] - count - group, LANES), f32)
-
-
-def spread(value):
-    return jnp.broadcast_to(jnp.sum(value, axis=1, keepdims=True), value.shape)
+    totals = jnp.concatenate([jnp.sum(acc_ref[...], axis=1), jnp.sum(square_ref[...], axis=1)], axis=0)
+    sums_ref[...] = rows_to_lanes(totals)
 
 
 def residual_kernel(shape, ncell, planes_ref, source_ref, applied_ref, overlap_ref, along_ref, *refs):
     norb, layers, group, parts = shape
     sums_refs = refs[:parts]
     ahead_ref, plain_ref, numbers_ref, coef_ref, step_ref = refs[parts:]
-    total = spread(add_all(sums_refs))
     count = group * norb
+    total = lanes_to_rows(add_all(sums_refs)[:1], count + 2 * group)
     curve = total[count : count + group]
     norm = total[count + group : count + 2 * group]
     step = norm / curve
@@ -328,7 +375,8 @@
 
 def pairs_kernel(shape, ahead_ref, after_ref, acc_ref, sums_ref):
     layers, group = shape
-    sums_ref[...] = jnp.sum(acc_ref[...], axis=1)
+    sums = jnp.sum(acc_ref[...], axis=1)
+    lines = []
     for n in range(group):
         total = None
         for z in range(layers):
@@ -341,7 +389,8 @@
             if line is not None:
                 line = line * ahead_ref[n, z]
                 total = line if total is None else total + line
-        sums_ref[n : n + 1, :] += jnp.sum(jnp.sum(total, axis=0), axis=0, keepdims=True)
+        lines.append(jnp.sum(jnp.sum(total, axis=0), axis=0, keepdims=True))
+    sums_ref[...] = rows_to_lanes(jnp.concatenate([sums[:group] + jnp.concatenate(lines, axis=0), sums[group:]], axis=0))
 
 
 def density_kernel(shape, planes_ref, source_ref, residual_ref, numbers_ref, *refs):
@@ -349,7 +398,7 @@
     sums_refs = refs[:parts]
     cuts_ref, scales_ref, ring_ref = refs[parts:]
     first = lax.axis_index("orb")
-    total = spread(add_all(sums_refs))
+    total = lanes_to_rows(add_all(sums_refs)[:1], 3 * group)
     norm, curve, alpha = (numbers_ref[i * group : (i + 1) * group, :] for i in range(3))
     squares, cross, bend = total[2 * group : 3 * group], total[group : 2 * group], total[:group]
     beta = squares / norm
@@ -376,7 +425,10 @@
         owner = lax.rem(first + k, members)
         for z in range(layers):
             for h in range(halves):
-                cuts_ref[k, z, h] = ring_ref[z, h, pl.ds(owner * width + SUB - margin, width + 2 * margin), :]
+                rows = width + 2 * margin
+                cuts_ref[k, pl.ds((z * halves + h) * rows, rows)] = ring_ref[
+                    z, h, pl.ds(owner * width + SUB - margin, rows), :
+                ]
 
 
 def response_kernel(shape, source_ref, residual_ref, scales_ref, response_ref):
@@ -396,21 +448,26 @@
     lax.fori_loop(0, layers, layer, 0)
 
 
-def gather_kernel(cuts_ref, *refs):
+def gather_kernel(edge, cuts_ref, *refs):
+    dense_ref, top_ref, bottom_ref = refs[-3:]
     total = cuts_ref[0]
-    for ref in refs[:-1]:
+    for ref in refs[:-3]:
         total = total + ref[...]
-    refs[-1][...] = total
+    dense_ref[...] = total
+    top_ref[...] = total[-edge:]
+    bottom_ref[...] = total[:edge]
 
 
 def jacobi_kernel(shape, dense_ref, before_ref, after_ref, induced_ref):
     layers, halves, width, margin = shape
+    rows = width + 2 * margin
     scale = 1.0 / (6.0 + SCREEN)
-    dense = [[before_ref[j, h] for h in range(halves)] for j in range(2)]
-    dense = dense + [[dense_ref[z, h] for h in range(halves)] for z in range(layers)]
-    dense = dense + [[after_ref[j, h] for h in range(halves)] for j in range(2)]
+
+    def sheets(ref, count):
+        return [[ref[pl.ds((z * halves + h) * rows, rows), :] for h in range(halves)] for z in range(count)]
+
+    dense = sheets(before_ref, 2) + sheets(dense_ref, layers) + sheets(after_ref, 2)
     field = [[scale * v for v in sheet] for sheet in dense]
-    rows = width + 2 * margin
 
     def up(value):
         return pltpu.roll(value, 1, 0)
@@ -455,30 +512,46 @@
     own = (group, layers, spots, SUB, LANES)
     flat = (group * norb, LANES)
 
+    size = norb * tiles
     planes, gram = call(
-        functools.partial(gram_kernel, (norb, layers, halves)),
-        [(norb, layers, spots, SUB, LANES), (2 * norb, norb)],
-        [],
+        functools.partial(gram_kernel, (norb, layers, halves, group)),
+        [(norb, layers, spots, SUB, LANES), (norb + SUB, norb)],
+        [
+            (layers * size, LANES),
+            (layers, columns),
+            pltpu.SemaphoreType.DMA((layers,)),
+            pltpu.SemaphoreType.DMA,
+        ],
         0,
         rows,
         perturb,
+        far=2,
     )
     grams = parts_of(gram, "brick")
     perturb_planes, potential_planes = as_planes(perturb), as_planes(potential)
-    (inner,) = call(
-        functools.partial(inner_kernel, (norb, layers, group, len(grams)), ncell),
-        [own],
-        [flat],
+    share = 3 * spots // 8 if lax.axis_size("freq") == 2 else 0
+    cells = (SUB, LANES)
+    inner, rest, *shared = call(
+        functools.partial(inner_kernel, (norb, layers, group, len(grams), share), ncell),
+        [own, (group, layers, spots - 2 * share) + cells] + [(group, layers, share) + cells] * (share > 0),
+        [flat, (SUB, norb)],
         0,
         planes,
         perturb_planes,
         *grams,
     )
-    before, after = shifted(inner, "brick", 1), shifted(inner, "brick", -1)
+    halos = []
+    if share:
+        before, after = shifted(shared[0], "brick", 1), shifted(shared[0], "brick", -1)
+        halos = call(
+            functools.partial(halo_kernel, (layers, group)), [shared[0].shape], [], 0, before, after
+        )
+        halos = [halos[0], lax.ppermute(halos[0], "freq", [(0, 1), (1, 0)])]
+    before, after = shifted(rest, "brick", 1), shifted(rest, "brick", -1)
     source, partial, overlap, along, square = call(
         functools.partial(local_kernel, (norb, layers, group, len(grams), halves), ncell),
         [own, own, (norb, norb, LANES), flat, (group, SUB, LANES)],
-        [flat],
+        [flat, (SUB, norb)],
         1,
         shift,
         planes,
@@ -487,11 +560,10 @@
         inner,
         *grams,
     )
-    height = -(-(group * norb + 2 * group) // SUB) * SUB
     applied, sums = call(
-        functools.partial(image_kernel, (norb, layers, group)),
-        [own, (height, LANES)],
-        [(group * norb + group, SUB, LANES)],
+        functools.partial(image_kernel, (norb, layers, group, share)),
+        [own, cells],
+        [(group * norb + group,) + cells],
         0,
         planes,
         inner,
@@ -499,6 +571,7 @@
         square,
         before,
         after,
+        *halos,
     )
     sums = parts_of(sums, "brick")
     ahead, plain, numbers = call(
@@ -530,7 +603,7 @@
     )
     (sums,) = call(
         functools.partial(pairs_kernel, (layers, group)),
-        [(3 * group, LANES)],
+        [cells],
         [],
         0,
         ahead,
@@ -539,8 +612,9 @@
     )
     sums = parts_of(sums, "brick")
     width = NY // members
-    margin = 4 if width % SUB == 0 else 2
-    cut = (layers, halves, width + 2 * margin, LANES)
+    margin = 2
+    edge = 2 * halves * (width + 2 * margin)
+    cut = (layers * halves * (width + 2 * margin), LANES)
     cuts, scales = call(
         functools.partial(density_kernel, (layers, group, len(sums), halves, members, width, margin)),
         [(members,) + cut, (2 * group, LANES)],
@@ -562,9 +636,10 @@
         residual,
         scales,
     )
-    (dense,) = call(gather_kernel, [cut], [], 0, cuts, *others)
-    before = shifted(dense[layers - 2 :], "brick", 1)
-    after = shifted(dense[:2], "brick", -1)
+    dense, top, bottom = call(
+        functools.partial(gather_kernel, edge), [cut, (edge, LANES), (edge, LANES)], [], 0, cuts, *others
+    )
+    before, after = shifted(top, "brick", 1), shifted(bottom, "brick", -1)
     (induced,) = call(
         functools.partial(jacobi_kernel, (layers, halves, width, margin)),
         [(layers, width * halves * LANES)],

time: 109 us -> 99.2 us (0.910)
  waiting for transfers between devices: 53.1 us -> 37 us
  starting transfers between devices: 19.9 us -> 27.4 us
  Pallas kernels: 29.1 us -> 22.9 us
  local copies, waits for them, and re-layouts: 5.54 us -> 10.1 us
    ppermute x8 -> x10, waiting for transfers between devices: 41.3 us -> 28.3 us  [shifted(): lax.ppermute(array, axis, [(i, (i + step) % size) for i in range(size)])]
    pallas_call x11 -> x12, Pallas kernels: 29.1 us -> 22.9 us  [call(): pl.pallas_call(kernel, out_shape=[jax.ShapeDtypeStruct(s, f32) for s in o...]
    unnamed x12 -> x16, local copies, waits for them, and re-layouts: 0.97 us -> 5.53 us
    ppermute x8 -> x10, starting transfers between devices: 6.77 us -> 11.3 us  [shifted(): lax.ppermute(array, axis, [(i, (i + step) % size) for i in range(size)])]
    ppermute x9 -> x10, waiting for transfers between devices: 11.8 us -> 8.72 us  [the longest x9 8.72 us: parts_of(): lax.ppermute(array, axis, [(i, i ^ k) for i in range(size)])]
    ppermute x9 -> x10, starting transfers between devices: 13.2 us -> 16.1 us  [the longest x9 14.6 us: parts_of(): lax.ppermute(array, axis, [(i, i ^ k) for i in range(size)])]
  transfers between devices with their start and end apart: 17 -> 20, of which waited for: 16 -> 13; matrix products, arithmetic and copies ran while one was open for 4% -> 5% of each run, Pallas kernels for 13% -> 13%
where the time goes in v1:
time: 99.2 us; the launch traced here: 98.8 us
  waiting for transfers between devices  37 us (37%)
  starting transfers between devices  27.4 us (28%)
  Pallas kernels  22.9 us (23%)
  local copies, waits for them, and re-layouts  10.1 us (10%)
  between operations  1.42 us (1%)
    ppermute x10, waiting for transfers between devices, shifted(): lax.ppermute(array, axis, [(i, (i + step) % size) for i in range(size)])  28.3 us
    pallas_call x12, Pallas kernels, call(): pl.pallas_call(kernel, out_shape=[jax.ShapeDtypeStruct(s, f32) for s in o...  22.9 us
    ppermute x9, starting transfers between devices, parts_of(): lax.ppermute(array, axis, [(i, i ^ k) for i in range(size)])  14.6 us
    ppermute x10, starting transfers between devices, shifted(): lax.ppermute(array, axis, [(i, (i + step) % size) for i in range(size)])  11.3 us
    ppermute x9, waiting for transfers between devices, parts_of(): lax.ppermute(array, axis, [(i, i ^ k) for i in range(size)])  8.72 us
    unnamed x16, local copies, waits for them, and re-layouts  5.53 us
    reshape x4, local copies, waits for them, and re-layouts, as_planes(): array = array.reshape(layers, NY, halves, LANES).transpose(0, 2, 1, 3)  4.56 us
  transfers between devices with their start and end apart: 20, of which 13 were waited for; matrix products, arithmetic and copies ran while one was open for 5% of the time, Pallas kernels for 13%

profile of v1, /device:TPU:0, one launch (start us, length us, event | category | flops | bytes accessed | tf_op | source)
XLA Modules:
  0.0 98.8 jit_solution(14662155928199180618)
XLA Ops:
  0.6 0.0 copy-start
  0.6 1.9 %copy-done = f32[16,6,8192]{2,0,1:T(8,128)S(1)} copy-done((f32[16,6,8192]{2,0,1:T(8,128)S(1)}, f32[16,6,8192]{2,0,1:T(8,128)}, u32[]{:S(2)}) %copy-start) | copy-done | bytes 3145752
  2.5 0.9 copy-done.4
  3.5 3.4 %shard_map.68 = (f32[16,6,8,8,128]{4,3,2,1,0:T(8,128)S(1)}, f32[24,16]{1,0:T(8,128)S(1)}) custom-call(f32[6144,128]{1,0:T(8,128)S(1)} %bitcast.26, f32[6,8192]{1,0:T(8,128)S(1)} %copy-done.4), custom_call_target="tpu_custom_call" | custom-call | tf_op jit(solution)/shard_map/pallas_call | solution.py:32
  6.9 0.0 copy-start.7
  6.9 5.1 %collective-permute-start.2 = (f32[24,16]{1,0:T(8,128)S(1)}, f32[24,16]{1,0:T(8,128)S(1)}, u32[]{:S(2)}, u32[]{:S(2)}) collective-permute-start(f32[24,16]{1,0:T(8,128)S(1)} %get-tuple-element.25.refs_0_), channel_id=1, source_target_pairs={{0,12},{4,8},{8,4},{12,0},{1,13},{5,9},{9,5},{13,1},{2,14},{6,10},... | collective-permute-start | bytes 4616 | tf_op jit(solution)/shard_map/ppermute | solution.py:46
  12.0 0.0 collective-permute-start.1
  12.0 0.6 collective-permute-start
  12.7 0.0 copy-done.5
  12.7 0.9 reshape.30
  13.5 0.9 copy.7
  14.5 0.0 collective-permute-done.2.refs_3_
  14.5 2.1 %collective-permute-done.1.refs_2_ = f32[24,16]{1,0:T(8,128)S(1)} collective-permute-done((f32[24,16]{1,0:T(8,128)S(1)}, f32[24,16]{1,0:T(8,128)S(1)}, u32[]{:S(2)}, u32[]{:S(2)}) %collective-permute-start.1) | collective-permute-done | bytes 1568 | tf_op jit(solution)/shard_map/ppermute | solution.py:46
  16.6 0.0 collective-permute-done.refs_1_
  16.6 1.2 %shard_map.69 = (f32[4,6,8,8,128]{4,3,2,1,0:T(8,128)S(1)}, f32[4,6,2,8,128]{4,3,2,1,0:T(8,128)S(1)}, f32[4,6,3,8,128]{4,3,2,1,0:T(8,128)S(1)}) custom-call(f32[16,6,8,8,128]{4,3,2,1,0:T(8,128)S(1)} %get-tuple-element.24.planes_ref, f32[6,8,8,128]{3,2,1,0:T(8,128)S(1)} %bitcast.29, f32[24,16]{1,0:T(8,128)S(1)} %get-tuple-element.25.refs_0_, ...), custom_call_target="tpu_custom_call" | custom-call | tf_op jit(solution)/shard_map/pallas_call | solution.py:32
  17.8 0.0 copy-start.1
  17.8 0.9 copy-done.1
  18.7 0.7 copy-done.6
  19.4 1.6 %collective-permute-start.6 = (f32[4,6,3,8,128]{4,3,2,1,0:T(8,128)S(1)}, f32[4,6,3,8,128]{4,3,2,1,0:T(8,128)S(1)}, u32[]{:S(2)}, u32[]{:S(2)}) collective-permute-start(f32[4,6,3,8,128]{4,3,2,1,0:T(8,128)S(1)} %get-tuple-element.31), channel_id=1, source_target_pairs={{0,12},{4,0},{8,4},{12,8},{1,13},{5,1},{9,5},{13,9},{2,14},{6,2},{... | collective-permute-start | bytes 884744 | tf_op jit(solution)/shard_map/ppermute | solution.py:52
  21.0 0.4 collective-permute-start.5
  21.4 7.1 %collective-permute-done.6.after_ref = f32[4,6,3,8,128]{4,3,2,1,0:T(8,128)S(1)} collective-permute-done((f32[4,6,3,8,128]{4,3,2,1,0:T(8,128)S(1)}, f32[4,6,3,8,128]{4,3,2,1,0:T(8,128)S(1)}, u32[]{:S(2)}, u32[]{:S(2)}) %collective-permute-start.6) | collective-permute-done | bytes 294944 | tf_op jit(solution)/shard_map/ppermute | solution.py:52
  28.4 5.8 %collective-permute-done.5.before_ref = f32[4,6,3,8,128]{4,3,2,1,0:T(8,128)S(1)} collective-permute-done((f32[4,6,3,8,128]{4,3,2,1,0:T(8,128)S(1)}, f32[4,6,3,8,128]{4,3,2,1,0:T(8,128)S(1)}, u32[]{:S(2)}, u32[]{:S(2)}) %collective-permute-start.5) | collective-permute-done | bytes 294944 | tf_op jit(solution)/shard_map/ppermute | solution.py:52
  34.3 0.9 shard_map.71.refs_0_
  35.1 1.5 %collective-permute-start.7 = (f32[4,6,3,8,128]{4,3,2,1,0:T(8,128)}, f32[4,6,3,8,128]{4,3,2,1,0:T(8,128)}, u32[]{:S(2)}, u32[]{:S(2)}) collective-permute-start(f32[4,6,3,8,128]{4,3,2,1,0:T(8,128)} %shard_map.71.refs_0_), channel_id=1, source_target_pairs={{0,16},{16,0},{1,17},{17,1},{2,18},{18,2},{3,19},{19,3},{4,20},{20... | collective-permute-start | bytes 884744 | tf_op jit(solution)/shard_map/ppermute | solution.py:549
  37.3 1.8 %reshape.32 = f32[6,32,2,128]{3,2,1,0:T(2,128)} reshape(f32[6,8192]{1,0:T(8,128)} %param.6) | data formatting | bytes 393216 | tf_op jit(solution)/shard_map/reshape | solution.py:508
  39.2 0.9 copy.8
  40.1 1.8 %collective-permute-start.4 = (f32[4,6,2,8,128]{4,3,2,1,0:T(8,128)}, f32[4,6,2,8,128]{4,3,2,1,0:T(8,128)S(1)}, u32[]{:S(2)}, u32[]{:S(2)}) collective-permute-start(f32[4,6,2,8,128]{4,3,2,1,0:T(8,128)} %copy-done.6), channel_id=1, source_target_pairs={{0,12},{4,0},{8,4},{12,8},{1,13},{5,1},{9,5},{13,9},{2,14},{6,2},{... | collective-permute-start | bytes 589832 | tf_op jit(solution)/shard_map/ppermute | solution.py:52
  41.9 0.3 collective-permute-start.3
  42.2 1.1 %copy-done.2 = f32[4,6,8,8,128]{4,3,2,1,0:T(8,128)S(1)} copy-done((f32[4,6,8,8,128]{4,3,2,1,0:T(8,128)S(1)}, f32[4,6,8,8,128]{4,3,2,1,0:T(8,128)}, u32[]{:S(2)}) %copy-start.2) | copy-done | bytes 786456
  43.3 6.4 %shard_map.70 = (f32[4,6,8,8,128]{4,3,2,1,0:T(8,128)S(1)}, f32[4,6,8,8,128]{4,3,2,1,0:T(8,128)S(1)}, f32[16,16,128]{2,1,0:T(8,128)S(1)}, f32[64,128]{1,0:T(8,128)S(1)}, f32[4,8,128]{2,1,0:T(8,128)S(1)}) custom-call(f32[4]{0:T(128)S(1)} %broadcast_subtract_fusion.shift_ref, f32[16,6,8,8,128]{4,3,2,1,0:T(8,128)S(1)} %get-tuple-element.24.planes_ref, ...), custom_call_target="tpu_custom_call" | custom-call | tf_op jit(solution)/shard_map/pallas_call | solution.py:32
  49.7 0.0 collective-permute-done.4.after_ref
  49.7 0.6 collective-permute-done.3.before_ref
  50.3 0.0 collective-permute-done.7.refs_1_
  50.3 2.3 %shard_map.72 = (f32[4,6,8,8,128]{4,3,2,1,0:T(8,128)S(1)}, f32[8,128]{1,0:T(8,128)S(1)}) custom-call(f32[16,6,8,8,128]{4,3,2,1,0:T(8,128)S(1)} %get-tuple-element.24.planes_ref, f32[4,6,8,8,128]{4,3,2,1,0:T(8,128)S(1)} %copy-done.3, f32[4,6,8,8,128]{4,3,2,1,0:T(8,128)S(1)} %get-tuple-element.28.partial_ref, f32[4,8,128]{2,1,0:T(8,128)S(1)} %get-tuple-element.29.square_ref, ...), custom_call_target="tpu_custom_call" | custom-call | tf_op jit(solution)/shard_map/pallas_call | solution.py:32
  52.6 3.0 %collective-permute-start.10 = (f32[8,128]{1,0:T(8,128)S(1)}, f32[8,128]{1,0:T(8,128)S(1)}, u32[]{:S(2)}, u32[]{:S(2)}) collective-permute-start(f32[8,128]{1,0:T(8,128)S(1)} %get-tuple-element.35.refs_0_), channel_id=1, source_target_pairs={{0,12},{4,8},{8,4},{12,0},{1,13},{5,9},{9,5},{13,1},{2,14},{6,10},... | collective-permute-start | bytes 12296 | tf_op jit(solution)/shard_map/ppermute | solution.py:46
  55.7 0.0 collective-permute-start.9
  55.7 1.4 %collective-permute-start.8 = (f32[8,128]{1,0:T(8,128)S(1)}, f32[8,128]{1,0:T(8,128)S(1)}, u32[]{:S(2)}, u32[]{:S(2)}) collective-permute-start(f32[8,128]{1,0:T(8,128)S(1)} %get-tuple-element.35.refs_0_), channel_id=1, source_target_pairs={{0,4},{4,0},{8,12},{12,8},{1,5},{5,1},{9,13},{13,9},{2,6},{6,2},{1... | collective-permute-start | bytes 12296 | tf_op jit(solution)/shard_map/ppermute | solution.py:46
  57.0 1.0 %collective-permute-done.10.refs_3_ = f32[8,128]{1,0:T(8,128)S(1)} collective-permute-done((f32[8,128]{1,0:T(8,128)S(1)}, f32[8,128]{1,0:T(8,128)S(1)}, u32[]{:S(2)}, u32[]{:S(2)}) %collective-permute-start.10) | collective-permute-done | bytes 4128 | tf_op jit(solution)/shard_map/ppermute | solution.py:46
  58.1 2.1 %collective-permute-done.9.refs_2_ = f32[8,128]{1,0:T(8,128)S(1)} collective-permute-done((f32[8,128]{1,0:T(8,128)S(1)}, f32[8,128]{1,0:T(8,128)S(1)}, u32[]{:S(2)}, u32[]{:S(2)}) %collective-permute-start.9) | collective-permute-done | bytes 4128 | tf_op jit(solution)/shard_map/ppermute | solution.py:46
  60.2 0.0 collective-permute-done.8.refs_1_
  60.2 1.2 %shard_map.73 = (f32[4,6,8,8,128]{4,3,2,1,0:T(8,128)S(1)}, f32[64,128]{1,0:T(8,128)S(1)}, f32[12,128]{1,0:T(8,128)S(1)}) custom-call(f32[16,6,8,8,128]{4,3,2,1,0:T(8,128)S(1)} %get-tuple-element.24.planes_ref, f32[4,6,8,8,128]{4,3,2,1,0:T(8,128)S(1)} %get-tuple-element.27.source_ref, f32[4,6,8,8,128]{4,3,2,1,0:T(8,128)S(1)} %get-tuple-element.32.applied_ref, ...), custom_call_target="tpu_custom_call" | custom-call | tf_op jit(solution)/shard_map/pallas_call | solution.py:32
  61.4 1.5 %collective-permute-start.11 = (f32[4,6,8,8,128]{4,3,2,1,0:T(8,128)S(1)}, f32[4,6,8,8,128]{4,3,2,1,0:T(8,128)S(1)}, u32[]{:S(2)}, u32[]{:S(2)}) collective-permute-start(f32[4,6,8,8,128]{4,3,2,1,0:T(8,128)S(1)} %get-tuple-element.36.ahead_ref), channel_id=1, source_target_pairs={{0,12},{4,0},{8,4},{12,8},{1,13},{5,1},{9,5},{13,9},{2,14},{6,2},{... | collective-permute-start | bytes 2359304 | tf_op jit(solution)/shard_map/ppermute | solution.py:52
  62.9 5.0 %shard_map.74 = (f32[4,6,8,8,128]{4,3,2,1,0:T(8,128)S(1)}, f32[12,8,128]{2,1,0:T(8,128)S(1)}) custom-call(f32[4]{0:T(128)S(1)} %broadcast_subtract_fusion.shift_ref, f32[16,6,8,8,128]{4,3,2,1,0:T(8,128)S(1)} %get-tuple-element.24.planes_ref, f32[6,8,8,128]{3,2,1,0:T(8,128)S(1)} %bitcast.28, f32[4,6,8,8,128]{4,3,2,1,0:T(8,128)S(1)} %get-tuple-element.27.source_ref, ...), custom_call_target="tpu_custom_call" | custom-call | tf_op jit(solution)/shard_map/pallas_call | solution.py:32
  67.8 9.6 %collective-permute-done.11.after_ref = f32[4,6,8,8,128]{4,3,2,1,0:T(8,128)S(1)} collective-permute-done((f32[4,6,8,8,128]{4,3,2,1,0:T(8,128)S(1)}, f32[4,6,8,8,128]{4,3,2,1,0:T(8,128)S(1)}, u32[]{:S(2)}, u32[]{:S(2)}) %collective-permute-start.11) | collective-permute-done | bytes 786464 | tf_op jit(solution)/shard_map/ppermute | solution.py:52
  77.5 0.3 shard_map.75.refs_0_
  77.8 3.3 %collective-permute-start.14 = (f32[8,128]{1,0:T(8,128)S(1)}, f32[8,128]{1,0:T(8,128)S(1)}, u32[]{:S(2)}, u32[]{:S(2)}) collective-permute-start(f32[8,128]{1,0:T(8,128)S(1)} %shard_map.75.refs_0_), channel_id=1, source_target_pairs={{0,12},{4,8},{8,4},{12,0},{1,13},{5,9},{9,5},{13,1},{2,14},{6,10},... | collective-permute-start | bytes 12296 | tf_op jit(solution)/shard_map/ppermute | solution.py:46
  81.1 0.0 collective-permute-start.13
  81.1 1.1 %collective-permute-start.12 = (f32[8,128]{1,0:T(8,128)S(1)}, f32[8,128]{1,0:T(8,128)S(1)}, u32[]{:S(2)}, u32[]{:S(2)}) collective-permute-start(f32[8,128]{1,0:T(8,128)S(1)} %shard_map.75.refs_0_), channel_id=1, source_target_pairs={{0,4},{4,0},{8,12},{12,8},{1,5},{5,1},{9,13},{13,9},{2,6},{6,2},{1... | collective-permute-start | bytes 12296 | tf_op jit(solution)/shard_map/ppermute | solution.py:46
  82.2 1.0 %collective-permute-done.14.refs_3_ = f32[8,128]{1,0:T(8,128)S(1)} collective-permute-done((f32[8,128]{1,0:T(8,128)S(1)}, f32[8,128]{1,0:T(8,128)S(1)}, u32[]{:S(2)}, u32[]{:S(2)}) %collective-permute-start.14) | collective-permute-done | bytes 4128 | tf_op jit(solution)/shard_map/ppermute | solution.py:46
  83.2 2.4 %collective-permute-done.13.refs_2_ = f32[8,128]{1,0:T(8,128)S(1)} collective-permute-done((f32[8,128]{1,0:T(8,128)S(1)}, f32[8,128]{1,0:T(8,128)S(1)}, u32[]{:S(2)}, u32[]{:S(2)}) %collective-permute-start.13) | collective-permute-done | bytes 4128 | tf_op jit(solution)/shard_map/ppermute | solution.py:46
  85.6 0.0 collective-permute-done.12.refs_1_
  85.6 0.3 shard_map.76
  86.0 0.1 collective-permute-start.17
  86.1 1.6 %collective-permute-start.16 = (f32[144,128]{1,0:T(8,128)S(1)}, f32[144,128]{1,0:T(8,128)S(1)}, u32[]{:S(2)}, u32[]{:S(2)}) collective-permute-start(f32[144,128]{1,0:T(8,128)S(1)} %get-tuple-element.47), channel_id=1, source_target_pairs={{0,2},{1,3},{2,0},{3,1},{4,6},{5,7},{6,4},{7,5},{8,10},{9,11},{10,... | collective-permute-start | bytes 221192 | tf_op jit(solution)/shard_map/ppermute | solution.py:52
  87.6 0.2 collective-permute-start.15
  87.8 0.3 collective-permute-done.17.refs_2_
  88.1 4.1 %collective-permute-done.16.refs_1_ = f32[144,128]{1,0:T(8,128)S(1)} collective-permute-done((f32[144,128]{1,0:T(8,128)S(1)}, f32[144,128]{1,0:T(8,128)S(1)}, u32[]{:S(2)}, u32[]{:S(2)}) %collective-permute-start.16) | collective-permute-done | bytes 73760 | tf_op jit(solution)/shard_map/ppermute | solution.py:52
  92.2 0.1 collective-permute-done.15.refs_0_
  92.3 0.2 collective-permute-start.18
  92.5 3.7 %collective-permute-start.19 = (f32[48,128]{1,0:T(8,128)S(1)}, f32[48,128]{1,0:T(8,128)S(1)}, u32[]{:S(2)}, u32[]{:S(2)}) collective-permute-start(f32[48,128]{1,0:T(8,128)S(1)} %get-tuple-element.45), channel_id=1, source_target_pairs={{0,12},{4,0},{8,4},{12,8},{1,13},{5,1},{9,5},{13,9},{2,14},{6,2},{... | collective-permute-start | bytes 73736 | tf_op jit(solution)/shard_map/ppermute | solution.py:52
  96.2 1.1 %shard_map.77 = f32[1536,128]{1,0:T(8,128)} custom-call(f32[4,6,8,8,128]{4,3,2,1,0:T(8,128)S(1)} %get-tuple-element.27.source_ref, f32[4,6,8,8,128]{4,3,2,1,0:T(8,128)S(1)} %get-tuple-element.39.residual_ref, f32[8,128]{1,0:T(8,128)S(1)} %get-tuple-element.41.scales_ref), custom_call_target="tpu_custom_call" | custom-call | tf_op jit(solution)/shard_map/pallas_call | solution.py:32
  97.2 0.7 collective-permute-done.18.before_ref
  98.0 0.0 collective-permute-done.19.after_ref
  98.0 0.9 shard_map.79
  (10 shorter events, 0.1 us)
Async XLA Ops:
  0.6 1.9 %copy-start = (f32[16,6,8192]{2,0,1:T(8,128)S(1)}, f32[16,6,8192]{2,0,1:T(8,128)}, u32[]{:S(2)}) copy-start(f32[16,6,8192]{2,0,1:T(8,128)} %param.5) | copy-start | bytes 9437188
  2.5 0.9 copy-start.4
  3.5 9.2 %copy-start.5 = (f32[6,8192]{1,0:T(8,128)S(1)}, f32[6,8192]{1,0:T(8,128)}, u32[]{:S(2)}) copy-start(f32[6,8192]{1,0:T(8,128)} %far_perturb_ref.1) | copy-start | bytes 589828
  6.9 35.3 %copy-start.7 = (f32[4]{0:T(128)S(1)}, f32[4]{0:T(128)}, u32[]{:S(2)}) copy-start(f32[4]{0:T(128)} %param.8) | copy-start | bytes 52
  6.9 7.6 %collective-permute-start.2 = (f32[24,16]{1,0:T(8,128)S(1)}, f32[24,16]{1,0:T(8,128)S(1)}, u32[]{:S(2)}, u32[]{:S(2)}) collective-permute-start(f32[24,16]{1,0:T(8,128)S(1)} %get-tuple-element.25.refs_0_), channel_id=1, source_target_pairs={{0,12},{4,8},{8,4},{12,0},{1,13},{5,9},{9,5},{13,1},{2,14},{6,10},... | collective-permute-start | bytes 4616 | tf_op jit(solution)/shard_map/ppermute | solution.py:46
  12.0 4.6 %collective-permute-start.1 = (f32[24,16]{1,0:T(8,128)S(1)}, f32[24,16]{1,0:T(8,128)S(1)}, u32[]{:S(2)}, u32[]{:S(2)}) collective-permute-start(f32[24,16]{1,0:T(8,128)S(1)} %get-tuple-element.25.refs_0_), channel_id=1, source_target_pairs={{0,8},{4,12},{8,0},{12,4},{1,9},{5,13},{9,1},{13,5},{2,10},{6,14},... | collective-permute-start | bytes 4616 | tf_op jit(solution)/shard_map/ppermute | solution.py:46
  12.0 4.6 %collective-permute-start = (f32[24,16]{1,0:T(8,128)S(1)}, f32[24,16]{1,0:T(8,128)S(1)}, u32[]{:S(2)}, u32[]{:S(2)}) collective-permute-start(f32[24,16]{1,0:T(8,128)S(1)} %get-tuple-element.25.refs_0_), channel_id=1, source_target_pairs={{0,4},{4,0},{8,12},{12,8},{1,5},{5,1},{9,13},{13,9},{2,6},{6,2},{1... | collective-permute-start | bytes 4616 | tf_op jit(solution)/shard_map/ppermute | solution.py:46
  17.8 0.9 copy-start.1
  18.7 0.7 copy-start.6
  19.4 9.1 %collective-permute-start.6 = (f32[4,6,3,8,128]{4,3,2,1,0:T(8,128)S(1)}, f32[4,6,3,8,128]{4,3,2,1,0:T(8,128)S(1)}, u32[]{:S(2)}, u32[]{:S(2)}) collective-permute-start(f32[4,6,3,8,128]{4,3,2,1,0:T(8,128)S(1)} %get-tuple-element.31), channel_id=1, source_target_pairs={{0,12},{4,0},{8,4},{12,8},{1,13},{5,1},{9,5},{13,9},{2,14},{6,2},{... | collective-permute-start | bytes 884744 | tf_op jit(solution)/shard_map/ppermute | solution.py:52
  21.0 13.3 %collective-permute-start.5 = (f32[4,6,3,8,128]{4,3,2,1,0:T(8,128)S(1)}, f32[4,6,3,8,128]{4,3,2,1,0:T(8,128)S(1)}, u32[]{:S(2)}, u32[]{:S(2)}) collective-permute-start(f32[4,6,3,8,128]{4,3,2,1,0:T(8,128)S(1)} %get-tuple-element.31), channel_id=1, source_target_pairs={{0,4},{4,8},{8,12},{12,0},{1,5},{5,9},{9,13},{13,1},{2,6},{6,10},{... | collective-permute-start | bytes 884744 | tf_op jit(solution)/shard_map/ppermute | solution.py:52
  35.1 15.2 %collective-permute-start.7 = (f32[4,6,3,8,128]{4,3,2,1,0:T(8,128)}, f32[4,6,3,8,128]{4,3,2,1,0:T(8,128)}, u32[]{:S(2)}, u32[]{:S(2)}) collective-permute-start(f32[4,6,3,8,128]{4,3,2,1,0:T(8,128)} %shard_map.71.refs_0_), channel_id=1, source_target_pairs={{0,16},{16,0},{1,17},{17,1},{2,18},{18,2},{3,19},{19,3},{4,20},{20... | collective-permute-start | bytes 884744 | tf_op jit(solution)/shard_map/ppermute | solution.py:549
  40.1 9.6 %collective-permute-start.4 = (f32[4,6,2,8,128]{4,3,2,1,0:T(8,128)}, f32[4,6,2,8,128]{4,3,2,1,0:T(8,128)S(1)}, u32[]{:S(2)}, u32[]{:S(2)}) collective-permute-start(f32[4,6,2,8,128]{4,3,2,1,0:T(8,128)} %copy-done.6), channel_id=1, source_target_pairs={{0,12},{4,0},{8,4},{12,8},{1,13},{5,1},{9,5},{13,9},{2,14},{6,2},{... | collective-permute-start | bytes 589832 | tf_op jit(solution)/shard_map/ppermute | solution.py:52
  41.9 8.4 %collective-permute-start.3 = (f32[4,6,2,8,128]{4,3,2,1,0:T(8,128)}, f32[4,6,2,8,128]{4,3,2,1,0:T(8,128)S(1)}, u32[]{:S(2)}, u32[]{:S(2)}) collective-permute-start(f32[4,6,2,8,128]{4,3,2,1,0:T(8,128)} %copy-done.6), channel_id=1, source_target_pairs={{0,4},{4,8},{8,12},{12,0},{1,5},{5,9},{9,13},{13,1},{2,6},{6,10},{... | collective-permute-start | bytes 589832 | tf_op jit(solution)/shard_map/ppermute | solution.py:52
  42.2 1.1 %copy-start.2 = (f32[4,6,8,8,128]{4,3,2,1,0:T(8,128)S(1)}, f32[4,6,8,8,128]{4,3,2,1,0:T(8,128)}, u32[]{:S(2)}) copy-start(f32[4,6,8,8,128]{4,3,2,1,0:T(8,128)} %copy-done.1) | copy-start | bytes 2359300
  43.3 7.0 %copy-start.3 = (f32[4,6,8,8,128]{4,3,2,1,0:T(8,128)S(1)}, f32[4,6,8,8,128]{4,3,2,1,0:T(8,128)}, u32[]{:S(2)}) copy-start(f32[4,6,8,8,128]{4,3,2,1,0:T(8,128)} %copy-done.1) | copy-start | bytes 2359300
  52.6 5.5 %collective-permute-start.10 = (f32[8,128]{1,0:T(8,128)S(1)}, f32[8,128]{1,0:T(8,128)S(1)}, u32[]{:S(2)}, u32[]{:S(2)}) collective-permute-start(f32[8,128]{1,0:T(8,128)S(1)} %get-tuple-element.35.refs_0_), channel_id=1, source_target_pairs={{0,12},{4,8},{8,4},{12,0},{1,13},{5,9},{9,5},{13,1},{2,14},{6,10},... | collective-permute-start | bytes 12296 | tf_op jit(solution)/shard_map/ppermute | solution.py:46
  55.7 4.5 %collective-permute-start.9 = (f32[8,128]{1,0:T(8,128)S(1)}, f32[8,128]{1,0:T(8,128)S(1)}, u32[]{:S(2)}, u32[]{:S(2)}) collective-permute-start(f32[8,128]{1,0:T(8,128)S(1)} %get-tuple-element.35.refs_0_), channel_id=1, source_target_pairs={{0,8},{4,12},{8,0},{12,4},{1,9},{5,13},{9,1},{13,5},{2,10},{6,14},... | collective-permute-start | bytes 12296 | tf_op jit(solution)/shard_map/ppermute | solution.py:46
  55.7 4.5 %collective-permute-start.8 = (f32[8,128]{1,0:T(8,128)S(1)}, f32[8,128]{1,0:T(8,128)S(1)}, u32[]{:S(2)}, u32[]{:S(2)}) collective-permute-start(f32[8,128]{1,0:T(8,128)S(1)} %get-tuple-element.35.refs_0_), channel_id=1, source_target_pairs={{0,4},{4,0},{8,12},{12,8},{1,5},{5,1},{9,13},{13,9},{2,6},{6,2},{1... | collective-permute-start | bytes 12296 | tf_op jit(solution)/shard_map/ppermute | solution.py:46
  61.4 16.1 %collective-permute-start.11 = (f32[4,6,8,8,128]{4,3,2,1,0:T(8,128)S(1)}, f32[4,6,8,8,128]{4,3,2,1,0:T(8,128)S(1)}, u32[]{:S(2)}, u32[]{:S(2)}) collective-permute-start(f32[4,6,8,8,128]{4,3,2,1,0:T(8,128)S(1)} %get-tuple-element.36.ahead_ref), channel_id=1, source_target_pairs={{0,12},{4,0},{8,4},{12,8},{1,13},{5,1},{9,5},{13,9},{2,14},{6,2},{... | collective-permute-start | bytes 2359304 | tf_op jit(solution)/shard_map/ppermute | solution.py:52
  77.8 5.4 %collective-permute-start.14 = (f32[8,128]{1,0:T(8,128)S(1)}, f32[8,128]{1,0:T(8,128)S(1)}, u32[]{:S(2)}, u32[]{:S(2)}) collective-permute-start(f32[8,128]{1,0:T(8,128)S(1)} %shard_map.75.refs_0_), channel_id=1, source_target_pairs={{0,12},{4,8},{8,4},{12,0},{1,13},{5,9},{9,5},{13,1},{2,14},{6,10},... | collective-permute-start | bytes 12296 | tf_op jit(solution)/shard_map/ppermute | solution.py:46
  81.1 4.5 %collective-permute-start.13 = (f32[8,128]{1,0:T(8,128)S(1)}, f32[8,128]{1,0:T(8,128)S(1)}, u32[]{:S(2)}, u32[]{:S(2)}) collective-permute-start(f32[8,128]{1,0:T(8,128)S(1)} %shard_map.75.refs_0_), channel_id=1, source_target_pairs={{0,8},{4,12},{8,0},{12,4},{1,9},{5,13},{9,1},{13,5},{2,10},{6,14},... | collective-permute-start | bytes 12296 | tf_op jit(solution)/shard_map/ppermute | solution.py:46
  81.1 4.5 %collective-permute-start.12 = (f32[8,128]{1,0:T(8,128)S(1)}, f32[8,128]{1,0:T(8,128)S(1)}, u32[]{:S(2)}, u32[]{:S(2)}) collective-permute-start(f32[8,128]{1,0:T(8,128)S(1)} %shard_map.75.refs_0_), channel_id=1, source_target_pairs={{0,4},{4,0},{8,12},{12,8},{1,5},{5,1},{9,13},{13,9},{2,6},{6,2},{1... | collective-permute-start | bytes 12296 | tf_op jit(solution)/shard_map/ppermute | solution.py:46
  86.0 2.0 %collective-permute-start.17 = (f32[144,128]{1,0:T(8,128)S(1)}, f32[144,128]{1,0:T(8,128)S(1)}, u32[]{:S(2)}, u32[]{:S(2)}) collective-permute-start(f32[144,128]{1,0:T(8,128)S(1)} %get-tuple-element.46), channel_id=1, source_target_pairs={{0,3},{1,0},{2,1},{3,2},{4,7},{5,4},{6,5},{7,6},{8,11},{9,8},{10,9... | collective-permute-start | bytes 221192 | tf_op jit(solution)/shard_map/ppermute | solution.py:52
  86.1 6.1 %collective-permute-start.16 = (f32[144,128]{1,0:T(8,128)S(1)}, f32[144,128]{1,0:T(8,128)S(1)}, u32[]{:S(2)}, u32[]{:S(2)}) collective-permute-start(f32[144,128]{1,0:T(8,128)S(1)} %get-tuple-element.47), channel_id=1, source_target_pairs={{0,2},{1,3},{2,0},{3,1},{4,6},{5,7},{6,4},{7,5},{8,10},{9,11},{10,... | collective-permute-start | bytes 221192 | tf_op jit(solution)/shard_map/ppermute | solution.py:52
  87.6 4.6 %collective-permute-start.15 = (f32[144,128]{1,0:T(8,128)S(1)}, f32[144,128]{1,0:T(8,128)S(1)}, u32[]{:S(2)}, u32[]{:S(2)}) collective-permute-start(f32[144,128]{1,0:T(8,128)S(1)} %get-tuple-element.48), channel_id=1, source_target_pairs={{0,1},{1,2},{2,3},{3,0},{4,5},{5,6},{6,7},{7,4},{8,9},{9,10},{10,1... | collective-permute-start | bytes 221192 | tf_op jit(solution)/shard_map/ppermute | solution.py:52
  92.3 5.7 %collective-permute-start.18 = (f32[48,128]{1,0:T(8,128)S(1)}, f32[48,128]{1,0:T(8,128)S(1)}, u32[]{:S(2)}, u32[]{:S(2)}) collective-permute-start(f32[48,128]{1,0:T(8,128)S(1)} %get-tuple-element.44), channel_id=1, source_target_pairs={{0,4},{4,8},{8,12},{12,0},{1,5},{5,9},{9,13},{13,1},{2,6},{6,10},{... | collective-permute-start | bytes 73736 | tf_op jit(solution)/shard_map/ppermute | solution.py:52
  92.5 5.5 %collective-permute-start.19 = (f32[48,128]{1,0:T(8,128)S(1)}, f32[48,128]{1,0:T(8,128)S(1)}, u32[]{:S(2)}, u32[]{:S(2)}) collective-permute-start(f32[48,128]{1,0:T(8,128)S(1)} %get-tuple-element.45), channel_id=1, source_target_pairs={{0,12},{4,0},{8,4},{12,8},{1,13},{5,1},{9,5},{13,9},{2,14},{6,2},{... | collective-permute-start | bytes 73736 | tf_op jit(solution)/shard_map/ppermute | solution.py:52

commit v2 on v1

--- a/solution.py
+++ b/solution.py
@@ -28,14 +28,14 @@
 f32 = jnp.float32
 
 
-def call(kernel, outs, scratch, smem, *args, far=0):
+def call(kernel, outs, scratch, smem, *args, far=0, limit=VMEM_LIMIT):
     return pl.pallas_call(
         kernel,
         out_shape=[jax.ShapeDtypeStruct(s, f32) for s in outs],
         in_specs=[SMEM] * smem + [HBM] * far + [VMEM] * (len(args) - smem - far),
         out_specs=[VMEM] * len(outs),
         scratch_shapes=[pltpu.VMEM(s, f32) if isinstance(s, tuple) else s for s in scratch],
-        compiler_params=pltpu.CompilerParams(vmem_limit_bytes=VMEM_LIMIT),
+        compiler_params=pltpu.CompilerParams(vmem_limit_bytes=limit),
     )(*args)
 
 
@@ -136,6 +136,19 @@
     gram_ref[norb:, :] = total[2 * norb : 2 * norb + SUB] + total[2 * norb + SUB :]
 
 
+def tile_kernel(shape, *refs):
+    layers, halves = shape
+    count = len(refs) // 2
+    for array_ref, planes_ref in zip(refs[:count], refs[count:]):
+        for z in range(layers):
+            for y in range(NY):
+                for h in range(halves):
+                    c = y * halves + h
+                    planes_ref[z, h * (NY // SUB) + y // SUB, y % SUB : y % SUB + 1, :] = array_ref[
+                        z : z + 1, c * LANES : (c + 1) * LANES
+                    ]
+
+
 def small_matrices(shape, ncell, gram_refs, lines_ref):
     norb, group = shape
     total = add_all(gram_refs)
@@ -203,7 +216,7 @@
     return pltpu.roll(value, amount % NY, 0)
 
 
-def local_kernel(shape, ncell, shift_ref, planes_ref, perturb_ref, potential_ref, inner_ref, *refs):
+def local_kernel(shape, ncell, omega_ref, energies_ref, planes_ref, perturb_ref, potential_ref, inner_ref, *refs):
     norb, layers, group, parts, halves = shape
     gram_refs = refs[:parts]
     source_ref, partial_ref, overlap_ref, along_ref, square_ref, coef_ref, lines_ref = refs[parts:]
@@ -237,7 +250,7 @@
                     around = right[h] + left[h] + roll_y(sheets[h], k) + roll_y(sheets[h], -k)
                     sums[h] = sums[h] + COEFFS[k] * around
             total = jnp.stack(sums).reshape(inner_ref.shape[2:])
-            shift = potential_ref[z] + shift_ref[n]
+            shift = potential_ref[z] + (omega_ref[0] - energies_ref[n])
             partial_ref[n, z] = shift * inner_ref[n, z] - 0.5 * total
             return carry
 
@@ -264,16 +277,18 @@
     return total
 
 
-def halo_kernel(shape, before_ref, after_ref, halo_ref):
+def halo_kernel(shape, before_ref, after_ref, square_ref, *halo_refs):
     layers, group = shape
+    each = group // len(halo_refs)
     for n in range(group):
         for z in range(layers):
-            halo_ref[n, z] = halo_sum(layers, n, z, before_ref, after_ref)
+            halo_refs[n // each][n % each, z] = halo_sum(layers, n, z, before_ref, after_ref)
 
 
 def image_kernel(shape, planes_ref, inner_ref, partial_ref, square_ref, before_ref, after_ref, *refs):
     norb, layers, group, share = shape
     applied_ref, sums_ref, acc_ref = refs[-3:]
+    pieces = (len(refs) - 3) // 2
     place = lax.axis_index("freq") * share
     acc_ref[...] = jnp.zeros_like(acc_ref)
     for n in range(group):
@@ -283,8 +298,9 @@
             )
             if share:
                 mine, other = pl.ds(place, share), pl.ds(share - place, share)
-                applied_ref[n, z, mine] = partial_ref[n, z, mine] + refs[0][n, z]
-                applied_ref[n, z, other] = partial_ref[n, z, other] + refs[1][n, z]
+                piece, i = divmod(n, group // pieces)
+                applied_ref[n, z, mine] = partial_ref[n, z, mine] + refs[piece][i, z]
+                applied_ref[n, z, other] = partial_ref[n, z, other] + refs[pieces + piece][i, z]
 
     def layer(z, carry):
         fields = [applied_ref[n, z] for n in range(group)]
@@ -334,7 +350,7 @@
     combine(layers, group, norb, planes_ref, coef_ref, start, finish)
 
 
-def second_kernel(shape, shift_ref, planes_ref, potential_ref, source_ref, applied_ref, ahead_ref, plain_ref, numbers_ref, residual_ref, acc_ref):
+def second_kernel(shape, omega_ref, energies_ref, planes_ref, potential_ref, source_ref, applied_ref, ahead_ref, plain_ref, numbers_ref, residual_ref, acc_ref):
     norb, layers, group, halves = shape
     acc_ref[...] = jnp.zeros_like(acc_ref)
 
@@ -359,7 +375,7 @@
                 for h in range(halves):
                     sums[h] = sums[h] - COEFFS[k] * (right[h] + roll_y(sheets[h], k))
             total = jnp.stack(sums).reshape(whole.shape)
-            total = total + (potential_ref[z] + shift_ref[n]) * whole
+            total = total + (potential_ref[z] + (omega_ref[0] - energies_ref[n])) * whole
             acc_ref[n] += jnp.sum(whole * total, axis=0)
             acc_ref[group + n] += jnp.sum(whole * applied_ref[n, z], axis=0)
             return carry
@@ -503,12 +519,6 @@
     spots = tiles // SUB
     rows = orbitals.transpose(1, 0, 2).reshape(layers, norb // SUB, SUB, tiles, LANES)
     rows = rows.transpose(0, 1, 3, 2, 4).reshape(layers * norb * tiles, LANES)
-
-    def as_planes(array):
-        array = array.reshape(layers, NY, halves, LANES).transpose(0, 2, 1, 3)
-        return array.reshape(layers, spots, SUB, LANES)
-
-    shift = omega[0] - energies
     own = (group, layers, spots, SUB, LANES)
     flat = (group * norb, LANES)
 
@@ -526,9 +536,13 @@
         rows,
         perturb,
         far=2,
+        limit=48 * 1024 * 1024,
     )
     grams = parts_of(gram, "brick")
-    perturb_planes, potential_planes = as_planes(perturb), as_planes(potential)
+    plane = (layers, spots, SUB, LANES)
+    perturb_planes, potential_planes = call(
+        functools.partial(tile_kernel, (layers, halves)), [plane, plane], [], 0, perturb, potential
+    )
     share = 3 * spots // 8 if lax.axis_size("freq") == 2 else 0
     cells = (SUB, LANES)
     inner, rest, *shared = call(
@@ -540,26 +554,34 @@
         perturb_planes,
         *grams,
     )
-    halos = []
-    if share:
-        before, after = shifted(shared[0], "brick", 1), shifted(shared[0], "brick", -1)
-        halos = call(
-            functools.partial(halo_kernel, (layers, group)), [shared[0].shape], [], 0, before, after
-        )
-        halos = [halos[0], lax.ppermute(halos[0], "freq", [(0, 1), (1, 0)])]
-    before, after = shifted(rest, "brick", 1), shifted(rest, "brick", -1)
     source, partial, overlap, along, square = call(
         functools.partial(local_kernel, (norb, layers, group, len(grams), halves), ncell),
         [own, own, (norb, norb, LANES), flat, (group, SUB, LANES)],
         [flat, (SUB, norb)],
-        1,
-        shift,
+        2,
+        omega,
+        energies,
         planes,
         perturb_planes,
         potential_planes,
         inner,
         *grams,
     )
+    halos = []
+    pieces = 1 if group % 2 else 2
+    if share:
+        before, after = shifted(shared[0], "brick", 1), shifted(shared[0], "brick", -1)
+        halos = call(
+            functools.partial(halo_kernel, (layers, group)),
+            [(group // pieces, layers, share) + cells] * pieces,
+            [],
+            0,
+            before,
+            after,
+            square,
+        )
+        halos = [*halos] + [lax.ppermute(halo, "freq", [(0, 1), (1, 0)]) for halo in halos]
+    before, after = shifted(rest, "brick", 1), shifted(rest, "brick", -1)
     applied, sums = call(
         functools.partial(image_kernel, (norb, layers, group, share)),
         [own, cells],
@@ -591,8 +613,9 @@
         functools.partial(second_kernel, (norb, layers, group, halves)),
         [own, (3 * group, SUB, LANES)],
         [],
-        1,
-        shift,
+        2,
+        omega,
+        energies,
         planes,
         potential_planes,
         source,

time: 99.2 us -> 88 us (0.89)
  local copies, waits for them, and re-layouts: 10.1 us -> 0.97 us
  waiting for transfers between devices: 37 us -> 33.4 us
  starting transfers between devices: 27.4 us -> 29.7 us
    ppermute x10, waiting for transfers between devices: 28.3 us -> 22.7 us  [shifted(): lax.ppermute(array, axis, [(i, (i + step) % size) for i in range(size)])]
    unnamed x16 -> x6, local copies, waits for them, and re-layouts: 5.53 us -> 0.95 us
    reshape x4 -> x0, local copies, waits for them, and re-layouts: 4.56 us -> none  [as_planes(): array = array.reshape(layers, NY, halves, LANES).transpose(0, 2, 1, 3)]
    ppermute x10, starting transfers between devices: 11.3 us -> 13 us  [shifted(): lax.ppermute(array, axis, [(i, (i + step) % size) for i in range(size)])]
    ppermute x1 -> x2, waiting for transfers between devices: 0.01 us -> 1.43 us  [per_device(): lax.ppermute(halo, 'freq', [(0, 1), (1, 0)])]
    pallas_call x12 -> x13, Pallas kernels: 22.9 us -> 22.3 us  [call(): pl.pallas_call(kernel, out_shape=[jax.ShapeDtypeStruct(s, f32) for s in o...]
    ppermute x1 -> x2, starting transfers between devices: 1.54 us -> 2.09 us  [per_device(): lax.ppermute(halo, 'freq', [(0, 1), (1, 0)])]
  transfers between devices with their start and end apart: 20 -> 21, of which waited for: 13 -> 14; matrix products, arithmetic and copies ran while one was open for 5% -> 0% of each run, Pallas kernels for 13% -> 15%
where the time goes in v2:
time: 88 us; the launch traced here: 87.8 us
  waiting for transfers between devices  33.4 us (38%)
  starting transfers between devices  29.7 us (34%)
  Pallas kernels  22.3 us (25%)
  between operations  1.4 us (2%)
  local copies, waits for them, and re-layouts  0.97 us (1%)
    ppermute x10, waiting for transfers between devices, shifted(): lax.ppermute(array, axis, [(i, (i + step) % size) for i in range(size)])  22.7 us
    pallas_call x13, Pallas kernels, call(): pl.pallas_call(kernel, out_shape=[jax.ShapeDtypeStruct(s, f32) for s in o...  22.3 us
    ppermute x9, starting transfers between devices, parts_of(): lax.ppermute(array, axis, [(i, i ^ k) for i in range(size)])  14.6 us
    ppermute x10, starting transfers between devices, shifted(): lax.ppermute(array, axis, [(i, (i + step) % size) for i in range(size)])  13 us
    ppermute x9, waiting for transfers between devices, parts_of(): lax.ppermute(array, axis, [(i, i ^ k) for i in range(size)])  9.35 us
    ppermute x2, starting transfers between devices, per_device(): lax.ppermute(halo, 'freq', [(0, 1), (1, 0)])  2.09 us
  transfers between devices with their start and end apart: 21, of which 14 were waited for; matrix products, arithmetic and copies ran while one was open for 0% of the time, Pallas kernels for 15%

profile of v2, /device:TPU:0, one launch (start us, length us, event | category | flops | bytes accessed | tf_op | source)
XLA Modules:
  0.0 87.8 jit_solution(12277745090965413101)
XLA Ops:
  0.6 0.0 copy-start
  0.6 0.9 %copy-done = f32[6,8192]{1,0:T(8,128)S(1)} copy-done((f32[6,8192]{1,0:T(8,128)S(1)}, f32[6,8192]{1,0:T(8,128)}, u32[]{:S(2)}) %copy-start) | copy-done | bytes 196632
  1.6 0.0 copy-start.1
  1.6 0.0 copy-start.2
  1.6 4.3 %shard_map.68 = (f32[16,6,8,8,128]{4,3,2,1,0:T(8,128)S(1)}, f32[24,16]{1,0:T(8,128)S(1)}) custom-call(f32[6144,128]{1,0:T(8,128)} %bitcast.18, f32[6,8192]{1,0:T(8,128)S(1)} %copy-done), custom_call_target="tpu_custom_call" | custom-call | tf_op jit(solution)/shard_map/pallas_call | solution.py:32
  5.9 5.1 %collective-permute-start.2 = (f32[24,16]{1,0:T(8,128)S(1)}, f32[24,16]{1,0:T(8,128)S(1)}, u32[]{:S(2)}, u32[]{:S(2)}) collective-permute-start(f32[24,16]{1,0:T(8,128)S(1)} %get-tuple-element.31.refs_0_), channel_id=1, source_target_pairs={{0,12},{4,8},{8,4},{12,0},{1,13},{5,9},{9,5},{13,1},{2,14},{6,10},... | collective-permute-start | bytes 4616 | tf_op jit(solution)/shard_map/ppermute | solution.py:46
  11.0 0.0 collective-permute-start.1
  11.0 0.6 collective-permute-start
  11.6 0.0 copy-done.1
  11.6 0.3 shard_map.69
  11.9 0.8 collective-permute-done.2.refs_3_
  12.7 2.9 %collective-permute-done.1.refs_2_ = f32[24,16]{1,0:T(8,128)S(1)} collective-permute-done((f32[24,16]{1,0:T(8,128)S(1)}, f32[24,16]{1,0:T(8,128)S(1)}, u32[]{:S(2)}, u32[]{:S(2)}) %collective-permute-start.1) | collective-permute-done | bytes 1568 | tf_op jit(solution)/shard_map/ppermute | solution.py:46
  15.6 0.0 collective-permute-done.refs_1_
  15.6 1.2 %shard_map.70 = (f32[4,6,8,8,128]{4,3,2,1,0:T(8,128)S(1)}, f32[4,6,2,8,128]{4,3,2,1,0:T(8,128)S(1)}, f32[4,6,3,8,128]{4,3,2,1,0:T(8,128)S(1)}) custom-call(f32[16,6,8,8,128]{4,3,2,1,0:T(8,128)S(1)} %get-tuple-element.28.planes_ref, f32[6,8,8,128]{3,2,1,0:T(8,128)S(1)} %get-tuple-element.29.perturb_ref, f32[24,16]{1,0:T(8,128)S(1)} %get-tuple-element.31.refs_0_, ...), custom_call_target="tpu_custom_call" | custom-call | tf_op jit(solution)/shard_map/pallas_call | solution.py:32
  16.7 1.5 %collective-permute-start.6 = (f32[4,6,3,8,128]{4,3,2,1,0:T(8,128)S(1)}, f32[4,6,3,8,128]{4,3,2,1,0:T(8,128)S(1)}, u32[]{:S(2)}, u32[]{:S(2)}) collective-permute-start(f32[4,6,3,8,128]{4,3,2,1,0:T(8,128)S(1)} %get-tuple-element.37), channel_id=1, source_target_pairs={{0,12},{4,0},{8,4},{12,8},{1,13},{5,1},{9,5},{13,9},{2,14},{6,2},{... | collective-permute-start | bytes 884744 | tf_op jit(solution)/shard_map/ppermute | solution.py:52
  18.3 0.6 collective-permute-start.5
  18.8 3.3 %collective-permute-start.4 = (f32[4,6,2,8,128]{4,3,2,1,0:T(8,128)S(1)}, f32[4,6,2,8,128]{4,3,2,1,0:T(8,128)S(1)}, u32[]{:S(2)}, u32[]{:S(2)}) collective-permute-start(f32[4,6,2,8,128]{4,3,2,1,0:T(8,128)S(1)} %get-tuple-element.36), channel_id=1, source_target_pairs={{0,12},{4,0},{8,4},{12,8},{1,13},{5,1},{9,5},{13,9},{2,14},{6,2},{... | collective-permute-start | bytes 589832 | tf_op jit(solution)/shard_map/ppermute | solution.py:52
  22.1 0.0 collective-permute-start.3
  22.7 0.0 copy-done.2
  22.7 6.4 %shard_map.71 = (f32[4,6,8,8,128]{4,3,2,1,0:T(8,128)S(1)}, f32[4,6,8,8,128]{4,3,2,1,0:T(8,128)S(1)}, f32[16,16,128]{2,1,0:T(8,128)S(1)}, f32[64,128]{1,0:T(8,128)S(1)}, f32[4,8,128]{2,1,0:T(8,128)S(1)}) custom-call(f32[1]{0:T(128)S(6)} %copy.8.omega_ref, f32[4]{0:T(128)S(1)} %copy-done.2, f32[16,6,8,8,128]{4,3,2,1,0:T(8,128)S(1)} %get-tuple-element.28.planes_ref, ...), custom_call_target="tpu_custom_call" | custom-call | tf_op jit(solution)/shard_map/pallas_call | solution.py:32
  29.2 1.4 %collective-permute-done.6.after_ref = f32[4,6,3,8,128]{4,3,2,1,0:T(8,128)S(1)} collective-permute-done((f32[4,6,3,8,128]{4,3,2,1,0:T(8,128)S(1)}, f32[4,6,3,8,128]{4,3,2,1,0:T(8,128)S(1)}, u32[]{:S(2)}, u32[]{:S(2)}) %collective-permute-start.6) | collective-permute-done | bytes 294944 | tf_op jit(solution)/shard_map/ppermute | solution.py:52
  30.6 4.1 %collective-permute-done.5.before_ref = f32[4,6,3,8,128]{4,3,2,1,0:T(8,128)S(1)} collective-permute-done((f32[4,6,3,8,128]{4,3,2,1,0:T(8,128)S(1)}, f32[4,6,3,8,128]{4,3,2,1,0:T(8,128)S(1)}, u32[]{:S(2)}, u32[]{:S(2)}) %collective-permute-start.5) | collective-permute-done | bytes 294944 | tf_op jit(solution)/shard_map/ppermute | solution.py:52
  34.6 0.1 shard_map.72
  34.8 1.6 %collective-permute-start.7 = (f32[2,6,3,8,128]{4,3,2,1,0:T(8,128)S(1)}, f32[2,6,3,8,128]{4,3,2,1,0:T(8,128)S(1)}, u32[]{:S(2)}, u32[]{:S(2)}) collective-permute-start(f32[2,6,3,8,128]{4,3,2,1,0:T(8,128)S(1)} %get-tuple-element.38.refs_0_), channel_id=1, source_target_pairs={{0,16},{16,0},{1,17},{17,1},{2,18},{18,2},{3,19},{19,3},{4,20},{20... | collective-permute-start | bytes 442376 | tf_op jit(solution)/shard_map/ppermute | solution.py:583
  36.4 0.5 collective-permute-start.8
  36.9 0.0 collective-permute-done.4.after_ref
  36.9 3.3 %collective-permute-done.3.before_ref = f32[4,6,2,8,128]{4,3,2,1,0:T(8,128)S(1)} collective-permute-done((f32[4,6,2,8,128]{4,3,2,1,0:T(8,128)S(1)}, f32[4,6,2,8,128]{4,3,2,1,0:T(8,128)S(1)}, u32[]{:S(2)}, u32[]{:S(2)}) %collective-permute-start.3) | collective-permute-done | bytes 196640 | tf_op jit(solution)/shard_map/ppermute | solution.py:52
  40.1 0.0 collective-permute-done.7.refs_2_
  40.1 1.4 %collective-permute-done.8.refs_3_ = f32[2,6,3,8,128]{4,3,2,1,0:T(8,128)S(1)} collective-permute-done((f32[2,6,3,8,128]{4,3,2,1,0:T(8,128)S(1)}, f32[2,6,3,8,128]{4,3,2,1,0:T(8,128)S(1)}, u32[]{:S(2)}, u32[]{:S(2)}) %collective-permute-start.8) | collective-permute-done | bytes 147488 | tf_op jit(solution)/shard_map/ppermute | solution.py:583
  41.6 1.3 %shard_map.73 = (f32[4,6,8,8,128]{4,3,2,1,0:T(8,128)S(1)}, f32[8,128]{1,0:T(8,128)S(1)}) custom-call(f32[16,6,8,8,128]{4,3,2,1,0:T(8,128)S(1)} %get-tuple-element.28.planes_ref, f32[4,6,8,8,128]{4,3,2,1,0:T(8,128)S(1)} %get-tuple-element.32.inner_ref, f32[4,6,8,8,128]{4,3,2,1,0:T(8,128)S(1)} %get-tuple-element.34.partial_ref, ...), custom_call_target="tpu_custom_call" | custom-call | tf_op jit(solution)/shard_map/pallas_call | solution.py:32
  42.8 2.0 %collective-permute-start.11 = (f32[8,128]{1,0:T(8,128)S(1)}, f32[8,128]{1,0:T(8,128)S(1)}, u32[]{:S(2)}, u32[]{:S(2)}) collective-permute-start(f32[8,128]{1,0:T(8,128)S(1)} %get-tuple-element.43.refs_0_), channel_id=1, source_target_pairs={{0,12},{4,8},{8,4},{12,0},{1,13},{5,9},{9,5},{13,1},{2,14},{6,10},... | collective-permute-start | bytes 12296 | tf_op jit(solution)/shard_map/ppermute | solution.py:46
  44.8 0.0 collective-permute-start.10
  44.8 2.4 %collective-permute-start.9 = (f32[8,128]{1,0:T(8,128)S(1)}, f32[8,128]{1,0:T(8,128)S(1)}, u32[]{:S(2)}, u32[]{:S(2)}) collective-permute-start(f32[8,128]{1,0:T(8,128)S(1)} %get-tuple-element.43.refs_0_), channel_id=1, source_target_pairs={{0,4},{4,0},{8,12},{12,8},{1,5},{5,1},{9,13},{13,9},{2,6},{6,2},{1... | collective-permute-start | bytes 12296 | tf_op jit(solution)/shard_map/ppermute | solution.py:46
  47.3 1.0 %collective-permute-done.11.refs_3_ = f32[8,128]{1,0:T(8,128)S(1)} collective-permute-done((f32[8,128]{1,0:T(8,128)S(1)}, f32[8,128]{1,0:T(8,128)S(1)}, u32[]{:S(2)}, u32[]{:S(2)}) %collective-permute-start.11) | collective-permute-done | bytes 4128 | tf_op jit(solution)/shard_map/ppermute | solution.py:46
  48.3 1.0 %collective-permute-done.10.refs_2_ = f32[8,128]{1,0:T(8,128)S(1)} collective-permute-done((f32[8,128]{1,0:T(8,128)S(1)}, f32[8,128]{1,0:T(8,128)S(1)}, u32[]{:S(2)}, u32[]{:S(2)}) %collective-permute-start.10) | collective-permute-done | bytes 4128 | tf_op jit(solution)/shard_map/ppermute | solution.py:46
  49.3 0.0 collective-permute-done.9.refs_1_
  49.3 1.2 %shard_map.74 = (f32[4,6,8,8,128]{4,3,2,1,0:T(8,128)S(1)}, f32[64,128]{1,0:T(8,128)S(1)}, f32[12,128]{1,0:T(8,128)S(1)}) custom-call(f32[16,6,8,8,128]{4,3,2,1,0:T(8,128)S(1)} %get-tuple-element.28.planes_ref, f32[4,6,8,8,128]{4,3,2,1,0:T(8,128)S(1)} %get-tuple-element.33.source_ref, f32[4,6,8,8,128]{4,3,2,1,0:T(8,128)S(1)} %get-tuple-element.40.applied_ref, ...), custom_call_target="tpu_custom_call" | custom-call | tf_op jit(solution)/shard_map/pallas_call | solution.py:32
  50.5 1.9 %collective-permute-start.12 = (f32[4,6,8,8,128]{4,3,2,1,0:T(8,128)S(1)}, f32[4,6,8,8,128]{4,3,2,1,0:T(8,128)S(1)}, u32[]{:S(2)}, u32[]{:S(2)}) collective-permute-start(f32[4,6,8,8,128]{4,3,2,1,0:T(8,128)S(1)} %get-tuple-element.44.ahead_ref), channel_id=1, source_target_pairs={{0,12},{4,0},{8,4},{12,8},{1,13},{5,1},{9,5},{13,9},{2,14},{6,2},{... | collective-permute-start | bytes 2359304 | tf_op jit(solution)/shard_map/ppermute | solution.py:52
  52.4 5.0 %shard_map.75 = (f32[4,6,8,8,128]{4,3,2,1,0:T(8,128)S(1)}, f32[12,8,128]{2,1,0:T(8,128)S(1)}) custom-call(f32[1]{0:T(128)S(6)} %copy.8.omega_ref, f32[4]{0:T(128)S(1)} %copy-done.2, f32[16,6,8,8,128]{4,3,2,1,0:T(8,128)S(1)} %get-tuple-element.28.planes_ref, f32[6,8,8,128]{3,2,1,0:T(8,128)S(1)} %get-tuple-element.30.potential_ref, ...), custom_call_target="tpu_custom_call" | custom-call | tf_op jit(solution)/shard_map/pallas_call | solution.py:32
  57.4 8.8 %collective-permute-done.12.after_ref = f32[4,6,8,8,128]{4,3,2,1,0:T(8,128)S(1)} collective-permute-done((f32[4,6,8,8,128]{4,3,2,1,0:T(8,128)S(1)}, f32[4,6,8,8,128]{4,3,2,1,0:T(8,128)S(1)}, u32[]{:S(2)}, u32[]{:S(2)}) %collective-permute-start.12) | collective-permute-done | bytes 786464 | tf_op jit(solution)/shard_map/ppermute | solution.py:52
  66.2 0.3 shard_map.76.refs_0_
  66.5 3.5 %collective-permute-start.15 = (f32[8,128]{1,0:T(8,128)S(1)}, f32[8,128]{1,0:T(8,128)S(1)}, u32[]{:S(2)}, u32[]{:S(2)}) collective-permute-start(f32[8,128]{1,0:T(8,128)S(1)} %shard_map.76.refs_0_), channel_id=1, source_target_pairs={{0,12},{4,8},{8,4},{12,0},{1,13},{5,9},{9,5},{13,1},{2,14},{6,10},... | collective-permute-start | bytes 12296 | tf_op jit(solution)/shard_map/ppermute | solution.py:46
  70.0 0.0 collective-permute-start.14
  70.0 0.9 %collective-permute-start.13 = (f32[8,128]{1,0:T(8,128)S(1)}, f32[8,128]{1,0:T(8,128)S(1)}, u32[]{:S(2)}, u32[]{:S(2)}) collective-permute-start(f32[8,128]{1,0:T(8,128)S(1)} %shard_map.76.refs_0_), channel_id=1, source_target_pairs={{0,4},{4,0},{8,12},{12,8},{1,5},{5,1},{9,13},{13,9},{2,6},{6,2},{1... | collective-permute-start | bytes 12296 | tf_op jit(solution)/shard_map/ppermute | solution.py:46
  70.9 1.0 %collective-permute-done.15.refs_3_ = f32[8,128]{1,0:T(8,128)S(1)} collective-permute-done((f32[8,128]{1,0:T(8,128)S(1)}, f32[8,128]{1,0:T(8,128)S(1)}, u32[]{:S(2)}, u32[]{:S(2)}) %collective-permute-start.15) | collective-permute-done | bytes 4128 | tf_op jit(solution)/shard_map/ppermute | solution.py:46
  71.9 2.6 %collective-permute-done.14.refs_2_ = f32[8,128]{1,0:T(8,128)S(1)} collective-permute-done((f32[8,128]{1,0:T(8,128)S(1)}, f32[8,128]{1,0:T(8,128)S(1)}, u32[]{:S(2)}, u32[]{:S(2)}) %collective-permute-start.14) | collective-permute-done | bytes 4128 | tf_op jit(solution)/shard_map/ppermute | solution.py:46
  74.5 0.0 collective-permute-done.13.refs_1_
  74.5 0.3 shard_map.77
  74.9 0.1 collective-permute-start.18
  75.0 1.7 %collective-permute-start.17 = (f32[144,128]{1,0:T(8,128)S(1)}, f32[144,128]{1,0:T(8,128)S(1)}, u32[]{:S(2)}, u32[]{:S(2)}) collective-permute-start(f32[144,128]{1,0:T(8,128)S(1)} %get-tuple-element.55), channel_id=1, source_target_pairs={{0,2},{1,3},{2,0},{3,1},{4,6},{5,7},{6,4},{7,5},{8,10},{9,11},{10,... | collective-permute-start | bytes 221192 | tf_op jit(solution)/shard_map/ppermute | solution.py:52
  76.6 0.2 collective-permute-start.16
  76.8 0.1 collective-permute-done.18.refs_2_
  76.9 4.3 %collective-permute-done.17.refs_1_ = f32[144,128]{1,0:T(8,128)S(1)} collective-permute-done((f32[144,128]{1,0:T(8,128)S(1)}, f32[144,128]{1,0:T(8,128)S(1)}, u32[]{:S(2)}, u32[]{:S(2)}) %collective-permute-start.17) | collective-permute-done | bytes 73760 | tf_op jit(solution)/shard_map/ppermute | solution.py:52
  81.2 0.0 collective-permute-done.16.refs_0_
  81.2 0.1 collective-permute-start.19
  81.3 3.8 %collective-permute-start.20 = (f32[48,128]{1,0:T(8,128)S(1)}, f32[48,128]{1,0:T(8,128)S(1)}, u32[]{:S(2)}, u32[]{:S(2)}) collective-permute-start(f32[48,128]{1,0:T(8,128)S(1)} %get-tuple-element.53), channel_id=1, source_target_pairs={{0,12},{4,0},{8,4},{12,8},{1,13},{5,1},{9,5},{13,9},{2,14},{6,2},{... | collective-permute-start | bytes 73736 | tf_op jit(solution)/shard_map/ppermute | solution.py:52
  85.1 1.1 %shard_map.78 = f32[1536,128]{1,0:T(8,128)} custom-call(f32[4,6,8,8,128]{4,3,2,1,0:T(8,128)S(1)} %get-tuple-element.33.source_ref, f32[4,6,8,8,128]{4,3,2,1,0:T(8,128)S(1)} %get-tuple-element.47.residual_ref, f32[8,128]{1,0:T(8,128)S(1)} %get-tuple-element.49.scales_ref), custom_call_target="tpu_custom_call" | custom-call | tf_op jit(solution)/shard_map/pallas_call | solution.py:32
  86.2 0.7 collective-permute-done.19.before_ref
  86.9 0.0 collective-permute-done.20.after_ref
  86.9 0.9 shard_map.80
  (2 shorter events, 0.0 us)
Async XLA Ops:
  0.6 1.0 %copy-start = (f32[6,8192]{1,0:T(8,128)S(1)}, f32[6,8192]{1,0:T(8,128)}, u32[]{:S(2)}) copy-start(f32[6,8192]{1,0:T(8,128)} %refs_0_.1) | copy-start | bytes 589828
  1.6 10.0 %copy-start.1 = (f32[6,8192]{1,0:T(8,128)S(1)}, f32[6,8192]{1,0:T(8,128)}, u32[]{:S(2)}) copy-start(f32[6,8192]{1,0:T(8,128)} %refs_1_.1) | copy-start | bytes 589828
  1.6 21.2 %copy-start.2 = (f32[4]{0:T(128)S(1)}, f32[4]{0:T(128)}, u32[]{:S(2)}) copy-start(f32[4]{0:T(128)} %energies_ref.3) | copy-start | bytes 52
  5.9 6.8 %collective-permute-start.2 = (f32[24,16]{1,0:T(8,128)S(1)}, f32[24,16]{1,0:T(8,128)S(1)}, u32[]{:S(2)}, u32[]{:S(2)}) collective-permute-start(f32[24,16]{1,0:T(8,128)S(1)} %get-tuple-element.31.refs_0_), channel_id=1, source_target_pairs={{0,12},{4,8},{8,4},{12,0},{1,13},{5,9},{9,5},{13,1},{2,14},{6,10},... | collective-permute-start | bytes 4616 | tf_op jit(solution)/shard_map/ppermute | solution.py:46
  11.0 4.6 %collective-permute-start.1 = (f32[24,16]{1,0:T(8,128)S(1)}, f32[24,16]{1,0:T(8,128)S(1)}, u32[]{:S(2)}, u32[]{:S(2)}) collective-permute-start(f32[24,16]{1,0:T(8,128)S(1)} %get-tuple-element.31.refs_0_), channel_id=1, source_target_pairs={{0,8},{4,12},{8,0},{12,4},{1,9},{5,13},{9,1},{13,5},{2,10},{6,14},... | collective-permute-start | bytes 4616 | tf_op jit(solution)/shard_map/ppermute | solution.py:46
  11.0 4.6 %collective-permute-start = (f32[24,16]{1,0:T(8,128)S(1)}, f32[24,16]{1,0:T(8,128)S(1)}, u32[]{:S(2)}, u32[]{:S(2)}) collective-permute-start(f32[24,16]{1,0:T(8,128)S(1)} %get-tuple-element.31.refs_0_), channel_id=1, source_target_pairs={{0,4},{4,0},{8,12},{12,8},{1,5},{5,1},{9,13},{13,9},{2,6},{6,2},{1... | collective-permute-start | bytes 4616 | tf_op jit(solution)/shard_map/ppermute | solution.py:46
  16.7 13.8 %collective-permute-start.6 = (f32[4,6,3,8,128]{4,3,2,1,0:T(8,128)S(1)}, f32[4,6,3,8,128]{4,3,2,1,0:T(8,128)S(1)}, u32[]{:S(2)}, u32[]{:S(2)}) collective-permute-start(f32[4,6,3,8,128]{4,3,2,1,0:T(8,128)S(1)} %get-tuple-element.37), channel_id=1, source_target_pairs={{0,12},{4,0},{8,4},{12,8},{1,13},{5,1},{9,5},{13,9},{2,14},{6,2},{... | collective-permute-start | bytes 884744 | tf_op jit(solution)/shard_map/ppermute | solution.py:52
  18.3 16.4 %collective-permute-start.5 = (f32[4,6,3,8,128]{4,3,2,1,0:T(8,128)S(1)}, f32[4,6,3,8,128]{4,3,2,1,0:T(8,128)S(1)}, u32[]{:S(2)}, u32[]{:S(2)}) collective-permute-start(f32[4,6,3,8,128]{4,3,2,1,0:T(8,128)S(1)} %get-tuple-element.37), channel_id=1, source_target_pairs={{0,4},{4,8},{8,12},{12,0},{1,5},{5,9},{9,13},{13,1},{2,6},{6,10},{... | collective-permute-start | bytes 884744 | tf_op jit(solution)/shard_map/ppermute | solution.py:52
  18.8 18.0 %collective-permute-start.4 = (f32[4,6,2,8,128]{4,3,2,1,0:T(8,128)S(1)}, f32[4,6,2,8,128]{4,3,2,1,0:T(8,128)S(1)}, u32[]{:S(2)}, u32[]{:S(2)}) collective-permute-start(f32[4,6,2,8,128]{4,3,2,1,0:T(8,128)S(1)} %get-tuple-element.36), channel_id=1, source_target_pairs={{0,12},{4,0},{8,4},{12,8},{1,13},{5,1},{9,5},{13,9},{2,14},{6,2},{... | collective-permute-start | bytes 589832 | tf_op jit(solution)/shard_map/ppermute | solution.py:52
  22.1 18.1 %collective-permute-start.3 = (f32[4,6,2,8,128]{4,3,2,1,0:T(8,128)S(1)}, f32[4,6,2,8,128]{4,3,2,1,0:T(8,128)S(1)}, u32[]{:S(2)}, u32[]{:S(2)}) collective-permute-start(f32[4,6,2,8,128]{4,3,2,1,0:T(8,128)S(1)} %get-tuple-element.36), channel_id=1, source_target_pairs={{0,4},{4,8},{8,12},{12,0},{1,5},{5,9},{9,13},{13,1},{2,6},{6,10},{... | collective-permute-start | bytes 589832 | tf_op jit(solution)/shard_map/ppermute | solution.py:52
  34.8 5.4 %collective-permute-start.7 = (f32[2,6,3,8,128]{4,3,2,1,0:T(8,128)S(1)}, f32[2,6,3,8,128]{4,3,2,1,0:T(8,128)S(1)}, u32[]{:S(2)}, u32[]{:S(2)}) collective-permute-start(f32[2,6,3,8,128]{4,3,2,1,0:T(8,128)S(1)} %get-tuple-element.38.refs_0_), channel_id=1, source_target_pairs={{0,16},{16,0},{1,17},{17,1},{2,18},{18,2},{3,19},{19,3},{4,20},{20... | collective-permute-start | bytes 442376 | tf_op jit(solution)/shard_map/ppermute | solution.py:583
  36.4 5.2 %collective-permute-start.8 = (f32[2,6,3,8,128]{4,3,2,1,0:T(8,128)S(1)}, f32[2,6,3,8,128]{4,3,2,1,0:T(8,128)S(1)}, u32[]{:S(2)}, u32[]{:S(2)}) collective-permute-start(f32[2,6,3,8,128]{4,3,2,1,0:T(8,128)S(1)} %get-tuple-element.39.refs_1_), channel_id=1, source_target_pairs={{0,16},{16,0},{1,17},{17,1},{2,18},{18,2},{3,19},{19,3},{4,20},{20... | collective-permute-start | bytes 442376 | tf_op jit(solution)/shard_map/ppermute | solution.py:583
  42.8 5.5 %collective-permute-start.11 = (f32[8,128]{1,0:T(8,128)S(1)}, f32[8,128]{1,0:T(8,128)S(1)}, u32[]{:S(2)}, u32[]{:S(2)}) collective-permute-start(f32[8,128]{1,0:T(8,128)S(1)} %get-tuple-element.43.refs_0_), channel_id=1, source_target_pairs={{0,12},{4,8},{8,4},{12,0},{1,13},{5,9},{9,5},{13,1},{2,14},{6,10},... | collective-permute-start | bytes 12296 | tf_op jit(solution)/shard_map/ppermute | solution.py:46
  44.8 4.5 %collective-permute-start.10 = (f32[8,128]{1,0:T(8,128)S(1)}, f32[8,128]{1,0:T(8,128)S(1)}, u32[]{:S(2)}, u32[]{:S(2)}) collective-permute-start(f32[8,128]{1,0:T(8,128)S(1)} %get-tuple-element.43.refs_0_), channel_id=1, source_target_pairs={{0,8},{4,12},{8,0},{12,4},{1,9},{5,13},{9,1},{13,5},{2,10},{6,14},... | collective-permute-start | bytes 12296 | tf_op jit(solution)/shard_map/ppermute | solution.py:46
  44.8 4.5 %collective-permute-start.9 = (f32[8,128]{1,0:T(8,128)S(1)}, f32[8,128]{1,0:T(8,128)S(1)}, u32[]{:S(2)}, u32[]{:S(2)}) collective-permute-start(f32[8,128]{1,0:T(8,128)S(1)} %get-tuple-element.43.refs_0_), channel_id=1, source_target_pairs={{0,4},{4,0},{8,12},{12,8},{1,5},{5,1},{9,13},{13,9},{2,6},{6,2},{1... | collective-permute-start | bytes 12296 | tf_op jit(solution)/shard_map/ppermute | solution.py:46
  50.5 15.7 %collective-permute-start.12 = (f32[4,6,8,8,128]{4,3,2,1,0:T(8,128)S(1)}, f32[4,6,8,8,128]{4,3,2,1,0:T(8,128)S(1)}, u32[]{:S(2)}, u32[]{:S(2)}) collective-permute-start(f32[4,6,8,8,128]{4,3,2,1,0:T(8,128)S(1)} %get-tuple-element.44.ahead_ref), channel_id=1, source_target_pairs={{0,12},{4,0},{8,4},{12,8},{1,13},{5,1},{9,5},{13,9},{2,14},{6,2},{... | collective-permute-start | bytes 2359304 | tf_op jit(solution)/shard_map/ppermute | solution.py:52
  66.5 5.4 %collective-permute-start.15 = (f32[8,128]{1,0:T(8,128)S(1)}, f32[8,128]{1,0:T(8,128)S(1)}, u32[]{:S(2)}, u32[]{:S(2)}) collective-permute-start(f32[8,128]{1,0:T(8,128)S(1)} %shard_map.76.refs_0_), channel_id=1, source_target_pairs={{0,12},{4,8},{8,4},{12,0},{1,13},{5,9},{9,5},{13,1},{2,14},{6,10},... | collective-permute-start | bytes 12296 | tf_op jit(solution)/shard_map/ppermute | solution.py:46
  70.0 4.5 %collective-permute-start.14 = (f32[8,128]{1,0:T(8,128)S(1)}, f32[8,128]{1,0:T(8,128)S(1)}, u32[]{:S(2)}, u32[]{:S(2)}) collective-permute-start(f32[8,128]{1,0:T(8,128)S(1)} %shard_map.76.refs_0_), channel_id=1, source_target_pairs={{0,8},{4,12},{8,0},{12,4},{1,9},{5,13},{9,1},{13,5},{2,10},{6,14},... | collective-permute-start | bytes 12296 | tf_op jit(solution)/shard_map/ppermute | solution.py:46
  70.0 4.5 %collective-permute-start.13 = (f32[8,128]{1,0:T(8,128)S(1)}, f32[8,128]{1,0:T(8,128)S(1)}, u32[]{:S(2)}, u32[]{:S(2)}) collective-permute-start(f32[8,128]{1,0:T(8,128)S(1)} %shard_map.76.refs_0_), channel_id=1, source_target_pairs={{0,4},{4,0},{8,12},{12,8},{1,5},{5,1},{9,13},{13,9},{2,6},{6,2},{1... | collective-permute-start | bytes 12296 | tf_op jit(solution)/shard_map/ppermute | solution.py:46
  74.9 2.0 %collective-permute-start.18 = (f32[144,128]{1,0:T(8,128)S(1)}, f32[144,128]{1,0:T(8,128)S(1)}, u32[]{:S(2)}, u32[]{:S(2)}) collective-permute-start(f32[144,128]{1,0:T(8,128)S(1)} %get-tuple-element.54), channel_id=1, source_target_pairs={{0,3},{1,0},{2,1},{3,2},{4,7},{5,4},{6,5},{7,6},{8,11},{9,8},{10,9... | collective-permute-start | bytes 221192 | tf_op jit(solution)/shard_map/ppermute | solution.py:52
  75.0 6.3 %collective-permute-start.17 = (f32[144,128]{1,0:T(8,128)S(1)}, f32[144,128]{1,0:T(8,128)S(1)}, u32[]{:S(2)}, u32[]{:S(2)}) collective-permute-start(f32[144,128]{1,0:T(8,128)S(1)} %get-tuple-element.55), channel_id=1, source_target_pairs={{0,2},{1,3},{2,0},{3,1},{4,6},{5,7},{6,4},{7,5},{8,10},{9,11},{10,... | collective-permute-start | bytes 221192 | tf_op jit(solution)/shard_map/ppermute | solution.py:52
  76.6 4.6 %collective-permute-start.16 = (f32[144,128]{1,0:T(8,128)S(1)}, f32[144,128]{1,0:T(8,128)S(1)}, u32[]{:S(2)}, u32[]{:S(2)}) collective-permute-start(f32[144,128]{1,0:T(8,128)S(1)} %get-tuple-element.56), channel_id=1, source_target_pairs={{0,1},{1,2},{2,3},{3,0},{4,5},{5,6},{6,7},{7,4},{8,9},{9,10},{10,1... | collective-permute-start | bytes 221192 | tf_op jit(solution)/shard_map/ppermute | solution.py:52
  81.2 5.7 %collective-permute-start.19 = (f32[48,128]{1,0:T(8,128)S(1)}, f32[48,128]{1,0:T(8,128)S(1)}, u32[]{:S(2)}, u32[]{:S(2)}) collective-permute-start(f32[48,128]{1,0:T(8,128)S(1)} %get-tuple-element.52), channel_id=1, source_target_pairs={{0,4},{4,8},{8,12},{12,0},{1,5},{5,9},{9,13},{13,1},{2,6},{6,10},{... | collective-permute-start | bytes 73736 | tf_op jit(solution)/shard_map/ppermute | solution.py:52
  81.3 5.6 %collective-permute-start.20 = (f32[48,128]{1,0:T(8,128)S(1)}, f32[48,128]{1,0:T(8,128)S(1)}, u32[]{:S(2)}, u32[]{:S(2)}) collective-permute-start(f32[48,128]{1,0:T(8,128)S(1)} %get-tuple-element.53), channel_id=1, source_target_pairs={{0,12},{4,0},{8,4},{12,8},{1,13},{5,1},{9,5},{13,9},{2,14},{6,2},{... | collective-permute-start | bytes 73736 | tf_op jit(solution)/shard_map/ppermute | solution.py:52

commit v3 on v2

--- a/solution.py
+++ b/solution.py
@@ -39,12 +39,28 @@
     )(*args)
 
 
-def parts_of(array, axis):
+def copies(axis, rows, columns):
     size = lax.axis_size(axis)
-    if size > 4 or size & (size - 1):
-        return [lax.psum(array, axis)]
-    others = [lax.ppermute(array, axis, [(i, i ^ k) for i in range(size)]) for k in range(1, size)]
-    return [array] + others
+    direct = size <= 4 and size & (size - 1) == 0
+    return [(rows + SUB * k, columns) for k in range(size - 1 if direct else 1)]
+
+
+def parts_of(arrays, axis):
+    size = lax.axis_size(axis)
+    if len(arrays) < size - 1:
+        return [lax.psum(arrays[0], axis)]
+    others = [
+        lax.ppermute(array, axis, [(i, i ^ (k + 1)) for i in range(size)]) for k, array in enumerate(arrays)
+    ]
+    return [arrays[0]] + others
+
+
+def put_copies(refs, value):
+    rows = value.shape[0]
+    for ref in refs:
+        ref[:rows, :] = value
+        if ref.shape[0] > rows:
+            ref[rows:, :] = jnp.zeros((ref.shape[0] - rows, ref.shape[1]), f32)
 
 
 def shifted(array, axis, step):
@@ -55,7 +71,7 @@
 def add_all(refs):
     total = refs[0][...]
     for ref in refs[1:]:
-        total = total + ref[...]
+        total = total + ref[: total.shape[0], :]
     return total
 
 
@@ -80,11 +96,13 @@
     return plane.reshape(-1, NY, LANES)
 
 
-def gram_kernel(shape, far_rows_ref, far_perturb_ref, planes_ref, gram_ref, rows_ref, perturb_ref, row_sems, perturb_sem):
+def gram_kernel(shape, far_rows_ref, far_perturb_ref, *refs):
+    gram_refs, (rows_ref, perturb_ref, row_sems, perturb_sem) = refs[:-4], refs[-4:]
     norb, layers, halves, group = shape
     groups = norb // SUB
     tiles = NY * halves
     step = 16
+    ahead = 3
     size = norb * tiles
     own = lax.axis_index("orb") * group // SUB
 
@@ -95,7 +113,7 @@
     weights = pltpu.make_async_copy(far_perturb_ref, perturb_ref, perturb_sem)
     fetch(0).start()
     weights.start()
-    for z in range(1, layers):
+    for z in range(1, min(ahead, layers)):
         fetch(z).start()
     weights.wait()
 
@@ -108,38 +126,46 @@
 
     def layer(z, total):
         fetch(z).wait()
+
+        @pl.when(z + ahead < layers)
+        def _():
+            fetch(z + ahead).start()
+
         for c0 in range(0, tiles, step):
             field = jnp.concatenate([tile_row(z, t, c0) for t in range(groups)], axis=0)
             weighted = perturb_ref[pl.ds(z, 1), c0 * LANES : (c0 + step) * LANES] * tile_row(z, own, c0)
             rest = (field - rounded(field)).astype(jnp.bfloat16)
             field = field.astype(jnp.bfloat16)
             pair = jnp.concatenate([weighted, weighted - rounded(weighted)], axis=0).astype(jnp.bfloat16)
-            left = jnp.concatenate([field, rest, pair], axis=0)
+            left = jnp.concatenate([field, pair], axis=0)
             right = jnp.concatenate([field, rest], axis=0)
             total = total + lax.dot_general(
                 left, right, (((1,), (1,)), ((), ())), preferred_element_type=f32
             )
-        for t in range(groups):
-            base = (z * groups + t) * tiles * SUB
-            for s in range(SUB):
-                for h in range(halves):
-                    for q in range(NY // SUB):
-                        start = base + (q * SUB * halves + h) * SUB + s
-                        planes_ref[t * SUB + s, z, h * (NY // SUB) + q] = rows_ref[
-                            pl.ds(start, SUB, stride=SUB * halves), :
-                        ]
         return total
 
-    total = lax.fori_loop(0, layers, layer, jnp.zeros((2 * norb + 2 * SUB, 2 * norb), f32))
-    total = total[:, :norb] + total[:, norb:]
-    gram_ref[:norb, :] = total[:norb] + total[norb : 2 * norb]
-    gram_ref[norb:, :] = total[2 * norb : 2 * norb + SUB] + total[2 * norb + SUB :]
-
-
-def tile_kernel(shape, *refs):
-    layers, halves = shape
-    count = len(refs) // 2
-    for array_ref, planes_ref in zip(refs[:count], refs[count:]):
+    total = lax.fori_loop(0, layers, layer, jnp.zeros((norb + 2 * SUB, 2 * norb), f32))
+    cross = total[:norb, norb:]
+    overlap = total[:norb, :norb] + cross + cross.T
+    total = total[norb:, :norb] + total[norb:, norb:]
+    put_copies(gram_refs, jnp.concatenate([overlap, total[:SUB] + total[SUB:]], axis=0))
+
+
+def tile_kernel(shape, rows_ref, perturb_ref, potential_ref, planes_ref, *refs):
+    norb, layers, halves = shape
+    tiles = NY * halves
+
+    def layer(z, carry):
+        for m in range(norb):
+            base = (z * (norb // SUB) + m // SUB) * tiles * SUB + m % SUB
+            for h in range(halves):
+                for q in range(NY // SUB):
+                    start = base + (q * SUB * halves + h) * SUB
+                    planes_ref[m, z, h * (NY // SUB) + q] = rows_ref[pl.ds(start, SUB, stride=SUB * halves), :]
+        return carry
+
+    lax.fori_loop(0, layers, layer, 0)
+    for array_ref, planes_ref in zip((perturb_ref, potential_ref), refs):
         for z in range(layers):
             for y in range(NY):
                 for h in range(halves):
@@ -163,11 +189,15 @@
     return overlap, rows
 
 
-def combine(layers, group, norb, planes_ref, coef_ref, start, finish):
+def whole(ref, n, z):
+    return ref[n, z]
+
+
+def combine(layers, group, norb, planes_ref, coef_ref, start, finish, pick=whole):
     def layer(z, carry):
         sums = [start(n, z) for n in range(group)]
         for m in range(norb):
-            field = planes_ref[m, z]
+            field = pick(planes_ref, m, z)
             for n in range(group):
                 sums[n] = sums[n] + field * coef_ref[pl.ds(n * norb + m, 1), :]
         for n in range(group):
@@ -180,25 +210,26 @@
 def inner_kernel(shape, ncell, planes_ref, perturb_ref, *refs):
     norb, layers, group, parts, share = shape
     gram_refs = refs[:parts]
-    inner_ref, rest_ref = refs[parts : parts + 2]
-    coef_ref, lines_ref = refs[-2:]
+    shared_ref, rest_ref, coef_ref, lines_ref = refs[parts:]
     first = lax.axis_index("orb") * group
     overlap, rows = small_matrices((norb, group), ncell, gram_refs, lines_ref)
     for n, (line, again) in enumerate(rows):
         coefs = (2.0 * line - again) * (1.0 / ncell)
         coef_ref[n * norb : (n + 1) * norb, :] = lanes_to_rows(coefs, norb)
-    place = lax.axis_index("freq") * share
+    mine = pl.ds(lax.axis_index("freq") * share, share)
+
+    def pick(ref, n, z):
+        return jnp.concatenate([ref[n, z, mine], ref[n, z, 2 * share :]], axis=0)
 
     def start(n, z):
-        return -(perturb_ref[z] * planes_ref[first + n, z])
+        weight = jnp.concatenate([perturb_ref[z, mine], perturb_ref[z, 2 * share :]], axis=0)
+        return -(weight * pick(planes_ref, first + n, z))
 
     def finish(n, z, value):
-        inner_ref[n, z] = value
-        rest_ref[n, z] = value[2 * share :]
-        if share:
-            refs[parts + 2][n, z] = inner_ref[n, z, pl.ds(place, share)]
-
-    combine(layers, group, norb, planes_ref, coef_ref, start, finish)
+        shared_ref[n, z] = value[:share]
+        rest_ref[n, z] = value[share:]
+
+    combine(layers, group, norb, planes_ref, coef_ref, start, finish, pick)
 
 
 def roll_x(halves_list, amount):
@@ -216,10 +247,10 @@
     return pltpu.roll(value, amount % NY, 0)
 
 
-def local_kernel(shape, ncell, omega_ref, energies_ref, planes_ref, perturb_ref, potential_ref, inner_ref, *refs):
-    norb, layers, group, parts, halves = shape
+def local_kernel(shape, ncell, omega_ref, energies_ref, planes_ref, perturb_ref, potential_ref, shared_ref, rest_ref, inner_coef_ref, *refs):
+    norb, layers, group, parts, halves, share = shape
     gram_refs = refs[:parts]
-    source_ref, partial_ref, overlap_ref, along_ref, square_ref, coef_ref, lines_ref = refs[parts:]
+    inner_ref, source_ref, partial_ref, overlap_ref, along_ref, square_ref, coef_ref, lines_ref = refs[parts:]
     first = lax.axis_index("orb") * group
     overlap, rows = small_matrices((norb, group), ncell, gram_refs, lines_ref)
     for m in range(norb):
@@ -238,6 +269,22 @@
         square_ref[n] += jnp.sum(value * value, axis=0)
 
     combine(layers, group, norb, planes_ref, coef_ref, start, finish)
+
+    place = lax.axis_index("freq") * share
+    mine, other = pl.ds(place, share), pl.ds(share - place, share)
+
+    def start_other(n, z):
+        return -(perturb_ref[z, other] * planes_ref[first + n, z, other])
+
+    def finish_other(n, z, value):
+        inner_ref[n, z, other] = value
+        inner_ref[n, z, mine] = shared_ref[n, z]
+        inner_ref[n, z, 2 * share :] = rest_ref[n, z]
+
+    def pick_other(ref, n, z):
+        return ref[n, z, other]
+
+    combine(layers, group, norb, planes_ref, inner_coef_ref, start_other, finish_other, pick_other)
 
     for n in range(group):
         def layer(z, carry):
@@ -277,7 +324,7 @@
     return total
 
 
-def halo_kernel(shape, before_ref, after_ref, square_ref, *halo_refs):
+def halo_kernel(shape, after_ref, before_ref, square_ref, *halo_refs):
     layers, group = shape
     each = group // len(halo_refs)
     for n in range(group):
@@ -285,88 +332,121 @@
             halo_refs[n // each][n % each, z] = halo_sum(layers, n, z, before_ref, after_ref)
 
 
-def image_kernel(shape, planes_ref, inner_ref, partial_ref, square_ref, before_ref, after_ref, *refs):
-    norb, layers, group, share = shape
-    applied_ref, sums_ref, acc_ref = refs[-3:]
-    pieces = (len(refs) - 3) // 2
-    place = lax.axis_index("freq") * share
+def multiply(shape, spots, planes_ref, inner_ref, field_ref, acc_ref):
+    norb, layers, group = shape
     acc_ref[...] = jnp.zeros_like(acc_ref)
-    for n in range(group):
-        for z in range(layers):
-            applied_ref[n, z, 2 * share :] = partial_ref[n, z, 2 * share :] + halo_sum(
-                layers, n, z, before_ref, after_ref
-            )
-            if share:
-                mine, other = pl.ds(place, share), pl.ds(share - place, share)
-                piece, i = divmod(n, group // pieces)
-                applied_ref[n, z, mine] = partial_ref[n, z, mine] + refs[piece][i, z]
-                applied_ref[n, z, other] = partial_ref[n, z, other] + refs[pieces + piece][i, z]
 
     def layer(z, carry):
-        fields = [applied_ref[n, z] for n in range(group)]
+        fields = [field_ref[n, z] for n in range(group)]
         for n in range(group):
-            acc_ref[group * norb + n] += jnp.sum(fields[n] * inner_ref[n, z], axis=0)
+            acc_ref[group * norb + n] += jnp.sum(fields[n] * inner_ref[n, z, spots], axis=0)
         for m in range(norb):
-            orbital = planes_ref[m, z]
+            orbital = planes_ref[m, z, spots]
             for n in range(group):
                 acc_ref[n * norb + m] += jnp.sum(orbital * fields[n], axis=0)
         return carry
 
     lax.fori_loop(0, layers, layer, 0)
-    totals = jnp.concatenate([jnp.sum(acc_ref[...], axis=1), jnp.sum(square_ref[...], axis=1)], axis=0)
-    sums_ref[...] = rows_to_lanes(totals)
+    return jnp.sum(acc_ref[...], axis=1)
+
+
+def mine_kernel(shape, share, planes_ref, inner_ref, partial_ref, *refs):
+    norb, layers, group = shape
+    field_ref, sums_ref, acc_ref = refs[-3:]
+    each = group // (len(refs) - 3)
+    spots = pl.ds(lax.axis_index("freq") * share, share)
+    for n in range(group):
+        for z in range(layers):
+            field_ref[n, z] = partial_ref[n, z, spots] + refs[n // each][n % each, z]
+    sums_ref[...] = multiply(shape, spots, planes_ref, inner_ref, field_ref, acc_ref)
+
+
+def rest_kernel(shape, share, planes_ref, inner_ref, partial_ref, after_ref, before_ref, field_ref, sums_ref, acc_ref):
+    norb, layers, group = shape
+    spots = pl.ds(2 * share, field_ref.shape[2])
+    for n in range(group):
+        for z in range(layers):
+            field_ref[n, z] = partial_ref[n, z, spots] + halo_sum(layers, n, z, before_ref, after_ref)
+    sums_ref[...] = multiply(shape, spots, planes_ref, inner_ref, field_ref, acc_ref)
+
+
+def other_kernel(shape, share, planes_ref, inner_ref, partial_ref, square_ref, mine_ref, mine_sums_ref, rest_ref, rest_sums_ref, *refs):
+    norb, layers, group, pieces = shape
+    halo_refs, applied_ref, sums_refs, (field_ref, acc_ref) = refs[:pieces], refs[pieces], refs[pieces + 1 : -2], refs[-2:]
+    each = group // pieces
+    place = lax.axis_index("freq") * share
+    mine, spots = pl.ds(place, share), pl.ds(share - place, share)
+    for n in range(group):
+        for z in range(layers):
+            field = partial_ref[n, z, spots] + halo_refs[n // each][n % each, z]
+            field_ref[n, z] = field
+            applied_ref[n, z, spots] = field
+            applied_ref[n, z, mine] = mine_ref[n, z]
+            applied_ref[n, z, 2 * share :] = rest_ref[n, z]
+    sums = multiply(shape[:3], spots, planes_ref, inner_ref, field_ref, acc_ref)
+    sums = sums + mine_sums_ref[...] + rest_sums_ref[...]
+    sums = rows_to_lanes(jnp.concatenate([sums, jnp.sum(square_ref[...], axis=1)], axis=0))
+    put_copies(sums_refs, sums)
 
 
 def residual_kernel(shape, ncell, planes_ref, source_ref, applied_ref, overlap_ref, along_ref, *refs):
-    norb, layers, group, parts = shape
+    norb, layers, group, parts, begin, count = shape
     sums_refs = refs[:parts]
-    ahead_ref, plain_ref, numbers_ref, coef_ref, step_ref = refs[parts:]
-    count = group * norb
-    total = lanes_to_rows(add_all(sums_refs)[:1], count + 2 * group)
-    curve = total[count : count + group]
-    norm = total[count + group : count + 2 * group]
+    ahead_ref, plain_ref, numbers_ref, coef_ref = refs[parts:]
+    size = group * norb
+    total = lanes_to_rows(add_all(sums_refs)[:1], size + 2 * group)
+    curve = total[size + begin : size + begin + count]
+    norm = total[size + group + begin : size + group + begin + count]
     step = norm / curve
-    numbers_ref[:group, :] = norm
-    numbers_ref[group : 2 * group, :] = curve
-    numbers_ref[2 * group : 3 * group, :] = step
-    step_ref[...] = step
-    for n in range(group):
-        rows = slice(n * norb, (n + 1) * norb)
-        product = total[rows]
-        alpha = step[n : n + 1]
+    numbers_ref[:count, :] = norm
+    numbers_ref[count : 2 * count, :] = curve
+    numbers_ref[2 * count : 3 * count, :] = step
+    for i in range(count):
+        n = begin + i
+        rows = slice(i * norb, (i + 1) * norb)
+        product = total[n * norb : (n + 1) * norb]
+        alpha = step[i : i + 1]
         again = jnp.zeros((norb, LANES), f32)
         for m in range(norb):
             again = again + overlap_ref[m] * product[m : m + 1]
-        left = along_ref[rows, :] - alpha * (product - again * (1.0 / ncell))
+        left = along_ref[n * norb : (n + 1) * norb, :] - alpha * (product - again * (1.0 / ncell))
         plain_ref[rows, :] = alpha * product * (1.0 / ncell)
         coef_ref[rows, :] = (alpha * product - left) * (1.0 / ncell)
 
-    def start(n, z):
-        return source_ref[n, z] - step_ref[n : n + 1, :] * applied_ref[n, z]
-
-    def finish(n, z, value):
-        ahead_ref[n, z] = value
-
-    combine(layers, group, norb, planes_ref, coef_ref, start, finish)
-
-
-def second_kernel(shape, omega_ref, energies_ref, planes_ref, potential_ref, source_ref, applied_ref, ahead_ref, plain_ref, numbers_ref, residual_ref, acc_ref):
-    norb, layers, group, halves = shape
+    def start(i, z):
+        return source_ref[begin + i, z] - numbers_ref[2 * count + i : 2 * count + i + 1, :] * applied_ref[begin + i, z]
+
+    def finish(i, z, value):
+        ahead_ref[i, z] = value
+
+    combine(layers, count, norb, planes_ref, coef_ref, start, finish)
+
+
+def second_kernel(shape, omega_ref, energies_ref, planes_ref, potential_ref, source_ref, applied_ref, *refs):
+    norb, layers, group, halves, parts = shape
+    ahead_refs, plain_refs, numbers_refs = refs[:parts], refs[parts : 2 * parts], refs[2 * parts : 3 * parts]
+    residual_ref, acc_ref = refs[3 * parts :]
+    each = group // parts
     acc_ref[...] = jnp.zeros_like(acc_ref)
 
-    def start(n, z):
-        alpha = numbers_ref[2 * group + n : 2 * group + n + 1, :]
-        return source_ref[n, z] - alpha * applied_ref[n, z]
-
-    def finish(n, z, value):
-        residual_ref[n, z] = value
-        acc_ref[2 * group + n] += jnp.sum(value * value, axis=0)
-
-    combine(layers, group, norb, planes_ref, plain_ref, start, finish)
+    for part in range(parts):
+        first = part * each
+
+        def start(i, z):
+            alpha = numbers_refs[part][2 * each + i : 2 * each + i + 1, :]
+            return source_ref[first + i, z] - alpha * applied_ref[first + i, z]
+
+        def finish(i, z, value):
+            residual_ref[first + i, z] = value
+            acc_ref[2 * group + first + i] += jnp.sum(value * value, axis=0)
+
+        combine(layers, each, norb, planes_ref, plain_refs[part], start, finish)
 
     for n in range(group):
+        ahead_ref, i = ahead_refs[n // each], n % each
+
         def layer(z, carry):
-            whole = ahead_ref[n, z]
+            whole = ahead_ref[i, z]
             plane = blocks(whole)
             sheets = [plane[h] for h in range(halves)]
             sums = [(-1.5 * COEFFS[0]) * v for v in sheets]
@@ -384,38 +464,45 @@
         for z in range(layers - 1):
             total = None
             for other in range(z + 1, min(layers, z + 7)):
-                term = -COEFFS[other - z] * ahead_ref[n, other]
+                term = -COEFFS[other - z] * ahead_ref[i, other]
                 total = term if total is None else total + term
-            acc_ref[n] += jnp.sum(ahead_ref[n, z] * total, axis=0)
-
-
-def pairs_kernel(shape, ahead_ref, after_ref, acc_ref, sums_ref):
-    layers, group = shape
+            acc_ref[n] += jnp.sum(ahead_ref[i, z] * total, axis=0)
+
+
+def pairs_kernel(shape, acc_ref, *refs):
+    layers, group, parts = shape
+    ahead_refs, after_refs, sums_refs = refs[:parts], refs[parts : 2 * parts], refs[2 * parts :]
+    each = group // parts
     sums = jnp.sum(acc_ref[...], axis=1)
     lines = []
     for n in range(group):
+        ahead_ref, after_ref, i = ahead_refs[n // each], after_refs[n // each], n % each
         total = None
         for z in range(layers):
             line = None
             for j in range(layers):
                 k = j + layers - z
                 if k <= 6:
-                    term = -COEFFS[k] * after_ref[n, j]
+                    term = -COEFFS[k] * after_ref[i, j]
                     line = term if line is None else line + term
             if line is not None:
-                line = line * ahead_ref[n, z]
+                line = line * ahead_ref[i, z]
                 total = line if total is None else total + line
         lines.append(jnp.sum(jnp.sum(total, axis=0), axis=0, keepdims=True))
-    sums_ref[...] = rows_to_lanes(jnp.concatenate([sums[:group] + jnp.concatenate(lines, axis=0), sums[group:]], axis=0))
-
-
-def density_kernel(shape, planes_ref, source_ref, residual_ref, numbers_ref, *refs):
-    layers, group, parts, halves, members, width, margin = shape
-    sums_refs = refs[:parts]
-    cuts_ref, scales_ref, ring_ref = refs[parts:]
+    sums = jnp.concatenate([sums[:group] + jnp.concatenate(lines, axis=0), sums[group:]], axis=0)
+    put_copies(sums_refs, rows_to_lanes(sums))
+
+
+def density_kernel(shape, planes_ref, source_ref, residual_ref, *refs):
+    layers, group, parts, halves, members, width, margin, cut = shape
+    sums_refs, numbers_refs, refs = refs[:parts], refs[parts : parts + cut], refs[parts + cut :]
+    cuts_ref, scales_ref, ring_ref = refs
+    each = group // cut
     first = lax.axis_index("orb")
     total = lanes_to_rows(add_all(sums_refs)[:1], 3 * group)
-    norm, curve, alpha = (numbers_ref[i * group : (i + 1) * group, :] for i in range(3))
+    norm, curve, alpha = (
+        jnp.concatenate([ref[i * each : (i + 1) * each, :] for ref in numbers_refs], axis=0) for i in range(3)
+    )
     squares, cross, bend = total[2 * group : 3 * group], total[group : 2 * group], total[:group]
     beta = squares / norm
     bend = bend + 2.0 * beta * cross + beta * beta * curve
@@ -474,22 +561,28 @@
     bottom_ref[...] = total[:edge]
 
 
-def jacobi_kernel(shape, dense_ref, before_ref, after_ref, induced_ref):
+def jacobi_kernel(shape, dense_ref, before_ref, after_ref, induced_ref, slab_ref, out_ref):
     layers, halves, width, margin = shape
     rows = width + 2 * margin
+    full = -(-rows // SUB) * SUB
     scale = 1.0 / (6.0 + SCREEN)
-
-    def sheets(ref, count):
-        return [[ref[pl.ds((z * halves + h) * rows, rows), :] for h in range(halves)] for z in range(count)]
-
-    dense = sheets(before_ref, 2) + sheets(dense_ref, layers) + sheets(after_ref, 2)
+    edge = 2 * halves * rows
+    middle = layers * halves * rows
+    slab_ref[:edge, :] = before_ref[...]
+    slab_ref[edge : edge + middle, :] = dense_ref[...]
+    slab_ref[edge + middle : 2 * edge + middle, :] = after_ref[...]
+    slab_ref[2 * edge + middle :, :] = jnp.zeros((slab_ref.shape[0] - 2 * edge - middle, LANES), f32)
+    dense = [
+        [slab_ref[(z * halves + h) * rows : (z * halves + h) * rows + full, :] for h in range(halves)]
+        for z in range(layers + 4)
+    ]
     field = [[scale * v for v in sheet] for sheet in dense]
 
     def up(value):
         return pltpu.roll(value, 1, 0)
 
     def down(value):
-        return pltpu.roll(value, rows - 1, 0)
+        return pltpu.roll(value, full - 1, 0)
 
     for sweep in range(2):
         fresh = []
@@ -504,9 +597,13 @@
         field, dense = fresh, dense[1:-1]
     for z in range(layers):
         for h in range(halves):
-            for y in range(width):
-                c = y * halves + h
-                induced_ref[z : z + 1, c * LANES : (c + 1) * LANES] = field[z][h][margin + y : margin + y + 1]
+            out_ref[pl.ds((z * halves + h) * full, full), :] = field[z][h]
+    for h in range(halves):
+        for y in range(width):
+            c = y * halves + h
+            induced_ref[:, c * LANES : (c + 1) * LANES] = out_ref[
+                pl.ds(h * full + margin + y, layers, stride=halves * full), :
+            ]
 
 
 def per_device(orbitals, potential, perturb, energies, omega):
@@ -523,9 +620,9 @@
     flat = (group * norb, LANES)
 
     size = norb * tiles
-    planes, gram = call(
+    gram = call(
         functools.partial(gram_kernel, (norb, layers, halves, group)),
-        [(norb, layers, spots, SUB, LANES), (norb + SUB, norb)],
+        copies("brick", norb + SUB, norb),
         [
             (layers * size, LANES),
             (layers, columns),
@@ -536,27 +633,33 @@
         rows,
         perturb,
         far=2,
-        limit=48 * 1024 * 1024,
+        limit=60 * 1024 * 1024,
     )
     grams = parts_of(gram, "brick")
     plane = (layers, spots, SUB, LANES)
-    perturb_planes, potential_planes = call(
-        functools.partial(tile_kernel, (layers, halves)), [plane, plane], [], 0, perturb, potential
-    )
-    share = 3 * spots // 8 if lax.axis_size("freq") == 2 else 0
+    planes, perturb_planes, potential_planes = call(
+        functools.partial(tile_kernel, (norb, layers, halves)),
+        [(norb,) + plane, plane, plane],
+        [],
+        0,
+        rows,
+        perturb,
+        potential,
+    )
+    share = 3 * spots // 8
     cells = (SUB, LANES)
-    inner, rest, *shared = call(
+    shared, rest, coefs = call(
         functools.partial(inner_kernel, (norb, layers, group, len(grams), share), ncell),
-        [own, (group, layers, spots - 2 * share) + cells] + [(group, layers, share) + cells] * (share > 0),
-        [flat, (SUB, norb)],
+        [(group, layers, share) + cells, (group, layers, spots - 2 * share) + cells, flat],
+        [(SUB, norb)],
         0,
         planes,
         perturb_planes,
         *grams,
     )
-    source, partial, overlap, along, square = call(
-        functools.partial(local_kernel, (norb, layers, group, len(grams), halves), ncell),
-        [own, own, (norb, norb, LANES), flat, (group, SUB, LANES)],
+    inner, source, partial, overlap, along, square = call(
+        functools.partial(local_kernel, (norb, layers, group, len(grams), halves, share), ncell),
+        [own, own, own, (norb, norb, LANES), flat, (group,) + cells],
         [flat, (SUB, norb)],
         2,
         omega,
@@ -564,54 +667,85 @@
         planes,
         perturb_planes,
         potential_planes,
+        shared,
+        rest,
+        coefs,
+        *grams,
+    )
+    before, after = shifted(shared, "brick", 1), shifted(shared, "brick", -1)
+    pieces = 1 if group % 2 else 2
+    each = group // pieces
+    halos = call(
+        functools.partial(halo_kernel, (layers, group)),
+        [(each, layers, share) + cells] * pieces,
+        [],
+        0,
+        after,
+        before,
+        square,
+    )
+    partner = [lax.ppermute(halo, "freq", [(0, 1), (1, 0)]) for halo in halos]
+    count = group * norb + group
+    before_rest, after_rest = shifted(rest, "brick", 1), shifted(rest, "brick", -1)
+    mine, mine_sums = call(
+        functools.partial(mine_kernel, (norb, layers, group), share),
+        [shared.shape, (count, LANES)],
+        [(count,) + cells],
+        0,
+        planes,
         inner,
-        *grams,
-    )
-    halos = []
-    pieces = 1 if group % 2 else 2
-    if share:
-        before, after = shifted(shared[0], "brick", 1), shifted(shared[0], "brick", -1)
-        halos = call(
-            functools.partial(halo_kernel, (layers, group)),
-            [(group // pieces, layers, share) + cells] * pieces,
-            [],
-            0,
-            before,
-            after,
-            square,
-        )
-        halos = [*halos] + [lax.ppermute(halo, "freq", [(0, 1), (1, 0)]) for halo in halos]
-    before, after = shifted(rest, "brick", 1), shifted(rest, "brick", -1)
-    applied, sums = call(
-        functools.partial(image_kernel, (norb, layers, group, share)),
-        [own, cells],
-        [(group * norb + group,) + cells],
+        partial,
+        *halos,
+    )
+    rest, rest_sums = call(
+        functools.partial(rest_kernel, (norb, layers, group), share),
+        [rest.shape, (count, LANES)],
+        [(count,) + cells],
+        0,
+        planes,
+        inner,
+        partial,
+        after_rest,
+        before_rest,
+    )
+    applied, *sums = call(
+        functools.partial(other_kernel, (norb, layers, group, pieces), share),
+        [own] + copies("brick", SUB, LANES),
+        [shared.shape, (count,) + cells],
         0,
         planes,
         inner,
         partial,
         square,
-        before,
-        after,
-        *halos,
+        mine,
+        mine_sums,
+        rest,
+        rest_sums,
+        *partner,
     )
     sums = parts_of(sums, "brick")
-    ahead, plain, numbers = call(
-        functools.partial(residual_kernel, (norb, layers, group, len(sums)), ncell),
-        [own, flat, (3 * group, LANES)],
-        [flat, (group, LANES)],
-        0,
-        planes,
-        source,
-        applied,
-        overlap,
-        along,
-        *sums,
-    )
-    after = shifted(ahead, "brick", -1)
+    runs = 1
+    part = group // runs
+    steps = [
+        call(
+            functools.partial(residual_kernel, (norb, layers, group, len(sums), i * part, part), ncell),
+            [(part,) + own[1:], (part * norb, LANES), (3 * part, LANES)],
+            [(part * norb, LANES)],
+            0,
+            planes,
+            source,
+            applied,
+            overlap,
+            along,
+            *sums,
+        )
+        for i in range(runs)
+    ]
+    aheads, plains, numbers = zip(*steps)
+    afters = [shifted(ahead, "brick", -1) for ahead in aheads]
     residual, acc = call(
-        functools.partial(second_kernel, (norb, layers, group, halves)),
-        [own, (3 * group, SUB, LANES)],
+        functools.partial(second_kernel, (norb, layers, group, halves, runs)),
+        [own, (3 * group,) + cells],
         [],
         2,
         omega,
@@ -620,34 +754,35 @@
         potential_planes,
         source,
         applied,
-        ahead,
-        plain,
-        numbers,
-    )
-    (sums,) = call(
-        functools.partial(pairs_kernel, (layers, group)),
-        [cells],
+        *aheads,
+        *plains,
+        *numbers,
+    )
+    sums = call(
+        functools.partial(pairs_kernel, (layers, group, runs)),
+        copies("brick", SUB, LANES),
         [],
         0,
-        ahead,
-        after,
         acc,
+        *aheads,
+        *afters,
     )
     sums = parts_of(sums, "brick")
     width = NY // members
     margin = 2
-    edge = 2 * halves * (width + 2 * margin)
-    cut = (layers * halves * (width + 2 * margin), LANES)
+    span = width + 2 * margin
+    edge = 2 * halves * span
+    cut = (layers * halves * span, LANES)
     cuts, scales = call(
-        functools.partial(density_kernel, (layers, group, len(sums), halves, members, width, margin)),
+        functools.partial(density_kernel, (layers, group, len(sums), halves, members, width, margin, runs)),
         [(members,) + cut, (2 * group, LANES)],
         [(layers, halves, NY + 2 * SUB, LANES)],
         0,
         planes,
         source,
         residual,
-        numbers,
         *sums,
+        *numbers,
     )
     others = [shifted(cuts[k], "orb", k) for k in range(1, members)]
     (response,) = call(
@@ -666,7 +801,7 @@
     (induced,) = call(
         functools.partial(jacobi_kernel, (layers, halves, width, margin)),
         [(layers, width * halves * LANES)],
-        [],
+        [((layers + 4) * halves * span + SUB, LANES), (layers * halves * (-(-span // SUB) * SUB), LANES)],
         0,
         dense,
         before,

time: 88 us -> 86.1 us (0.978)
  waiting for transfers between devices: 33.4 us -> 29.2 us
  Pallas kernels: 22.3 us -> 23.7 us
  starting transfers between devices: 29.7 us -> 30.6 us
    ppermute x11, waiting for transfers between devices: 10.8 us -> 8.63 us  [the longest x9 8.27 us: parts_of(): lax.ppermute(array, axis, [(i, i ^ k + 1) for i in range(size)])]
    ppermute x10, waiting for transfers between devices: 22.7 us -> 20.5 us  [shifted(): lax.ppermute(array, axis, [(i, (i + step) % size) for i in range(size)])]
    pallas_call x13 -> x15, Pallas kernels: 22.3 us -> 23.7 us  [call(): pl.pallas_call(kernel, out_shape=[jax.ShapeDtypeStruct(s, f32) for s in o...]
    ppermute x10, starting transfers between devices: 13 us -> 13.9 us  [shifted(): lax.ppermute(array, axis, [(i, (i + step) % size) for i in range(size)])]
  transfers between devices with their start and end apart: 21 -> 21, of which waited for: 14 -> 15; matrix products, arithmetic and copies ran while one was open for 0% -> 0% of each run, Pallas kernels for 15% -> 18%
where the time goes in v3:
time: 86.1 us; the launch traced here: 85.9 us
  starting transfers between devices  30.6 us (36%)
  waiting for transfers between devices  29.2 us (34%)
  Pallas kernels  23.7 us (28%)
  between operations  1.42 us (2%)
  local copies, waits for them, and re-layouts  0.98 us (1%)
    pallas_call x15, Pallas kernels, call(): pl.pallas_call(kernel, out_shape=[jax.ShapeDtypeStruct(s, f32) for s in o...  23.7 us
    ppermute x10, waiting for transfers between devices, shifted(): lax.ppermute(array, axis, [(i, (i + step) % size) for i in range(size)])  20.5 us
    ppermute x9, starting transfers between devices, parts_of(): lax.ppermute(array, axis, [(i, i ^ k + 1) for i in range(size)])  14.6 us
    ppermute x10, starting transfers between devices, shifted(): lax.ppermute(array, axis, [(i, (i + step) % size) for i in range(size)])  13.9 us
    ppermute x9, waiting for transfers between devices, parts_of(): lax.ppermute(array, axis, [(i, i ^ k + 1) for i in range(size)])  8.27 us
    ppermute x2, starting transfers between devices, per_device(): partner = [lax.ppermute(halo, 'freq', [(0, 1), (1, 0)]) for halo in halos]  2.09 us
  transfers between devices with their start and end apart: 21, of which 15 were waited for; matrix products, arithmetic and copies ran while one was open for 0% of the time, Pallas kernels for 18%

profile of v3, /device:TPU:0, one launch (start us, length us, event | category | flops | bytes accessed | tf_op | source)
XLA Modules:
  0.0 85.9 jit_solution(1965226322868297231)
XLA Ops:
  0.6 0.0 copy-start
  0.6 0.0 copy-start.1
  0.6 4.3 %shard_map.69 = (f32[24,16]{1,0:T(8,128)}, f32[32,16]{1,0:T(8,128)}, f32[40,16]{1,0:T(8,128)}) custom-call(f32[6144,128]{1,0:T(8,128)} %bitcast.18, f32[6,8192]{1,0:T(8,128)} %far_perturb_ref.1), custom_call_target="tpu_custom_call" | custom-call | tf_op jit(solution)/shard_map/pallas_call | solution.py:32
  5.0 5.1 %collective-permute-start.2 = (f32[40,16]{1,0:T(8,128)}, f32[40,16]{1,0:T(8,128)S(1)}, u32[]{:S(2)}, u32[]{:S(2)}) collective-permute-start(f32[40,16]{1,0:T(8,128)} %get-tuple-element.45), channel_id=1, source_target_pairs={{0,12},{4,8},{8,4},{12,0},{1,13},{5,9},{9,5},{13,1},{2,14},{6,10},... | collective-permute-start | bytes 7688 | tf_op jit(solution)/shard_map/ppermute | solution.py:53
  10.1 0.0 collective-permute-start.1
  10.1 0.6 collective-permute-start
  10.7 0.0 copy-done
  10.7 0.0 copy-done.1
  10.7 0.0 copy-start.2
  10.7 0.9 %copy-done.2 = f32[6,8192]{1,0:T(8,128)S(1)} copy-done((f32[6,8192]{1,0:T(8,128)S(1)}, f32[6,8192]{1,0:T(8,128)}, u32[]{:S(2)}) %copy-start.2) | copy-done | bytes 196632
  11.7 1.2 %shard_map.68 = (f32[16,6,8,8,128]{4,3,2,1,0:T(8,128)S(1)}, f32[6,8,8,128]{3,2,1,0:T(8,128)S(1)}, f32[6,8,8,128]{3,2,1,0:T(8,128)S(1)}) custom-call(f32[6144,128]{1,0:T(8,128)S(1)} %bitcast.19, f32[6,8192]{1,0:T(8,128)S(1)} %copy-done.1, f32[6,8192]{1,0:T(8,128)S(1)} %copy-done.2), custom_call_target="tpu_custom_call" | custom-call | tf_op jit(solution)/shard_map/pallas_call | solution.py:32
  12.9 1.1 %collective-permute-done.refs_1_ = f32[24,16]{1,0:T(8,128)S(1)} collective-permute-done((f32[24,16]{1,0:T(8,128)}, f32[24,16]{1,0:T(8,128)S(1)}, u32[]{:S(2)}, u32[]{:S(2)}) %collective-permute-start) | collective-permute-done | bytes 1568 | tf_op jit(solution)/shard_map/ppermute | solution.py:53
  14.0 0.9 %collective-permute-done.1.refs_2_ = f32[32,16]{1,0:T(8,128)S(1)} collective-permute-done((f32[32,16]{1,0:T(8,128)}, f32[32,16]{1,0:T(8,128)S(1)}, u32[]{:S(2)}, u32[]{:S(2)}) %collective-permute-start.1) | collective-permute-done | bytes 2080 | tf_op jit(solution)/shard_map/ppermute | solution.py:53
  14.9 0.0 collective-permute-done.2.refs_3_
  14.9 0.0 copy-done.3
  14.9 0.8 shard_map.70
  15.8 1.8 %collective-permute-start.3 = (f32[4,6,3,8,128]{4,3,2,1,0:T(8,128)S(1)}, f32[4,6,3,8,128]{4,3,2,1,0:T(8,128)S(1)}, u32[]{:S(2)}, u32[]{:S(2)}) collective-permute-start(f32[4,6,3,8,128]{4,3,2,1,0:T(8,128)S(1)} %get-tuple-element.46.shared_ref), channel_id=1, source_target_pairs={{0,12},{4,0},{8,4},{12,8},{1,13},{5,1},{9,5},{13,9},{2,14},{6,2},{... | collective-permute-start | bytes 884744 | tf_op jit(solution)/shard_map/ppermute | solution.py:68
  17.6 0.2 collective-permute-start.4
  17.9 3.6 %collective-permute-start.5 = (f32[4,6,2,8,128]{4,3,2,1,0:T(8,128)S(1)}, f32[4,6,2,8,128]{4,3,2,1,0:T(8,128)S(1)}, u32[]{:S(2)}, u32[]{:S(2)}) collective-permute-start(f32[4,6,2,8,128]{4,3,2,1,0:T(8,128)S(1)} %get-tuple-element.47.rest_ref), channel_id=1, source_target_pairs={{0,12},{4,0},{8,4},{12,8},{1,13},{5,1},{9,5},{13,9},{2,14},{6,2},{... | collective-permute-start | bytes 589832 | tf_op jit(solution)/shard_map/ppermute | solution.py:68
  21.4 0.0 collective-permute-start.6
  22.1 0.0 copy-done.4
  22.1 6.9 %shard_map.71 = (f32[4,6,8,8,128]{4,3,2,1,0:T(8,128)S(1)}, f32[4,6,8,8,128]{4,3,2,1,0:T(8,128)S(1)}, f32[4,6,8,8,128]{4,3,2,1,0:T(8,128)S(1)}, f32[16,16,128]{2,...) custom-call(f32[1]{0:T(128)S(6)} %copy.8.omega_ref, f32[4]{0:T(128)S(1)} %copy-done.4, ...), custom_call_target="tpu_custom_call" | custom-call | tf_op jit(solution)/shard_map/pallas_call | solution.py:32
  29.0 0.6 collective-permute-done.3.after_ref
  29.6 4.1 %collective-permute-done.4.before_ref = f32[4,6,3,8,128]{4,3,2,1,0:T(8,128)S(1)} collective-permute-done((f32[4,6,3,8,128]{4,3,2,1,0:T(8,128)S(1)}, f32[4,6,3,8,128]{4,3,2,1,0:T(8,128)S(1)}, u32[]{:S(2)}, u32[]{:S(2)}) %collective-permute-start.4) | collective-permute-done | bytes 294944 | tf_op jit(solution)/shard_map/ppermute | solution.py:68
  33.7 0.1 shard_map.72
  33.8 1.6 %collective-permute-start.7 = (f32[2,6,3,8,128]{4,3,2,1,0:T(8,128)S(1)}, f32[2,6,3,8,128]{4,3,2,1,0:T(8,128)S(1)}, u32[]{:S(2)}, u32[]{:S(2)}) collective-permute-start(f32[2,6,3,8,128]{4,3,2,1,0:T(8,128)S(1)} %get-tuple-element.53.refs_0_), channel_id=1, source_target_pairs={{0,16},{16,0},{1,17},{17,1},{2,18},{18,2},{3,19},{19,3},{4,20},{20... | collective-permute-start | bytes 442376 | tf_op jit(solution)/shard_map/ppermute | solution.py:687
  35.4 0.5 collective-permute-start.8
  35.9 0.0 collective-permute-done.5.after_ref
  35.9 3.4 %collective-permute-done.6.before_ref = f32[4,6,2,8,128]{4,3,2,1,0:T(8,128)S(1)} collective-permute-done((f32[4,6,2,8,128]{4,3,2,1,0:T(8,128)S(1)}, f32[4,6,2,8,128]{4,3,2,1,0:T(8,128)S(1)}, u32[]{:S(2)}, u32[]{:S(2)}) %collective-permute-start.6) | collective-permute-done | bytes 196640 | tf_op jit(solution)/shard_map/ppermute | solution.py:68
  39.3 0.4 shard_map.74
  39.7 0.5 shard_map.73
  40.2 0.0 collective-permute-done.7.refs_0_
  40.2 0.4 collective-permute-done.8.refs_1_
  40.6 0.6 shard_map.75
  41.2 2.6 %collective-permute-start.11 = (f32[24,128]{1,0:T(8,128)S(1)}, f32[24,128]{1,0:T(8,128)S(1)}, u32[]{:S(2)}, u32[]{:S(2)}) collective-permute-start(f32[24,128]{1,0:T(8,128)S(1)} %get-tuple-element.64), channel_id=1, source_target_pairs={{0,12},{4,8},{8,4},{12,0},{1,13},{5,9},{9,5},{13,1},{2,14},{6,10},... | collective-permute-start | bytes 36872 | tf_op jit(solution)/shard_map/ppermute | solution.py:53
  43.8 0.0 collective-permute-start.10
  43.8 1.8 %collective-permute-start.9 = (f32[8,128]{1,0:T(8,128)S(1)}, f32[8,128]{1,0:T(8,128)S(1)}, u32[]{:S(2)}, u32[]{:S(2)}) collective-permute-start(f32[8,128]{1,0:T(8,128)S(1)} %get-tuple-element.62.refs_0_), channel_id=1, source_target_pairs={{0,4},{4,0},{8,12},{12,8},{1,5},{5,1},{9,13},{13,9},{2,6},{6,2},{1... | collective-permute-start | bytes 12296 | tf_op jit(solution)/shard_map/ppermute | solution.py:53
  45.7 1.8 %collective-permute-done.9.refs_1_ = f32[8,128]{1,0:T(8,128)S(1)} collective-permute-done((f32[8,128]{1,0:T(8,128)S(1)}, f32[8,128]{1,0:T(8,128)S(1)}, u32[]{:S(2)}, u32[]{:S(2)}) %collective-permute-start.9) | collective-permute-done | bytes 4128 | tf_op jit(solution)/shard_map/ppermute | solution.py:53
  47.5 1.0 %collective-permute-done.10.refs_2_ = f32[16,128]{1,0:T(8,128)S(1)} collective-permute-done((f32[16,128]{1,0:T(8,128)S(1)}, f32[16,128]{1,0:T(8,128)S(1)}, u32[]{:S(2)}, u32[]{:S(2)}) %collective-permute-start.10) | collective-permute-done | bytes 8224 | tf_op jit(solution)/shard_map/ppermute | solution.py:53
  48.5 0.0 collective-permute-done.11.refs_3_
  48.5 1.2 %shard_map.76 = (f32[4,6,8,8,128]{4,3,2,1,0:T(8,128)S(1)}, f32[64,128]{1,0:T(8,128)S(1)}, f32[12,128]{1,0:T(8,128)S(1)}) custom-call(f32[16,6,8,8,128]{4,3,2,1,0:T(8,128)S(1)} %get-tuple-element.40.planes_ref, f32[4,6,8,8,128]{4,3,2,1,0:T(8,128)S(1)} %get-tuple-element.49.source_ref, f32[4,6,8,8,128]{4,3,2,1,0:T(8,128)S(1)} %get-tuple-element.59.applied_ref, ...), custom_call_target="tpu_custom_call" | custom-call | tf_op jit(solution)/shard_map/pallas_call | solution.py:32
  49.7 1.4 %collective-permute-start.12 = (f32[4,6,8,8,128]{4,3,2,1,0:T(8,128)S(1)}, f32[4,6,8,8,128]{4,3,2,1,0:T(8,128)S(1)}, u32[]{:S(2)}, u32[]{:S(2)}) collective-permute-start(f32[4,6,8,8,128]{4,3,2,1,0:T(8,128)S(1)} %get-tuple-element.65.refs_0_), channel_id=1, source_target_pairs={{0,12},{4,0},{8,4},{12,8},{1,13},{5,1},{9,5},{13,9},{2,14},{6,2},{... | collective-permute-start | bytes 2359304 | tf_op jit(solution)/shard_map/ppermute | solution.py:68
  51.1 5.0 %shard_map.77 = (f32[4,6,8,8,128]{4,3,2,1,0:T(8,128)S(1)}, f32[12,8,128]{2,1,0:T(8,128)S(1)}) custom-call(f32[1]{0:T(128)S(6)} %copy.8.omega_ref, f32[4]{0:T(128)S(1)} %copy-done.4, f32[16,6,8,8,128]{4,3,2,1,0:T(8,128)S(1)} %get-tuple-element.40.planes_ref, f32[6,8,8,128]{3,2,1,0:T(8,128)S(1)} %get-tuple-element.42.potential_ref, ...), custom_call_target="tpu_custom_call" | custom-call | tf_op jit(solution)/shard_map/pallas_call | solution.py:32
  56.1 9.2 %collective-permute-done.12.refs_1_ = f32[4,6,8,8,128]{4,3,2,1,0:T(8,128)S(1)} collective-permute-done((f32[4,6,8,8,128]{4,3,2,1,0:T(8,128)S(1)}, f32[4,6,8,8,128]{4,3,2,1,0:T(8,128)S(1)}, u32[]{:S(2)}, u32[]{:S(2)}) %collective-permute-start.12) | collective-permute-done | bytes 786464 | tf_op jit(solution)/shard_map/ppermute | solution.py:68
  65.3 0.3 shard_map.78
  65.6 3.3 %collective-permute-start.15 = (f32[24,128]{1,0:T(8,128)S(1)}, f32[24,128]{1,0:T(8,128)S(1)}, u32[]{:S(2)}, u32[]{:S(2)}) collective-permute-start(f32[24,128]{1,0:T(8,128)S(1)} %get-tuple-element.72), channel_id=1, source_target_pairs={{0,12},{4,8},{8,4},{12,0},{1,13},{5,9},{9,5},{13,1},{2,14},{6,10},... | collective-permute-start | bytes 36872 | tf_op jit(solution)/shard_map/ppermute | solution.py:53
  68.9 0.0 collective-permute-start.14
  68.9 1.1 %collective-permute-start.13 = (f32[8,128]{1,0:T(8,128)S(1)}, f32[8,128]{1,0:T(8,128)S(1)}, u32[]{:S(2)}, u32[]{:S(2)}) collective-permute-start(f32[8,128]{1,0:T(8,128)S(1)} %get-tuple-element.70.refs_0_), channel_id=1, source_target_pairs={{0,4},{4,0},{8,12},{12,8},{1,5},{5,1},{9,13},{13,9},{2,6},{6,2},{1... | collective-permute-start | bytes 12296 | tf_op jit(solution)/shard_map/ppermute | solution.py:53
  70.0 2.5 %collective-permute-done.13.refs_1_ = f32[8,128]{1,0:T(8,128)S(1)} collective-permute-done((f32[8,128]{1,0:T(8,128)S(1)}, f32[8,128]{1,0:T(8,128)S(1)}, u32[]{:S(2)}, u32[]{:S(2)}) %collective-permute-start.13) | collective-permute-done | bytes 4128 | tf_op jit(solution)/shard_map/ppermute | solution.py:53
  72.5 0.9 %collective-permute-done.14.refs_2_ = f32[16,128]{1,0:T(8,128)S(1)} collective-permute-done((f32[16,128]{1,0:T(8,128)S(1)}, f32[16,128]{1,0:T(8,128)S(1)}, u32[]{:S(2)}, u32[]{:S(2)}) %collective-permute-start.14) | collective-permute-done | bytes 8224 | tf_op jit(solution)/shard_map/ppermute | solution.py:53
  73.5 0.0 collective-permute-done.15.refs_3_
  73.5 0.3 shard_map.79
  73.9 0.1 collective-permute-start.16
  73.9 1.6 %collective-permute-start.17 = (f32[144,128]{1,0:T(8,128)S(1)}, f32[144,128]{1,0:T(8,128)S(1)}, u32[]{:S(2)}, u32[]{:S(2)}) collective-permute-start(f32[144,128]{1,0:T(8,128)S(1)} %get-tuple-element.79), channel_id=1, source_target_pairs={{0,2},{1,3},{2,0},{3,1},{4,6},{5,7},{6,4},{7,5},{8,10},{9,11},{10,... | collective-permute-start | bytes 221192 | tf_op jit(solution)/shard_map/ppermute | solution.py:68
  75.5 1.4 %collective-permute-start.18 = (f32[144,128]{1,0:T(8,128)S(1)}, f32[144,128]{1,0:T(8,128)S(1)}, u32[]{:S(2)}, u32[]{:S(2)}) collective-permute-start(f32[144,128]{1,0:T(8,128)S(1)} %get-tuple-element.78), channel_id=1, source_target_pairs={{0,3},{1,0},{2,1},{3,2},{4,7},{5,4},{6,5},{7,6},{8,11},{9,8},{10,9... | collective-permute-start | bytes 221192 | tf_op jit(solution)/shard_map/ppermute | solution.py:68
  76.9 1.0 %collective-permute-done.16.refs_0_ = f32[144,128]{1,0:T(8,128)S(1)} collective-permute-done((f32[144,128]{1,0:T(8,128)S(1)}, f32[144,128]{1,0:T(8,128)S(1)}, u32[]{:S(2)}, u32[]{:S(2)}) %collective-permute-start.16) | collective-permute-done | bytes 73760 | tf_op jit(solution)/shard_map/ppermute | solution.py:68
  77.9 1.0 %collective-permute-done.17.refs_1_ = f32[144,128]{1,0:T(8,128)S(1)} collective-permute-done((f32[144,128]{1,0:T(8,128)S(1)}, f32[144,128]{1,0:T(8,128)S(1)}, u32[]{:S(2)}, u32[]{:S(2)}) %collective-permute-start.17) | collective-permute-done | bytes 73760 | tf_op jit(solution)/shard_map/ppermute | solution.py:68
  78.9 0.1 collective-permute-done.18.refs_2_
  79.1 0.2 collective-permute-start.19
  79.3 3.7 %collective-permute-start.20 = (f32[48,128]{1,0:T(8,128)S(1)}, f32[48,128]{1,0:T(8,128)S(1)}, u32[]{:S(2)}, u32[]{:S(2)}) collective-permute-start(f32[48,128]{1,0:T(8,128)S(1)} %get-tuple-element.77), channel_id=1, source_target_pairs={{0,12},{4,0},{8,4},{12,8},{1,13},{5,1},{9,5},{13,9},{2,14},{6,2},{... | collective-permute-start | bytes 73736 | tf_op jit(solution)/shard_map/ppermute | solution.py:68
  83.0 1.1 %shard_map.80 = f32[1536,128]{1,0:T(8,128)} custom-call(f32[4,6,8,8,128]{4,3,2,1,0:T(8,128)S(1)} %get-tuple-element.49.source_ref, f32[4,6,8,8,128]{4,3,2,1,0:T(8,128)S(1)} %get-tuple-element.68.residual_ref, f32[8,128]{1,0:T(8,128)S(1)} %get-tuple-element.73.scales_ref), custom_call_target="tpu_custom_call" | custom-call | tf_op jit(solution)/shard_map/pallas_call | solution.py:32
  84.0 1.0 %collective-permute-done.19.before_ref = f32[48,128]{1,0:T(8,128)S(1)} collective-permute-done((f32[48,128]{1,0:T(8,128)S(1)}, f32[48,128]{1,0:T(8,128)S(1)}, u32[]{:S(2)}, u32[]{:S(2)}) %collective-permute-start.19) | collective-permute-done | bytes 24608 | tf_op jit(solution)/shard_map/ppermute | solution.py:68
  85.0 0.0 collective-permute-done.20.after_ref
  85.0 0.9 %shard_map.82 = f32[6,2048]{1,0:T(8,128)} custom-call(f32[144,128]{1,0:T(8,128)S(1)} %get-tuple-element.75.dense_ref, f32[48,128]{1,0:T(8,128)S(1)} %collective-permute-done.19.before_ref, f32[48,128]{1,0:T(8,128)S(1)} %collective-permute-done.20.after_ref), custom_call_target="tpu_custom_call" | custom-call | tf_op jit(solution)/shard_map/pallas_call | solution.py:32
  (4 shorter events, 0.0 us)
Async XLA Ops:
  0.6 10.1 %copy-start = (f32[16,6,8192]{2,0,1:T(8,128)S(1)}, f32[16,6,8192]{2,0,1:T(8,128)}, u32[]{:S(2)}) copy-start(f32[16,6,8192]{2,0,1:T(8,128)} %param.5) | copy-start | bytes 9437188
  0.6 10.1 %copy-start.1 = (f32[6,8192]{1,0:T(8,128)S(1)}, f32[6,8192]{1,0:T(8,128)}, u32[]{:S(2)}) copy-start(f32[6,8192]{1,0:T(8,128)} %far_perturb_ref.1) | copy-start | bytes 589828
  5.0 10.0 %collective-permute-start.2 = (f32[40,16]{1,0:T(8,128)}, f32[40,16]{1,0:T(8,128)S(1)}, u32[]{:S(2)}, u32[]{:S(2)}) collective-permute-start(f32[40,16]{1,0:T(8,128)} %get-tuple-element.45), channel_id=1, source_target_pairs={{0,12},{4,8},{8,4},{12,0},{1,13},{5,9},{9,5},{13,1},{2,14},{6,10},... | collective-permute-start | bytes 7688 | tf_op jit(solution)/shard_map/ppermute | solution.py:53
  10.1 4.8 %collective-permute-start.1 = (f32[32,16]{1,0:T(8,128)}, f32[32,16]{1,0:T(8,128)S(1)}, u32[]{:S(2)}, u32[]{:S(2)}) collective-permute-start(f32[32,16]{1,0:T(8,128)} %get-tuple-element.44), channel_id=1, source_target_pairs={{0,8},{4,12},{8,0},{12,4},{1,9},{5,13},{9,1},{13,5},{2,10},{6,14},... | collective-permute-start | bytes 6152 | tf_op jit(solution)/shard_map/ppermute | solution.py:53
  10.1 3.9 %collective-permute-start = (f32[24,16]{1,0:T(8,128)}, f32[24,16]{1,0:T(8,128)S(1)}, u32[]{:S(2)}, u32[]{:S(2)}) collective-permute-start(f32[24,16]{1,0:T(8,128)} %get-tuple-element.43.refs_0_), channel_id=1, source_target_pairs={{0,4},{4,0},{8,12},{12,8},{1,5},{5,1},{9,13},{13,9},{2,6},{6,2},{1... | collective-permute-start | bytes 4616 | tf_op jit(solution)/shard_map/ppermute | solution.py:53
  10.7 1.0 %copy-start.2 = (f32[6,8192]{1,0:T(8,128)S(1)}, f32[6,8192]{1,0:T(8,128)}, u32[]{:S(2)}) copy-start(f32[6,8192]{1,0:T(8,128)} %potential_ref.1) | copy-start | bytes 589828
  11.7 3.3 %copy-start.3 = (f32[24,16]{1,0:T(8,128)S(1)}, f32[24,16]{1,0:T(8,128)}, u32[]{:S(2)}) copy-start(f32[24,16]{1,0:T(8,128)} %get-tuple-element.43.refs_0_) | copy-start | bytes 4612
  11.7 10.4 %copy-start.4 = (f32[4]{0:T(128)S(1)}, f32[4]{0:T(128)}, u32[]{:S(2)}) copy-start(f32[4]{0:T(128)} %energies_ref.3) | copy-start | bytes 52
  15.8 13.8 %collective-permute-start.3 = (f32[4,6,3,8,128]{4,3,2,1,0:T(8,128)S(1)}, f32[4,6,3,8,128]{4,3,2,1,0:T(8,128)S(1)}, u32[]{:S(2)}, u32[]{:S(2)}) collective-permute-start(f32[4,6,3,8,128]{4,3,2,1,0:T(8,128)S(1)} %get-tuple-element.46.shared_ref), channel_id=1, source_target_pairs={{0,12},{4,0},{8,4},{12,8},{1,13},{5,1},{9,5},{13,9},{2,14},{6,2},{... | collective-permute-start | bytes 884744 | tf_op jit(solution)/shard_map/ppermute | solution.py:68
  17.6 16.0 %collective-permute-start.4 = (f32[4,6,3,8,128]{4,3,2,1,0:T(8,128)S(1)}, f32[4,6,3,8,128]{4,3,2,1,0:T(8,128)S(1)}, u32[]{:S(2)}, u32[]{:S(2)}) collective-permute-start(f32[4,6,3,8,128]{4,3,2,1,0:T(8,128)S(1)} %get-tuple-element.46.shared_ref), channel_id=1, source_target_pairs={{0,4},{4,8},{8,12},{12,0},{1,5},{5,9},{9,13},{13,1},{2,6},{6,10},{... | collective-permute-start | bytes 884744 | tf_op jit(solution)/shard_map/ppermute | solution.py:68
  17.9 18.0 %collective-permute-start.5 = (f32[4,6,2,8,128]{4,3,2,1,0:T(8,128)S(1)}, f32[4,6,2,8,128]{4,3,2,1,0:T(8,128)S(1)}, u32[]{:S(2)}, u32[]{:S(2)}) collective-permute-start(f32[4,6,2,8,128]{4,3,2,1,0:T(8,128)S(1)} %get-tuple-element.47.rest_ref), channel_id=1, source_target_pairs={{0,12},{4,0},{8,4},{12,8},{1,13},{5,1},{9,5},{13,9},{2,14},{6,2},{... | collective-permute-start | bytes 589832 | tf_op jit(solution)/shard_map/ppermute | solution.py:68
  21.4 17.9 %collective-permute-start.6 = (f32[4,6,2,8,128]{4,3,2,1,0:T(8,128)S(1)}, f32[4,6,2,8,128]{4,3,2,1,0:T(8,128)S(1)}, u32[]{:S(2)}, u32[]{:S(2)}) collective-permute-start(f32[4,6,2,8,128]{4,3,2,1,0:T(8,128)S(1)} %get-tuple-element.47.rest_ref), channel_id=1, source_target_pairs={{0,4},{4,8},{8,12},{12,0},{1,5},{5,9},{9,13},{13,1},{2,6},{6,10},{... | collective-permute-start | bytes 589832 | tf_op jit(solution)/shard_map/ppermute | solution.py:68
  33.8 6.4 %collective-permute-start.7 = (f32[2,6,3,8,128]{4,3,2,1,0:T(8,128)S(1)}, f32[2,6,3,8,128]{4,3,2,1,0:T(8,128)S(1)}, u32[]{:S(2)}, u32[]{:S(2)}) collective-permute-start(f32[2,6,3,8,128]{4,3,2,1,0:T(8,128)S(1)} %get-tuple-element.53.refs_0_), channel_id=1, source_target_pairs={{0,16},{16,0},{1,17},{17,1},{2,18},{18,2},{3,19},{19,3},{4,20},{20... | collective-permute-start | bytes 442376 | tf_op jit(solution)/shard_map/ppermute | solution.py:687
  35.4 5.2 %collective-permute-start.8 = (f32[2,6,3,8,128]{4,3,2,1,0:T(8,128)S(1)}, f32[2,6,3,8,128]{4,3,2,1,0:T(8,128)S(1)}, u32[]{:S(2)}, u32[]{:S(2)}) collective-permute-start(f32[2,6,3,8,128]{4,3,2,1,0:T(8,128)S(1)} %get-tuple-element.54.refs_1_), channel_id=1, source_target_pairs={{0,16},{16,0},{1,17},{17,1},{2,18},{18,2},{3,19},{19,3},{4,20},{20... | collective-permute-start | bytes 442376 | tf_op jit(solution)/shard_map/ppermute | solution.py:687
  41.2 7.3 %collective-permute-start.11 = (f32[24,128]{1,0:T(8,128)S(1)}, f32[24,128]{1,0:T(8,128)S(1)}, u32[]{:S(2)}, u32[]{:S(2)}) collective-permute-start(f32[24,128]{1,0:T(8,128)S(1)} %get-tuple-element.64), channel_id=1, source_target_pairs={{0,12},{4,8},{8,4},{12,0},{1,13},{5,9},{9,5},{13,1},{2,14},{6,10},... | collective-permute-start | bytes 36872 | tf_op jit(solution)/shard_map/ppermute | solution.py:53
  43.8 4.6 %collective-permute-start.10 = (f32[16,128]{1,0:T(8,128)S(1)}, f32[16,128]{1,0:T(8,128)S(1)}, u32[]{:S(2)}, u32[]{:S(2)}) collective-permute-start(f32[16,128]{1,0:T(8,128)S(1)} %get-tuple-element.63), channel_id=1, source_target_pairs={{0,8},{4,12},{8,0},{12,4},{1,9},{5,13},{9,1},{13,5},{2,10},{6,14},... | collective-permute-start | bytes 24584 | tf_op jit(solution)/shard_map/ppermute | solution.py:53
  43.8 3.6 %collective-permute-start.9 = (f32[8,128]{1,0:T(8,128)S(1)}, f32[8,128]{1,0:T(8,128)S(1)}, u32[]{:S(2)}, u32[]{:S(2)}) collective-permute-start(f32[8,128]{1,0:T(8,128)S(1)} %get-tuple-element.62.refs_0_), channel_id=1, source_target_pairs={{0,4},{4,0},{8,12},{12,8},{1,5},{5,1},{9,13},{13,9},{2,6},{6,2},{1... | collective-permute-start | bytes 12296 | tf_op jit(solution)/shard_map/ppermute | solution.py:53
  49.7 15.6 %collective-permute-start.12 = (f32[4,6,8,8,128]{4,3,2,1,0:T(8,128)S(1)}, f32[4,6,8,8,128]{4,3,2,1,0:T(8,128)S(1)}, u32[]{:S(2)}, u32[]{:S(2)}) collective-permute-start(f32[4,6,8,8,128]{4,3,2,1,0:T(8,128)S(1)} %get-tuple-element.65.refs_0_), channel_id=1, source_target_pairs={{0,12},{4,0},{8,4},{12,8},{1,13},{5,1},{9,5},{13,9},{2,14},{6,2},{... | collective-permute-start | bytes 2359304 | tf_op jit(solution)/shard_map/ppermute | solution.py:68
  65.6 7.8 %collective-permute-start.15 = (f32[24,128]{1,0:T(8,128)S(1)}, f32[24,128]{1,0:T(8,128)S(1)}, u32[]{:S(2)}, u32[]{:S(2)}) collective-permute-start(f32[24,128]{1,0:T(8,128)S(1)} %get-tuple-element.72), channel_id=1, source_target_pairs={{0,12},{4,8},{8,4},{12,0},{1,13},{5,9},{9,5},{13,1},{2,14},{6,10},... | collective-permute-start | bytes 36872 | tf_op jit(solution)/shard_map/ppermute | solution.py:53
  68.9 4.5 %collective-permute-start.14 = (f32[16,128]{1,0:T(8,128)S(1)}, f32[16,128]{1,0:T(8,128)S(1)}, u32[]{:S(2)}, u32[]{:S(2)}) collective-permute-start(f32[16,128]{1,0:T(8,128)S(1)} %get-tuple-element.71), channel_id=1, source_target_pairs={{0,8},{4,12},{8,0},{12,4},{1,9},{5,13},{9,1},{13,5},{2,10},{6,14},... | collective-permute-start | bytes 24584 | tf_op jit(solution)/shard_map/ppermute | solution.py:53
  68.9 3.6 %collective-permute-start.13 = (f32[8,128]{1,0:T(8,128)S(1)}, f32[8,128]{1,0:T(8,128)S(1)}, u32[]{:S(2)}, u32[]{:S(2)}) collective-permute-start(f32[8,128]{1,0:T(8,128)S(1)} %get-tuple-element.70.refs_0_), channel_id=1, source_target_pairs={{0,4},{4,0},{8,12},{12,8},{1,5},{5,1},{9,13},{13,9},{2,6},{6,2},{1... | collective-permute-start | bytes 12296 | tf_op jit(solution)/shard_map/ppermute | solution.py:53
  73.9 4.0 %collective-permute-start.16 = (f32[144,128]{1,0:T(8,128)S(1)}, f32[144,128]{1,0:T(8,128)S(1)}, u32[]{:S(2)}, u32[]{:S(2)}) collective-permute-start(f32[144,128]{1,0:T(8,128)S(1)} %get-tuple-element.80), channel_id=1, source_target_pairs={{0,1},{1,2},{2,3},{3,0},{4,5},{5,6},{6,7},{7,4},{8,9},{9,10},{10,1... | collective-permute-start | bytes 221192 | tf_op jit(solution)/shard_map/ppermute | solution.py:68
  73.9 5.0 %collective-permute-start.17 = (f32[144,128]{1,0:T(8,128)S(1)}, f32[144,128]{1,0:T(8,128)S(1)}, u32[]{:S(2)}, u32[]{:S(2)}) collective-permute-start(f32[144,128]{1,0:T(8,128)S(1)} %get-tuple-element.79), channel_id=1, source_target_pairs={{0,2},{1,3},{2,0},{3,1},{4,6},{5,7},{6,4},{7,5},{8,10},{9,11},{10,... | collective-permute-start | bytes 221192 | tf_op jit(solution)/shard_map/ppermute | solution.py:68
  75.5 3.6 %collective-permute-start.18 = (f32[144,128]{1,0:T(8,128)S(1)}, f32[144,128]{1,0:T(8,128)S(1)}, u32[]{:S(2)}, u32[]{:S(2)}) collective-permute-start(f32[144,128]{1,0:T(8,128)S(1)} %get-tuple-element.78), channel_id=1, source_target_pairs={{0,3},{1,0},{2,1},{3,2},{4,7},{5,4},{6,5},{7,6},{8,11},{9,8},{10,9... | collective-permute-start | bytes 221192 | tf_op jit(solution)/shard_map/ppermute | solution.py:68
  79.1 5.9 %collective-permute-start.19 = (f32[48,128]{1,0:T(8,128)S(1)}, f32[48,128]{1,0:T(8,128)S(1)}, u32[]{:S(2)}, u32[]{:S(2)}) collective-permute-start(f32[48,128]{1,0:T(8,128)S(1)} %get-tuple-element.76), channel_id=1, source_target_pairs={{0,4},{4,8},{8,12},{12,0},{1,5},{5,9},{9,13},{13,1},{2,6},{6,10},{... | collective-permute-start | bytes 73736 | tf_op jit(solution)/shard_map/ppermute | solution.py:68
  79.3 5.7 %collective-permute-start.20 = (f32[48,128]{1,0:T(8,128)S(1)}, f32[48,128]{1,0:T(8,128)S(1)}, u32[]{:S(2)}, u32[]{:S(2)}) collective-permute-start(f32[48,128]{1,0:T(8,128)S(1)} %get-tuple-element.77), channel_id=1, source_target_pairs={{0,12},{4,0},{8,4},{12,8},{1,13},{5,1},{9,5},{13,9},{2,14},{6,2},{... | collective-permute-start | bytes 73736 | tf_op jit(solution)/shard_map/ppermute | solution.py:68

commit v4 on v3

--- a/solution.py
+++ b/solution.py
@@ -42,7 +42,7 @@
 def copies(axis, rows, columns):
     size = lax.axis_size(axis)
     direct = size <= 4 and size & (size - 1) == 0
-    return [(rows + SUB * k, columns) for k in range(size - 1 if direct else 1)]
+    return [(rows, columns) for k in range(size - 1 if direct else 1)]
 
 
 def parts_of(arrays, axis):
@@ -324,7 +324,7 @@
     return total
 
 
-def halo_kernel(shape, after_ref, before_ref, square_ref, *halo_refs):
+def halo_kernel(shape, before_ref, after_ref, square_ref, *halo_refs):
     layers, group = shape
     each = group // len(halo_refs)
     for n in range(group):
@@ -361,30 +361,32 @@
     sums_ref[...] = multiply(shape, spots, planes_ref, inner_ref, field_ref, acc_ref)
 
 
-def rest_kernel(shape, share, planes_ref, inner_ref, partial_ref, after_ref, before_ref, field_ref, sums_ref, acc_ref):
+def other_kernel(shape, share, planes_ref, inner_ref, partial_ref, earlier_ref, *refs):
     norb, layers, group = shape
+    field_ref, sums_ref, acc_ref = refs[-3:]
+    each = group // (len(refs) - 3)
+    spots = pl.ds(share - lax.axis_index("freq") * share, share)
+    for n in range(group):
+        for z in range(layers):
+            field_ref[n, z] = partial_ref[n, z, spots] + refs[n // each][n % each, z]
+    sums = multiply(shape, spots, planes_ref, inner_ref, field_ref, acc_ref)
+    sums_ref[...] = sums + earlier_ref[...]
+
+
+def rest_kernel(shape, share, planes_ref, inner_ref, partial_ref, square_ref, mine_ref, other_ref, earlier_ref, after_ref, before_ref, *refs):
+    norb, layers, group = shape
+    applied_ref, sums_refs, (field_ref, acc_ref) = refs[0], refs[1:-2], refs[-2:]
+    place = lax.axis_index("freq") * share
+    mine, other = pl.ds(place, share), pl.ds(share - place, share)
     spots = pl.ds(2 * share, field_ref.shape[2])
     for n in range(group):
         for z in range(layers):
-            field_ref[n, z] = partial_ref[n, z, spots] + halo_sum(layers, n, z, before_ref, after_ref)
-    sums_ref[...] = multiply(shape, spots, planes_ref, inner_ref, field_ref, acc_ref)
-
-
-def other_kernel(shape, share, planes_ref, inner_ref, partial_ref, square_ref, mine_ref, mine_sums_ref, rest_ref, rest_sums_ref, *refs):
-    norb, layers, group, pieces = shape
-    halo_refs, applied_ref, sums_refs, (field_ref, acc_ref) = refs[:pieces], refs[pieces], refs[pieces + 1 : -2], refs[-2:]
-    each = group // pieces
-    place = lax.axis_index("freq") * share
-    mine, spots = pl.ds(place, share), pl.ds(share - place, share)
-    for n in range(group):
-        for z in range(layers):
-            field = partial_ref[n, z, spots] + halo_refs[n // each][n % each, z]
+            field = partial_ref[n, z, spots] + halo_sum(layers, n, z, before_ref, after_ref)
             field_ref[n, z] = field
-            applied_ref[n, z, spots] = field
+            applied_ref[n, z, 2 * share :] = field
             applied_ref[n, z, mine] = mine_ref[n, z]
-            applied_ref[n, z, 2 * share :] = rest_ref[n, z]
-    sums = multiply(shape[:3], spots, planes_ref, inner_ref, field_ref, acc_ref)
-    sums = sums + mine_sums_ref[...] + rest_sums_ref[...]
+            applied_ref[n, z, other] = other_ref[n, z]
+    sums = multiply(shape, spots, planes_ref, inner_ref, field_ref, acc_ref) + earlier_ref[...]
     sums = rows_to_lanes(jnp.concatenate([sums, jnp.sum(square_ref[...], axis=1)], axis=0))
     put_copies(sums_refs, sums)
 
@@ -680,14 +682,14 @@
         [(each, layers, share) + cells] * pieces,
         [],
         0,
+        before,
         after,
-        before,
         square,
     )
     partner = [lax.ppermute(halo, "freq", [(0, 1), (1, 0)]) for halo in halos]
     count = group * norb + group
     before_rest, after_rest = shifted(rest, "brick", 1), shifted(rest, "brick", -1)
-    mine, mine_sums = call(
+    mine, earlier = call(
         functools.partial(mine_kernel, (norb, layers, group), share),
         [shared.shape, (count, LANES)],
         [(count,) + cells],
@@ -697,31 +699,31 @@
         partial,
         *halos,
     )
-    rest, rest_sums = call(
-        functools.partial(rest_kernel, (norb, layers, group), share),
-        [rest.shape, (count, LANES)],
+    other, earlier = call(
+        functools.partial(other_kernel, (norb, layers, group), share),
+        [shared.shape, (count, LANES)],
         [(count,) + cells],
         0,
         planes,
         inner,
         partial,
-        after_rest,
-        before_rest,
+        earlier,
+        *partner,
     )
     applied, *sums = call(
-        functools.partial(other_kernel, (norb, layers, group, pieces), share),
+        functools.partial(rest_kernel, (norb, layers, group), share),
         [own] + copies("brick", SUB, LANES),
-        [shared.shape, (count,) + cells],
+        [rest.shape, (count,) + cells],
         0,
         planes,
         inner,
         partial,
         square,
         mine,
-        mine_sums,
-        rest,
-        rest_sums,
-        *partner,
+        other,
+        earlier,
+        after_rest,
+        before_rest,
     )
     sums = parts_of(sums, "brick")
     runs = 1

time: 86.1 us -> 83.7 us (0.972)
  starting transfers between devices: 30.6 us -> 29.2 us
  waiting for transfers between devices: 29.2 us -> 28.2 us
    ppermute x10, waiting for transfers between devices: 20.5 us -> 16.1 us  [shifted(): lax.ppermute(array, axis, [(i, (i + step) % size) for i in range(size)])]
    ppermute x2, waiting for transfers between devices: 0.36 us -> 4.22 us  [per_device(): partner = [lax.ppermute(halo, 'freq', [(0, 1), (1, 0)]) for halo in halos]]
    ppermute x9, starting transfers between devices: 14.6 us -> 13.7 us  [parts_of(): lax.ppermute(array, axis, [(i, i ^ k + 1) for i in range(size)])]
where the time goes in v4:
time: 83.7 us; the launch traced here: 83.5 us
  starting transfers between devices  29.2 us (35%)
  waiting for transfers between devices  28.2 us (34%)
  Pallas kernels  23.7 us (28%)
  between operations  1.44 us (2%)
  local copies, waits for them, and re-layouts  0.98 us (1%)
    pallas_call x15, Pallas kernels, call(): pl.pallas_call(kernel, out_shape=[jax.ShapeDtypeStruct(s, f32) for s in o...  23.7 us
    ppermute x10, waiting for transfers between devices, shifted(): lax.ppermute(array, axis, [(i, (i + step) % size) for i in range(size)])  16.1 us
    ppermute x9, starting transfers between devices, parts_of(): lax.ppermute(array, axis, [(i, i ^ k + 1) for i in range(size)])  13.7 us
    ppermute x10, starting transfers between devices, shifted(): lax.ppermute(array, axis, [(i, (i + step) % size) for i in range(size)])  13.4 us
    ppermute x9, waiting for transfers between devices, parts_of(): lax.ppermute(array, axis, [(i, i ^ k + 1) for i in range(size)])  7.92 us
    ppermute x2, waiting for transfers between devices, per_device(): partner = [lax.ppermute(halo, 'freq', [(0, 1), (1, 0)]) for halo in halos]  4.22 us
    ppermute x2, starting transfers between devices, per_device(): partner = [lax.ppermute(halo, 'freq', [(0, 1), (1, 0)]) for halo in halos]  2.09 us
  transfers between devices with their start and end apart: 21, of which 15 were waited for; matrix products, arithmetic and copies ran while one was open for 0% of the time, Pallas kernels for 18%

profile of v4, /device:TPU:0, one launch (start us, length us, event | category | flops | bytes accessed | tf_op | source)
XLA Modules:
  0.0 83.5 jit_solution(7668179730984749391)
XLA Ops:
  0.6 0.0 copy-start.1
  0.6 0.0 copy-start
  0.6 4.3 %shard_map.69 = (f32[24,16]{1,0:T(8,128)}, f32[24,16]{1,0:T(8,128)}, f32[24,16]{1,0:T(8,128)}) custom-call(f32[6144,128]{1,0:T(8,128)} %bitcast.18, f32[6,8192]{1,0:T(8,128)} %far_perturb_ref.1), custom_call_target="tpu_custom_call" | custom-call | tf_op jit(solution)/shard_map/pallas_call | solution.py:32
  5.0 4.1 %collective-permute-start.1 = (f32[24,16]{1,0:T(8,128)}, f32[24,16]{1,0:T(8,128)S(1)}, u32[]{:S(2)}, u32[]{:S(2)}) collective-permute-start(f32[24,16]{1,0:T(8,128)} %get-tuple-element.44), channel_id=1, source_target_pairs={{0,8},{4,12},{8,0},{12,4},{1,9},{5,13},{9,1},{13,5},{2,10},{6,14},... | collective-permute-start | bytes 4616 | tf_op jit(solution)/shard_map/ppermute | solution.py:53
  9.1 1.3 %collective-permute-start.2 = (f32[24,16]{1,0:T(8,128)}, f32[24,16]{1,0:T(8,128)S(1)}, u32[]{:S(2)}, u32[]{:S(2)}) collective-permute-start(f32[24,16]{1,0:T(8,128)} %get-tuple-element.45), channel_id=1, source_target_pairs={{0,12},{4,8},{8,4},{12,0},{1,13},{5,9},{9,5},{13,1},{2,14},{6,10},... | collective-permute-start | bytes 4616 | tf_op jit(solution)/shard_map/ppermute | solution.py:53
  10.4 0.2 collective-permute-start
  10.6 0.0 copy-done.1
  10.6 0.0 copy-done
  10.6 0.0 copy-start.2
  10.6 0.9 %copy-done.2 = f32[6,8192]{1,0:T(8,128)S(1)} copy-done((f32[6,8192]{1,0:T(8,128)S(1)}, f32[6,8192]{1,0:T(8,128)}, u32[]{:S(2)}) %copy-start.2) | copy-done | bytes 196632
  11.6 1.2 %shard_map.68 = (f32[16,6,8,8,128]{4,3,2,1,0:T(8,128)S(1)}, f32[6,8,8,128]{3,2,1,0:T(8,128)S(1)}, f32[6,8,8,128]{3,2,1,0:T(8,128)S(1)}) custom-call(f32[6144,128]{1,0:T(8,128)S(1)} %bitcast.19, f32[6,8192]{1,0:T(8,128)S(1)} %copy-done.1, f32[6,8192]{1,0:T(8,128)S(1)} %copy-done.2), custom_call_target="tpu_custom_call" | custom-call | tf_op jit(solution)/shard_map/pallas_call | solution.py:32
  12.8 0.0 collective-permute-done.1.refs_2_
  12.9 1.9 %collective-permute-done.2.refs_3_ = f32[24,16]{1,0:T(8,128)S(1)} collective-permute-done((f32[24,16]{1,0:T(8,128)}, f32[24,16]{1,0:T(8,128)S(1)}, u32[]{:S(2)}, u32[]{:S(2)}) %collective-permute-start.2) | collective-permute-done | bytes 1568 | tf_op jit(solution)/shard_map/ppermute | solution.py:53
  14.8 0.0 collective-permute-done.refs_1_
  14.8 0.0 copy-done.3
  14.8 0.8 shard_map.70
  15.6 2.1 %collective-permute-start.4 = (f32[4,6,3,8,128]{4,3,2,1,0:T(8,128)S(1)}, f32[4,6,3,8,128]{4,3,2,1,0:T(8,128)S(1)}, u32[]{:S(2)}, u32[]{:S(2)}) collective-permute-start(f32[4,6,3,8,128]{4,3,2,1,0:T(8,128)S(1)} %get-tuple-element.46.shared_ref), channel_id=1, source_target_pairs={{0,12},{4,0},{8,4},{12,8},{1,13},{5,1},{9,5},{13,9},{2,14},{6,2},{... | collective-permute-start | bytes 884744 | tf_op jit(solution)/shard_map/ppermute | solution.py:68
  17.7 0.0 collective-permute-start.3
  17.7 0.0 collective-permute-start.8
  17.7 3.8 %collective-permute-start.7 = (f32[4,6,2,8,128]{4,3,2,1,0:T(8,128)S(1)}, f32[4,6,2,8,128]{4,3,2,1,0:T(8,128)S(1)}, u32[]{:S(2)}, u32[]{:S(2)}) collective-permute-start(f32[4,6,2,8,128]{4,3,2,1,0:T(8,128)S(1)} %get-tuple-element.47.rest_ref), channel_id=1, source_target_pairs={{0,12},{4,0},{8,4},{12,8},{1,13},{5,1},{9,5},{13,9},{2,14},{6,2},{... | collective-permute-start | bytes 589832 | tf_op jit(solution)/shard_map/ppermute | solution.py:68
  22.2 0.0 copy-done.4
  22.2 6.9 %shard_map.71 = (f32[4,6,8,8,128]{4,3,2,1,0:T(8,128)S(1)}, f32[4,6,8,8,128]{4,3,2,1,0:T(8,128)S(1)}, f32[4,6,8,8,128]{4,3,2,1,0:T(8,128)S(1)}, f32[16,16,128]{2,...) custom-call(f32[1]{0:T(128)S(6)} %copy.8.omega_ref, f32[4]{0:T(128)S(1)} %copy-done.4, ...), custom_call_target="tpu_custom_call" | custom-call | tf_op jit(solution)/shard_map/pallas_call | solution.py:32
  29.1 5.3 %collective-permute-done.4.after_ref = f32[4,6,3,8,128]{4,3,2,1,0:T(8,128)S(1)} collective-permute-done((f32[4,6,3,8,128]{4,3,2,1,0:T(8,128)S(1)}, f32[4,6,3,8,128]{4,3,2,1,0:T(8,128)S(1)}, u32[]{:S(2)}, u32[]{:S(2)}) %collective-permute-start.4) | collective-permute-done | bytes 294944 | tf_op jit(solution)/shard_map/ppermute | solution.py:68
  34.4 0.0 collective-permute-done.3.before_ref
  34.4 0.1 shard_map.72
  34.5 1.6 %collective-permute-start.5 = (f32[2,6,3,8,128]{4,3,2,1,0:T(8,128)S(1)}, f32[2,6,3,8,128]{4,3,2,1,0:T(8,128)S(1)}, u32[]{:S(2)}, u32[]{:S(2)}) collective-permute-start(f32[2,6,3,8,128]{4,3,2,1,0:T(8,128)S(1)} %get-tuple-element.53.refs_0_), channel_id=1, source_target_pairs={{0,16},{16,0},{1,17},{17,1},{2,18},{18,2},{3,19},{19,3},{4,20},{20... | collective-permute-start | bytes 442376 | tf_op jit(solution)/shard_map/ppermute | solution.py:689
  36.1 0.5 collective-permute-start.6
  36.6 0.5 shard_map.73
  37.1 2.6 %collective-permute-done.5.refs_0_ = f32[2,6,3,8,128]{4,3,2,1,0:T(8,128)S(1)} collective-permute-done((f32[2,6,3,8,128]{4,3,2,1,0:T(8,128)S(1)}, f32[2,6,3,8,128]{4,3,2,1,0:T(8,128)S(1)}, u32[]{:S(2)}, u32[]{:S(2)}) %collective-permute-start.5) | collective-permute-done | bytes 147488 | tf_op jit(solution)/shard_map/ppermute | solution.py:689
  39.7 1.6 %collective-permute-done.6.refs_1_ = f32[2,6,3,8,128]{4,3,2,1,0:T(8,128)S(1)} collective-permute-done((f32[2,6,3,8,128]{4,3,2,1,0:T(8,128)S(1)}, f32[2,6,3,8,128]{4,3,2,1,0:T(8,128)S(1)}, u32[]{:S(2)}, u32[]{:S(2)}) %collective-permute-start.6) | collective-permute-done | bytes 147488 | tf_op jit(solution)/shard_map/ppermute | solution.py:689
  41.3 0.5 shard_map.74
  41.8 0.0 collective-permute-done.8.before_ref
  41.8 0.0 collective-permute-done.7.after_ref
  41.8 0.6 shard_map.75
  42.4 0.1 collective-permute-start.10
  42.4 2.7 %collective-permute-start.11 = (f32[8,128]{1,0:T(8,128)S(1)}, f32[8,128]{1,0:T(8,128)S(1)}, u32[]{:S(2)}, u32[]{:S(2)}) collective-permute-start(f32[8,128]{1,0:T(8,128)S(1)} %get-tuple-element.64), channel_id=1, source_target_pairs={{0,12},{4,8},{8,4},{12,0},{1,13},{5,9},{9,5},{13,1},{2,14},{6,10},... | collective-permute-start | bytes 12296 | tf_op jit(solution)/shard_map/ppermute | solution.py:53
  45.1 0.8 collective-permute-start.9
  45.9 1.1 %collective-permute-done.10.refs_2_ = f32[8,128]{1,0:T(8,128)S(1)} collective-permute-done((f32[8,128]{1,0:T(8,128)S(1)}, f32[8,128]{1,0:T(8,128)S(1)}, u32[]{:S(2)}, u32[]{:S(2)}) %collective-permute-start.10) | collective-permute-done | bytes 4128 | tf_op jit(solution)/shard_map/ppermute | solution.py:53
  47.0 1.0 %collective-permute-done.11.refs_3_ = f32[8,128]{1,0:T(8,128)S(1)} collective-permute-done((f32[8,128]{1,0:T(8,128)S(1)}, f32[8,128]{1,0:T(8,128)S(1)}, u32[]{:S(2)}, u32[]{:S(2)}) %collective-permute-start.11) | collective-permute-done | bytes 4128 | tf_op jit(solution)/shard_map/ppermute | solution.py:53
  48.0 0.8 collective-permute-done.9.refs_1_
  48.8 1.2 %shard_map.76 = (f32[4,6,8,8,128]{4,3,2,1,0:T(8,128)S(1)}, f32[64,128]{1,0:T(8,128)S(1)}, f32[12,128]{1,0:T(8,128)S(1)}) custom-call(f32[16,6,8,8,128]{4,3,2,1,0:T(8,128)S(1)} %get-tuple-element.40.planes_ref, f32[4,6,8,8,128]{4,3,2,1,0:T(8,128)S(1)} %get-tuple-element.49.source_ref, f32[4,6,8,8,128]{4,3,2,1,0:T(8,128)S(1)} %get-tuple-element.59.applied_ref, ...), custom_call_target="tpu_custom_call" | custom-call | tf_op jit(solution)/shard_map/pallas_call | solution.py:32
  50.0 1.9 %collective-permute-start.12 = (f32[4,6,8,8,128]{4,3,2,1,0:T(8,128)S(1)}, f32[4,6,8,8,128]{4,3,2,1,0:T(8,128)S(1)}, u32[]{:S(2)}, u32[]{:S(2)}) collective-permute-start(f32[4,6,8,8,128]{4,3,2,1,0:T(8,128)S(1)} %get-tuple-element.65.refs_0_), channel_id=1, source_target_pairs={{0,12},{4,0},{8,4},{12,8},{1,13},{5,1},{9,5},{13,9},{2,14},{6,2},{... | collective-permute-start | bytes 2359304 | tf_op jit(solution)/shard_map/ppermute | solution.py:68
  51.9 5.0 %shard_map.77 = (f32[4,6,8,8,128]{4,3,2,1,0:T(8,128)S(1)}, f32[12,8,128]{2,1,0:T(8,128)S(1)}) custom-call(f32[1]{0:T(128)S(6)} %copy.8.omega_ref, f32[4]{0:T(128)S(1)} %copy-done.4, f32[16,6,8,8,128]{4,3,2,1,0:T(8,128)S(1)} %get-tuple-element.40.planes_ref, f32[6,8,8,128]{3,2,1,0:T(8,128)S(1)} %get-tuple-element.42.potential_ref, ...), custom_call_target="tpu_custom_call" | custom-call | tf_op jit(solution)/shard_map/pallas_call | solution.py:32
  56.9 5.6 %collective-permute-done.12.refs_1_ = f32[4,6,8,8,128]{4,3,2,1,0:T(8,128)S(1)} collective-permute-done((f32[4,6,8,8,128]{4,3,2,1,0:T(8,128)S(1)}, f32[4,6,8,8,128]{4,3,2,1,0:T(8,128)S(1)}, u32[]{:S(2)}, u32[]{:S(2)}) %collective-permute-start.12) | collective-permute-done | bytes 786464 | tf_op jit(solution)/shard_map/ppermute | solution.py:68
  62.4 0.3 shard_map.78
  62.8 1.7 %collective-permute-start.14 = (f32[8,128]{1,0:T(8,128)S(1)}, f32[8,128]{1,0:T(8,128)S(1)}, u32[]{:S(2)}, u32[]{:S(2)}) collective-permute-start(f32[8,128]{1,0:T(8,128)S(1)} %get-tuple-element.71), channel_id=1, source_target_pairs={{0,8},{4,12},{8,0},{12,4},{1,9},{5,13},{9,1},{13,5},{2,10},{6,14},... | collective-permute-start | bytes 12296 | tf_op jit(solution)/shard_map/ppermute | solution.py:53
  64.4 2.3 %collective-permute-start.15 = (f32[8,128]{1,0:T(8,128)S(1)}, f32[8,128]{1,0:T(8,128)S(1)}, u32[]{:S(2)}, u32[]{:S(2)}) collective-permute-start(f32[8,128]{1,0:T(8,128)S(1)} %get-tuple-element.72), channel_id=1, source_target_pairs={{0,12},{4,8},{8,4},{12,0},{1,13},{5,9},{9,5},{13,1},{2,14},{6,10},... | collective-permute-start | bytes 12296 | tf_op jit(solution)/shard_map/ppermute | solution.py:53
  66.7 0.5 collective-permute-start.13
  67.2 0.1 collective-permute-done.14.refs_2_
  67.3 2.6 %collective-permute-done.15.refs_3_ = f32[8,128]{1,0:T(8,128)S(1)} collective-permute-done((f32[8,128]{1,0:T(8,128)S(1)}, f32[8,128]{1,0:T(8,128)S(1)}, u32[]{:S(2)}, u32[]{:S(2)}) %collective-permute-start.15) | collective-permute-done | bytes 4128 | tf_op jit(solution)/shard_map/ppermute | solution.py:53
  69.8 0.5 collective-permute-done.13.refs_1_
  70.3 0.4 shard_map.79
  70.7 0.1 collective-permute-start.18
  70.8 1.5 %collective-permute-start.17 = (f32[144,128]{1,0:T(8,128)S(1)}, f32[144,128]{1,0:T(8,128)S(1)}, u32[]{:S(2)}, u32[]{:S(2)}) collective-permute-start(f32[144,128]{1,0:T(8,128)S(1)} %get-tuple-element.79), channel_id=1, source_target_pairs={{0,2},{1,3},{2,0},{3,1},{4,6},{5,7},{6,4},{7,5},{8,10},{9,11},{10,... | collective-permute-start | bytes 221192 | tf_op jit(solution)/shard_map/ppermute | solution.py:68
  72.3 0.2 collective-permute-start.16
  72.5 0.3 collective-permute-done.18.refs_2_
  72.7 4.1 %collective-permute-done.17.refs_1_ = f32[144,128]{1,0:T(8,128)S(1)} collective-permute-done((f32[144,128]{1,0:T(8,128)S(1)}, f32[144,128]{1,0:T(8,128)S(1)}, u32[]{:S(2)}, u32[]{:S(2)}) %collective-permute-start.17) | collective-permute-done | bytes 73760 | tf_op jit(solution)/shard_map/ppermute | solution.py:68
  76.8 0.1 collective-permute-done.16.refs_0_
  77.0 0.6 collective-permute-start.19
  77.5 3.3 %collective-permute-start.20 = (f32[48,128]{1,0:T(8,128)S(1)}, f32[48,128]{1,0:T(8,128)S(1)}, u32[]{:S(2)}, u32[]{:S(2)}) collective-permute-start(f32[48,128]{1,0:T(8,128)S(1)} %get-tuple-element.77), channel_id=1, source_target_pairs={{0,12},{4,0},{8,4},{12,8},{1,13},{5,1},{9,5},{13,9},{2,14},{6,2},{... | collective-permute-start | bytes 73736 | tf_op jit(solution)/shard_map/ppermute | solution.py:68
  80.8 1.1 %shard_map.80 = f32[1536,128]{1,0:T(8,128)} custom-call(f32[4,6,8,8,128]{4,3,2,1,0:T(8,128)S(1)} %get-tuple-element.49.source_ref, f32[4,6,8,8,128]{4,3,2,1,0:T(8,128)S(1)} %get-tuple-element.68.residual_ref, f32[8,128]{1,0:T(8,128)S(1)} %get-tuple-element.73.scales_ref), custom_call_target="tpu_custom_call" | custom-call | tf_op jit(solution)/shard_map/pallas_call | solution.py:32
  81.9 0.8 collective-permute-done.19.before_ref
  82.6 0.0 collective-permute-done.20.after_ref
  82.6 0.9 %shard_map.82 = f32[6,2048]{1,0:T(8,128)} custom-call(f32[144,128]{1,0:T(8,128)S(1)} %get-tuple-element.75.dense_ref, f32[48,128]{1,0:T(8,128)S(1)} %collective-permute-done.19.before_ref, f32[48,128]{1,0:T(8,128)S(1)} %collective-permute-done.20.after_ref), custom_call_target="tpu_custom_call" | custom-call | tf_op jit(solution)/shard_map/pallas_call | solution.py:32
  (4 shorter events, 0.0 us)
Async XLA Ops:
  0.6 10.0 %copy-start.1 = (f32[6,8192]{1,0:T(8,128)S(1)}, f32[6,8192]{1,0:T(8,128)}, u32[]{:S(2)}) copy-start(f32[6,8192]{1,0:T(8,128)} %far_perturb_ref.1) | copy-start | bytes 589828
  0.6 10.0 %copy-start = (f32[16,6,8192]{2,0,1:T(8,128)S(1)}, f32[16,6,8192]{2,0,1:T(8,128)}, u32[]{:S(2)}) copy-start(f32[16,6,8192]{2,0,1:T(8,128)} %param.5) | copy-start | bytes 9437188
  5.0 7.9 %collective-permute-start.1 = (f32[24,16]{1,0:T(8,128)}, f32[24,16]{1,0:T(8,128)S(1)}, u32[]{:S(2)}, u32[]{:S(2)}) collective-permute-start(f32[24,16]{1,0:T(8,128)} %get-tuple-element.44), channel_id=1, source_target_pairs={{0,8},{4,12},{8,0},{12,4},{1,9},{5,13},{9,1},{13,5},{2,10},{6,14},... | collective-permute-start | bytes 4616 | tf_op jit(solution)/shard_map/ppermute | solution.py:53
  9.1 5.7 %collective-permute-start.2 = (f32[24,16]{1,0:T(8,128)}, f32[24,16]{1,0:T(8,128)S(1)}, u32[]{:S(2)}, u32[]{:S(2)}) collective-permute-start(f32[24,16]{1,0:T(8,128)} %get-tuple-element.45), channel_id=1, source_target_pairs={{0,12},{4,8},{8,4},{12,0},{1,13},{5,9},{9,5},{13,1},{2,14},{6,10},... | collective-permute-start | bytes 4616 | tf_op jit(solution)/shard_map/ppermute | solution.py:53
  10.4 4.4 %collective-permute-start = (f32[24,16]{1,0:T(8,128)}, f32[24,16]{1,0:T(8,128)S(1)}, u32[]{:S(2)}, u32[]{:S(2)}) collective-permute-start(f32[24,16]{1,0:T(8,128)} %get-tuple-element.43.refs_0_), channel_id=1, source_target_pairs={{0,4},{4,0},{8,12},{12,8},{1,5},{5,1},{9,13},{13,9},{2,6},{6,2},{1... | collective-permute-start | bytes 4616 | tf_op jit(solution)/shard_map/ppermute | solution.py:53
  10.6 1.0 %copy-start.2 = (f32[6,8192]{1,0:T(8,128)S(1)}, f32[6,8192]{1,0:T(8,128)}, u32[]{:S(2)}) copy-start(f32[6,8192]{1,0:T(8,128)} %potential_ref.1) | copy-start | bytes 589828
  11.6 3.2 %copy-start.3 = (f32[24,16]{1,0:T(8,128)S(1)}, f32[24,16]{1,0:T(8,128)}, u32[]{:S(2)}) copy-start(f32[24,16]{1,0:T(8,128)} %get-tuple-element.43.refs_0_) | copy-start | bytes 4612
  11.6 10.6 %copy-start.4 = (f32[4]{0:T(128)S(1)}, f32[4]{0:T(128)}, u32[]{:S(2)}) copy-start(f32[4]{0:T(128)} %energies_ref.3) | copy-start | bytes 52
  15.6 18.8 %collective-permute-start.4 = (f32[4,6,3,8,128]{4,3,2,1,0:T(8,128)S(1)}, f32[4,6,3,8,128]{4,3,2,1,0:T(8,128)S(1)}, u32[]{:S(2)}, u32[]{:S(2)}) collective-permute-start(f32[4,6,3,8,128]{4,3,2,1,0:T(8,128)S(1)} %get-tuple-element.46.shared_ref), channel_id=1, source_target_pairs={{0,12},{4,0},{8,4},{12,8},{1,13},{5,1},{9,5},{13,9},{2,14},{6,2},{... | collective-permute-start | bytes 884744 | tf_op jit(solution)/shard_map/ppermute | solution.py:68
  17.7 16.7 %collective-permute-start.3 = (f32[4,6,3,8,128]{4,3,2,1,0:T(8,128)S(1)}, f32[4,6,3,8,128]{4,3,2,1,0:T(8,128)S(1)}, u32[]{:S(2)}, u32[]{:S(2)}) collective-permute-start(f32[4,6,3,8,128]{4,3,2,1,0:T(8,128)S(1)} %get-tuple-element.46.shared_ref), channel_id=1, source_target_pairs={{0,4},{4,8},{8,12},{12,0},{1,5},{5,9},{9,13},{13,1},{2,6},{6,10},{... | collective-permute-start | bytes 884744 | tf_op jit(solution)/shard_map/ppermute | solution.py:68
  17.7 24.1 %collective-permute-start.8 = (f32[4,6,2,8,128]{4,3,2,1,0:T(8,128)S(1)}, f32[4,6,2,8,128]{4,3,2,1,0:T(8,128)S(1)}, u32[]{:S(2)}, u32[]{:S(2)}) collective-permute-start(f32[4,6,2,8,128]{4,3,2,1,0:T(8,128)S(1)} %get-tuple-element.47.rest_ref), channel_id=1, source_target_pairs={{0,4},{4,8},{8,12},{12,0},{1,5},{5,9},{9,13},{13,1},{2,6},{6,10},{... | collective-permute-start | bytes 589832 | tf_op jit(solution)/shard_map/ppermute | solution.py:68
  17.7 24.1 %collective-permute-start.7 = (f32[4,6,2,8,128]{4,3,2,1,0:T(8,128)S(1)}, f32[4,6,2,8,128]{4,3,2,1,0:T(8,128)S(1)}, u32[]{:S(2)}, u32[]{:S(2)}) collective-permute-start(f32[4,6,2,8,128]{4,3,2,1,0:T(8,128)S(1)} %get-tuple-element.47.rest_ref), channel_id=1, source_target_pairs={{0,12},{4,0},{8,4},{12,8},{1,13},{5,1},{9,5},{13,9},{2,14},{6,2},{... | collective-permute-start | bytes 589832 | tf_op jit(solution)/shard_map/ppermute | solution.py:68
  34.5 5.2 %collective-permute-start.5 = (f32[2,6,3,8,128]{4,3,2,1,0:T(8,128)S(1)}, f32[2,6,3,8,128]{4,3,2,1,0:T(8,128)S(1)}, u32[]{:S(2)}, u32[]{:S(2)}) collective-permute-start(f32[2,6,3,8,128]{4,3,2,1,0:T(8,128)S(1)} %get-tuple-element.53.refs_0_), channel_id=1, source_target_pairs={{0,16},{16,0},{1,17},{17,1},{2,18},{18,2},{3,19},{19,3},{4,20},{20... | collective-permute-start | bytes 442376 | tf_op jit(solution)/shard_map/ppermute | solution.py:689
  36.1 5.2 %collective-permute-start.6 = (f32[2,6,3,8,128]{4,3,2,1,0:T(8,128)S(1)}, f32[2,6,3,8,128]{4,3,2,1,0:T(8,128)S(1)}, u32[]{:S(2)}, u32[]{:S(2)}) collective-permute-start(f32[2,6,3,8,128]{4,3,2,1,0:T(8,128)S(1)} %get-tuple-element.54.refs_1_), channel_id=1, source_target_pairs={{0,16},{16,0},{1,17},{17,1},{2,18},{18,2},{3,19},{19,3},{4,20},{20... | collective-permute-start | bytes 442376 | tf_op jit(solution)/shard_map/ppermute | solution.py:689
  42.4 4.7 %collective-permute-start.10 = (f32[8,128]{1,0:T(8,128)S(1)}, f32[8,128]{1,0:T(8,128)S(1)}, u32[]{:S(2)}, u32[]{:S(2)}) collective-permute-start(f32[8,128]{1,0:T(8,128)S(1)} %get-tuple-element.63), channel_id=1, source_target_pairs={{0,8},{4,12},{8,0},{12,4},{1,9},{5,13},{9,1},{13,5},{2,10},{6,14},... | collective-permute-start | bytes 12296 | tf_op jit(solution)/shard_map/ppermute | solution.py:53
  42.4 5.6 %collective-permute-start.11 = (f32[8,128]{1,0:T(8,128)S(1)}, f32[8,128]{1,0:T(8,128)S(1)}, u32[]{:S(2)}, u32[]{:S(2)}) collective-permute-start(f32[8,128]{1,0:T(8,128)S(1)} %get-tuple-element.64), channel_id=1, source_target_pairs={{0,12},{4,8},{8,4},{12,0},{1,13},{5,9},{9,5},{13,1},{2,14},{6,10},... | collective-permute-start | bytes 12296 | tf_op jit(solution)/shard_map/ppermute | solution.py:53
  45.1 3.7 %collective-permute-start.9 = (f32[8,128]{1,0:T(8,128)S(1)}, f32[8,128]{1,0:T(8,128)S(1)}, u32[]{:S(2)}, u32[]{:S(2)}) collective-permute-start(f32[8,128]{1,0:T(8,128)S(1)} %get-tuple-element.62.refs_0_), channel_id=1, source_target_pairs={{0,4},{4,0},{8,12},{12,8},{1,5},{5,1},{9,13},{13,9},{2,6},{6,2},{1... | collective-permute-start | bytes 12296 | tf_op jit(solution)/shard_map/ppermute | solution.py:53
  50.0 12.4 %collective-permute-start.12 = (f32[4,6,8,8,128]{4,3,2,1,0:T(8,128)S(1)}, f32[4,6,8,8,128]{4,3,2,1,0:T(8,128)S(1)}, u32[]{:S(2)}, u32[]{:S(2)}) collective-permute-start(f32[4,6,8,8,128]{4,3,2,1,0:T(8,128)S(1)} %get-tuple-element.65.refs_0_), channel_id=1, source_target_pairs={{0,12},{4,0},{8,4},{12,8},{1,13},{5,1},{9,5},{13,9},{2,14},{6,2},{... | collective-permute-start | bytes 2359304 | tf_op jit(solution)/shard_map/ppermute | solution.py:68
  62.8 4.5 %collective-permute-start.14 = (f32[8,128]{1,0:T(8,128)S(1)}, f32[8,128]{1,0:T(8,128)S(1)}, u32[]{:S(2)}, u32[]{:S(2)}) collective-permute-start(f32[8,128]{1,0:T(8,128)S(1)} %get-tuple-element.71), channel_id=1, source_target_pairs={{0,8},{4,12},{8,0},{12,4},{1,9},{5,13},{9,1},{13,5},{2,10},{6,14},... | collective-permute-start | bytes 12296 | tf_op jit(solution)/shard_map/ppermute | solution.py:53
  64.4 5.4 %collective-permute-start.15 = (f32[8,128]{1,0:T(8,128)S(1)}, f32[8,128]{1,0:T(8,128)S(1)}, u32[]{:S(2)}, u32[]{:S(2)}) collective-permute-start(f32[8,128]{1,0:T(8,128)S(1)} %get-tuple-element.72), channel_id=1, source_target_pairs={{0,12},{4,8},{8,4},{12,0},{1,13},{5,9},{9,5},{13,1},{2,14},{6,10},... | collective-permute-start | bytes 12296 | tf_op jit(solution)/shard_map/ppermute | solution.py:53
  66.7 3.6 %collective-permute-start.13 = (f32[8,128]{1,0:T(8,128)S(1)}, f32[8,128]{1,0:T(8,128)S(1)}, u32[]{:S(2)}, u32[]{:S(2)}) collective-permute-start(f32[8,128]{1,0:T(8,128)S(1)} %get-tuple-element.70.refs_0_), channel_id=1, source_target_pairs={{0,4},{4,0},{8,12},{12,8},{1,5},{5,1},{9,13},{13,9},{2,6},{6,2},{1... | collective-permute-start | bytes 12296 | tf_op jit(solution)/shard_map/ppermute | solution.py:53
  70.7 2.0 %collective-permute-start.18 = (f32[144,128]{1,0:T(8,128)S(1)}, f32[144,128]{1,0:T(8,128)S(1)}, u32[]{:S(2)}, u32[]{:S(2)}) collective-permute-start(f32[144,128]{1,0:T(8,128)S(1)} %get-tuple-element.78), channel_id=1, source_target_pairs={{0,3},{1,0},{2,1},{3,2},{4,7},{5,4},{6,5},{7,6},{8,11},{9,8},{10,9... | collective-permute-start | bytes 221192 | tf_op jit(solution)/shard_map/ppermute | solution.py:68
  70.8 6.1 %collective-permute-start.17 = (f32[144,128]{1,0:T(8,128)S(1)}, f32[144,128]{1,0:T(8,128)S(1)}, u32[]{:S(2)}, u32[]{:S(2)}) collective-permute-start(f32[144,128]{1,0:T(8,128)S(1)} %get-tuple-element.79), channel_id=1, source_target_pairs={{0,2},{1,3},{2,0},{3,1},{4,6},{5,7},{6,4},{7,5},{8,10},{9,11},{10,... | collective-permute-start | bytes 221192 | tf_op jit(solution)/shard_map/ppermute | solution.py:68
  72.3 4.6 %collective-permute-start.16 = (f32[144,128]{1,0:T(8,128)S(1)}, f32[144,128]{1,0:T(8,128)S(1)}, u32[]{:S(2)}, u32[]{:S(2)}) collective-permute-start(f32[144,128]{1,0:T(8,128)S(1)} %get-tuple-element.80), channel_id=1, source_target_pairs={{0,1},{1,2},{2,3},{3,0},{4,5},{5,6},{6,7},{7,4},{8,9},{9,10},{10,1... | collective-permute-start | bytes 221192 | tf_op jit(solution)/shard_map/ppermute | solution.py:68
  77.0 5.7 %collective-permute-start.19 = (f32[48,128]{1,0:T(8,128)S(1)}, f32[48,128]{1,0:T(8,128)S(1)}, u32[]{:S(2)}, u32[]{:S(2)}) collective-permute-start(f32[48,128]{1,0:T(8,128)S(1)} %get-tuple-element.76), channel_id=1, source_target_pairs={{0,4},{4,8},{8,12},{12,0},{1,5},{5,9},{9,13},{13,1},{2,6},{6,10},{... | collective-permute-start | bytes 73736 | tf_op jit(solution)/shard_map/ppermute | solution.py:68
  77.5 5.1 %collective-permute-start.20 = (f32[48,128]{1,0:T(8,128)S(1)}, f32[48,128]{1,0:T(8,128)S(1)}, u32[]{:S(2)}, u32[]{:S(2)}) collective-permute-start(f32[48,128]{1,0:T(8,128)S(1)} %get-tuple-element.77), channel_id=1, source_target_pairs={{0,12},{4,0},{8,4},{12,8},{1,13},{5,1},{9,5},{13,9},{2,14},{6,2},{... | collective-permute-start | bytes 73736 | tf_op jit(solution)/shard_map/ppermute | solution.py:68

commit v5 on v4

--- a/solution.py
+++ b/solution.py
@@ -726,7 +726,7 @@
         before_rest,
     )
     sums = parts_of(sums, "brick")
-    runs = 1
+    runs = 1 if group % 2 else 2
     part = group // runs
     steps = [
         call(
@@ -797,7 +797,7 @@
         scales,
     )
     dense, top, bottom = call(
-        functools.partial(gather_kernel, edge), [cut, (edge, LANES), (edge, LANES)], [], 0, cuts, *others
+        functools.partial(gather_kernel, edge), [cut, (edge, LANES), (edge, LANES)], [], 0, cuts, *others[::-1]
     )
     before, after = shifted(top, "brick", 1), shifted(bottom, "brick", -1)
     (induced,) = call(

time: 83.7 us -> 82.4 us (0.984)
  waiting for transfers between devices: 28.2 us -> 25.1 us
  starting transfers between devices: 29.2 us -> 30.7 us
    ppermute x10 -> x11, waiting for transfers between devices: 16.1 us -> 13 us  [shifted(): lax.ppermute(array, axis, [(i, (i + step) % size) for i in range(size)])]
    ppermute x10 -> x11, starting transfers between devices: 13.4 us -> 14.9 us  [shifted(): lax.ppermute(array, axis, [(i, (i + step) % size) for i in range(size)])]
    pallas_call x15 -> x16, Pallas kernels: 23.7 us -> 24 us  [call(): pl.pallas_call(kernel, out_shape=[jax.ShapeDtypeStruct(s, f32) for s in o...]
  transfers between devices with their start and end apart: 21 -> 22, of which waited for: 15 -> 16; matrix products, arithmetic and copies ran while one was open for 0% -> 0% of each run, Pallas kernels for 18% -> 20%
where the time goes in v5:
time: 82.4 us; the launch traced here: 82.2 us
  starting transfers between devices  30.7 us (37%)
  waiting for transfers between devices  25.1 us (30%)
  Pallas kernels  24 us (29%)
  between operations  1.44 us (2%)
  local copies, waits for them, and re-layouts  0.98 us (1%)
    pallas_call x16, Pallas kernels, call(): pl.pallas_call(kernel, out_shape=[jax.ShapeDtypeStruct(s, f32) for s in o...  24 us
    ppermute x11, starting transfers between devices, shifted(): lax.ppermute(array, axis, [(i, (i + step) % size) for i in range(size)])  14.9 us
    ppermute x9, starting transfers between devices, parts_of(): lax.ppermute(array, axis, [(i, i ^ k + 1) for i in range(size)])  13.7 us
    ppermute x11, waiting for transfers between devices, shifted(): lax.ppermute(array, axis, [(i, (i + step) % size) for i in range(size)])  13 us
    ppermute x9, waiting for transfers between devices, parts_of(): lax.ppermute(array, axis, [(i, i ^ k + 1) for i in range(size)])  7.92 us
    ppermute x2, waiting for transfers between devices, per_device(): partner = [lax.ppermute(halo, 'freq', [(0, 1), (1, 0)]) for halo in halos]  4.22 us
    ppermute x2, starting transfers between devices, per_device(): partner = [lax.ppermute(halo, 'freq', [(0, 1), (1, 0)]) for halo in halos]  2.09 us
  transfers between devices with their start and end apart: 22, of which 16 were waited for; matrix products, arithmetic and copies ran while one was open for 0% of the time, Pallas kernels for 20%

profile of v5, /device:TPU:0, one launch (start us, length us, event | category | flops | bytes accessed | tf_op | source)
XLA Modules:
  0.0 82.2 jit_solution(7337168875330980699)
XLA Ops:
  0.6 0.0 copy-start.1
  0.6 0.0 copy-start
  0.6 4.3 %shard_map.69 = (f32[24,16]{1,0:T(8,128)}, f32[24,16]{1,0:T(8,128)}, f32[24,16]{1,0:T(8,128)}) custom-call(f32[6144,128]{1,0:T(8,128)} %bitcast.18, f32[6,8192]{1,0:T(8,128)} %far_perturb_ref.1), custom_call_target="tpu_custom_call" | custom-call | tf_op jit(solution)/shard_map/pallas_call | solution.py:32
  5.0 4.1 %collective-permute-start.1 = (f32[24,16]{1,0:T(8,128)}, f32[24,16]{1,0:T(8,128)S(1)}, u32[]{:S(2)}, u32[]{:S(2)}) collective-permute-start(f32[24,16]{1,0:T(8,128)} %get-tuple-element.47), channel_id=1, source_target_pairs={{0,8},{4,12},{8,0},{12,4},{1,9},{5,13},{9,1},{13,5},{2,10},{6,14},... | collective-permute-start | bytes 4616 | tf_op jit(solution)/shard_map/ppermute | solution.py:53
  9.1 1.3 %collective-permute-start.2 = (f32[24,16]{1,0:T(8,128)}, f32[24,16]{1,0:T(8,128)S(1)}, u32[]{:S(2)}, u32[]{:S(2)}) collective-permute-start(f32[24,16]{1,0:T(8,128)} %get-tuple-element.48), channel_id=1, source_target_pairs={{0,12},{4,8},{8,4},{12,0},{1,13},{5,9},{9,5},{13,1},{2,14},{6,10},... | collective-permute-start | bytes 4616 | tf_op jit(solution)/shard_map/ppermute | solution.py:53
  10.4 0.2 collective-permute-start
  10.6 0.0 copy-done.1
  10.6 0.9 %copy-done.2 = f32[6,8192]{1,0:T(8,128)S(1)} copy-done((f32[6,8192]{1,0:T(8,128)S(1)}, f32[6,8192]{1,0:T(8,128)}, u32[]{:S(2)}) %copy-start.2) | copy-done | bytes 196632
  11.6 1.2 %shard_map.68 = (f32[16,6,8,8,128]{4,3,2,1,0:T(8,128)S(1)}, f32[6,8,8,128]{3,2,1,0:T(8,128)S(1)}, f32[6,8,8,128]{3,2,1,0:T(8,128)S(1)}) custom-call(f32[6144,128]{1,0:T(8,128)S(1)} %bitcast.19, f32[6,8192]{1,0:T(8,128)S(1)} %copy-done.1, f32[6,8192]{1,0:T(8,128)S(1)} %copy-done.2), custom_call_target="tpu_custom_call" | custom-call | tf_op jit(solution)/shard_map/pallas_call | solution.py:32
  12.8 0.0 collective-permute-done.1.refs_2_
  12.9 1.9 %collective-permute-done.2.refs_3_ = f32[24,16]{1,0:T(8,128)S(1)} collective-permute-done((f32[24,16]{1,0:T(8,128)}, f32[24,16]{1,0:T(8,128)S(1)}, u32[]{:S(2)}, u32[]{:S(2)}) %collective-permute-start.2) | collective-permute-done | bytes 1568 | tf_op jit(solution)/shard_map/ppermute | solution.py:53
  14.8 0.0 collective-permute-done.refs_1_
  14.8 0.8 %shard_map.70 = (f32[4,6,3,8,128]{4,3,2,1,0:T(8,128)S(1)}, f32[4,6,2,8,128]{4,3,2,1,0:T(8,128)S(1)}, f32[64,128]{1,0:T(8,128)S(1)}) custom-call(f32[16,6,8,8,128]{4,3,2,1,0:T(8,128)S(1)} %get-tuple-element.43.planes_ref, f32[6,8,8,128]{3,2,1,0:T(8,128)S(1)} %get-tuple-element.44.perturb_ref, f32[24,16]{1,0:T(8,128)S(1)} %copy-done.3, ...), custom_call_target="tpu_custom_call" | custom-call | tf_op jit(solution)/shard_map/pallas_call | solution.py:32
  15.6 2.1 %collective-permute-start.4 = (f32[4,6,3,8,128]{4,3,2,1,0:T(8,128)S(1)}, f32[4,6,3,8,128]{4,3,2,1,0:T(8,128)S(1)}, u32[]{:S(2)}, u32[]{:S(2)}) collective-permute-start(f32[4,6,3,8,128]{4,3,2,1,0:T(8,128)S(1)} %get-tuple-element.49.shared_ref), channel_id=1, source_target_pairs={{0,12},{4,0},{8,4},{12,8},{1,13},{5,1},{9,5},{13,9},{2,14},{6,2},{... | collective-permute-start | bytes 884744 | tf_op jit(solution)/shard_map/ppermute | solution.py:68
  17.7 0.0 collective-permute-start.3
  17.7 0.0 collective-permute-start.8
  17.7 3.8 %collective-permute-start.7 = (f32[4,6,2,8,128]{4,3,2,1,0:T(8,128)S(1)}, f32[4,6,2,8,128]{4,3,2,1,0:T(8,128)S(1)}, u32[]{:S(2)}, u32[]{:S(2)}) collective-permute-start(f32[4,6,2,8,128]{4,3,2,1,0:T(8,128)S(1)} %get-tuple-element.50.rest_ref), channel_id=1, source_target_pairs={{0,12},{4,0},{8,4},{12,8},{1,13},{5,1},{9,5},{13,9},{2,14},{6,2},{... | collective-permute-start | bytes 589832 | tf_op jit(solution)/shard_map/ppermute | solution.py:68
  22.2 0.0 copy-done.4
  22.2 6.9 %shard_map.71 = (f32[4,6,8,8,128]{4,3,2,1,0:T(8,128)S(1)}, f32[4,6,8,8,128]{4,3,2,1,0:T(8,128)S(1)}, f32[4,6,8,8,128]{4,3,2,1,0:T(8,128)S(1)}, f32[16,16,128]{2,...) custom-call(f32[1]{0:T(128)S(6)} %copy.8.omega_ref, f32[4]{0:T(128)S(1)} %copy-done.4, ...), custom_call_target="tpu_custom_call" | custom-call | tf_op jit(solution)/shard_map/pallas_call | solution.py:32
  29.1 5.3 %collective-permute-done.4.after_ref = f32[4,6,3,8,128]{4,3,2,1,0:T(8,128)S(1)} collective-permute-done((f32[4,6,3,8,128]{4,3,2,1,0:T(8,128)S(1)}, f32[4,6,3,8,128]{4,3,2,1,0:T(8,128)S(1)}, u32[]{:S(2)}, u32[]{:S(2)}) %collective-permute-start.4) | collective-permute-done | bytes 294944 | tf_op jit(solution)/shard_map/ppermute | solution.py:68
  34.4 0.0 collective-permute-done.3.before_ref
  34.4 0.1 shard_map.72
  34.5 1.6 %collective-permute-start.5 = (f32[2,6,3,8,128]{4,3,2,1,0:T(8,128)S(1)}, f32[2,6,3,8,128]{4,3,2,1,0:T(8,128)S(1)}, u32[]{:S(2)}, u32[]{:S(2)}) collective-permute-start(f32[2,6,3,8,128]{4,3,2,1,0:T(8,128)S(1)} %get-tuple-element.56.refs_0_), channel_id=1, source_target_pairs={{0,16},{16,0},{1,17},{17,1},{2,18},{18,2},{3,19},{19,3},{4,20},{20... | collective-permute-start | bytes 442376 | tf_op jit(solution)/shard_map/ppermute | solution.py:689
  36.1 0.5 collective-permute-start.6
  36.6 0.5 shard_map.73
  37.1 2.6 %collective-permute-done.5.refs_0_ = f32[2,6,3,8,128]{4,3,2,1,0:T(8,128)S(1)} collective-permute-done((f32[2,6,3,8,128]{4,3,2,1,0:T(8,128)S(1)}, f32[2,6,3,8,128]{4,3,2,1,0:T(8,128)S(1)}, u32[]{:S(2)}, u32[]{:S(2)}) %collective-permute-start.5) | collective-permute-done | bytes 147488 | tf_op jit(solution)/shard_map/ppermute | solution.py:689
  39.7 1.6 %collective-permute-done.6.refs_1_ = f32[2,6,3,8,128]{4,3,2,1,0:T(8,128)S(1)} collective-permute-done((f32[2,6,3,8,128]{4,3,2,1,0:T(8,128)S(1)}, f32[2,6,3,8,128]{4,3,2,1,0:T(8,128)S(1)}, u32[]{:S(2)}, u32[]{:S(2)}) %collective-permute-start.6) | collective-permute-done | bytes 147488 | tf_op jit(solution)/shard_map/ppermute | solution.py:689
  41.3 0.5 shard_map.74
  41.8 0.0 collective-permute-done.8.before_ref
  41.8 0.0 collective-permute-done.7.after_ref
  41.8 0.6 shard_map.75
  42.4 0.1 collective-permute-start.10
  42.4 2.7 %collective-permute-start.11 = (f32[8,128]{1,0:T(8,128)S(1)}, f32[8,128]{1,0:T(8,128)S(1)}, u32[]{:S(2)}, u32[]{:S(2)}) collective-permute-start(f32[8,128]{1,0:T(8,128)S(1)} %get-tuple-element.67), channel_id=1, source_target_pairs={{0,12},{4,8},{8,4},{12,0},{1,13},{5,9},{9,5},{13,1},{2,14},{6,10},... | collective-permute-start | bytes 12296 | tf_op jit(solution)/shard_map/ppermute | solution.py:53
  45.1 0.8 collective-permute-start.9
  45.9 1.1 %collective-permute-done.10.refs_2_ = f32[8,128]{1,0:T(8,128)S(1)} collective-permute-done((f32[8,128]{1,0:T(8,128)S(1)}, f32[8,128]{1,0:T(8,128)S(1)}, u32[]{:S(2)}, u32[]{:S(2)}) %collective-permute-start.10) | collective-permute-done | bytes 4128 | tf_op jit(solution)/shard_map/ppermute | solution.py:53
  47.0 1.0 %collective-permute-done.11.refs_3_ = f32[8,128]{1,0:T(8,128)S(1)} collective-permute-done((f32[8,128]{1,0:T(8,128)S(1)}, f32[8,128]{1,0:T(8,128)S(1)}, u32[]{:S(2)}, u32[]{:S(2)}) %collective-permute-start.11) | collective-permute-done | bytes 4128 | tf_op jit(solution)/shard_map/ppermute | solution.py:53
  48.0 0.8 collective-permute-done.9.refs_1_
  48.8 0.7 shard_map.76
  49.5 1.9 %collective-permute-start.12 = (f32[2,6,8,8,128]{4,3,2,1,0:T(8,128)S(1)}, f32[2,6,8,8,128]{4,3,2,1,0:T(8,128)S(1)}, u32[]{:S(2)}, u32[]{:S(2)}) collective-permute-start(f32[2,6,8,8,128]{4,3,2,1,0:T(8,128)S(1)} %get-tuple-element.68.refs_0_), channel_id=1, source_target_pairs={{0,12},{4,0},{8,4},{12,8},{1,13},{5,1},{9,5},{13,9},{2,14},{6,2},{... | collective-permute-start | bytes 1179656 | tf_op jit(solution)/shard_map/ppermute | solution.py:68
  51.4 0.7 shard_map.77
  52.1 0.2 collective-permute-start.13
  52.3 5.1 %shard_map.78 = (f32[4,6,8,8,128]{4,3,2,1,0:T(8,128)S(1)}, f32[12,8,128]{2,1,0:T(8,128)S(1)}) custom-call(f32[1]{0:T(128)S(6)} %copy.8.omega_ref, f32[4]{0:T(128)S(1)} %copy-done.4, f32[16,6,8,8,128]{4,3,2,1,0:T(8,128)S(1)} %get-tuple-element.43.planes_ref, f32[6,8,8,128]{3,2,1,0:T(8,128)S(1)} %get-tuple-element.45.potential_ref, ...), custom_call_target="tpu_custom_call" | custom-call | tf_op jit(solution)/shard_map/pallas_call | solution.py:32
  57.4 0.2 collective-permute-done.12.refs_2_
  57.6 4.3 %collective-permute-done.13.refs_3_ = f32[2,6,8,8,128]{4,3,2,1,0:T(8,128)S(1)} collective-permute-done((f32[2,6,8,8,128]{4,3,2,1,0:T(8,128)S(1)}, f32[2,6,8,8,128]{4,3,2,1,0:T(8,128)S(1)}, u32[]{:S(2)}, u32[]{:S(2)}) %collective-permute-start.13) | collective-permute-done | bytes 393248 | tf_op jit(solution)/shard_map/ppermute | solution.py:68
  61.9 0.3 shard_map.79
  62.3 1.7 %collective-permute-start.15 = (f32[8,128]{1,0:T(8,128)S(1)}, f32[8,128]{1,0:T(8,128)S(1)}, u32[]{:S(2)}, u32[]{:S(2)}) collective-permute-start(f32[8,128]{1,0:T(8,128)S(1)} %get-tuple-element.77), channel_id=1, source_target_pairs={{0,8},{4,12},{8,0},{12,4},{1,9},{5,13},{9,1},{13,5},{2,10},{6,14},... | collective-permute-start | bytes 12296 | tf_op jit(solution)/shard_map/ppermute | solution.py:53
  63.9 2.3 %collective-permute-start.16 = (f32[8,128]{1,0:T(8,128)S(1)}, f32[8,128]{1,0:T(8,128)S(1)}, u32[]{:S(2)}, u32[]{:S(2)}) collective-permute-start(f32[8,128]{1,0:T(8,128)S(1)} %get-tuple-element.78), channel_id=1, source_target_pairs={{0,12},{4,8},{8,4},{12,0},{1,13},{5,9},{9,5},{13,1},{2,14},{6,10},... | collective-permute-start | bytes 12296 | tf_op jit(solution)/shard_map/ppermute | solution.py:53
  66.2 0.5 collective-permute-start.14
  66.7 0.1 collective-permute-done.15.refs_2_
  66.8 2.6 %collective-permute-done.16.refs_3_ = f32[8,128]{1,0:T(8,128)S(1)} collective-permute-done((f32[8,128]{1,0:T(8,128)S(1)}, f32[8,128]{1,0:T(8,128)S(1)}, u32[]{:S(2)}, u32[]{:S(2)}) %collective-permute-start.16) | collective-permute-done | bytes 4128 | tf_op jit(solution)/shard_map/ppermute | solution.py:53
  69.3 0.5 collective-permute-done.14.refs_1_
  69.8 0.4 shard_map.80
  70.2 0.1 collective-permute-start.19
  70.3 1.5 %collective-permute-start.18 = (f32[144,128]{1,0:T(8,128)S(1)}, f32[144,128]{1,0:T(8,128)S(1)}, u32[]{:S(2)}, u32[]{:S(2)}) collective-permute-start(f32[144,128]{1,0:T(8,128)S(1)} %get-tuple-element.85), channel_id=1, source_target_pairs={{0,2},{1,3},{2,0},{3,1},{4,6},{5,7},{6,4},{7,5},{8,10},{9,11},{10,... | collective-permute-start | bytes 221192 | tf_op jit(solution)/shard_map/ppermute | solution.py:68
  71.8 1.4 %collective-permute-start.17 = (f32[144,128]{1,0:T(8,128)S(1)}, f32[144,128]{1,0:T(8,128)S(1)}, u32[]{:S(2)}, u32[]{:S(2)}) collective-permute-start(f32[144,128]{1,0:T(8,128)S(1)} %get-tuple-element.86), channel_id=1, source_target_pairs={{0,3},{1,0},{2,1},{3,2},{4,7},{5,4},{6,5},{7,6},{8,11},{9,8},{10,9... | collective-permute-start | bytes 221192 | tf_op jit(solution)/shard_map/ppermute | solution.py:68
  73.2 1.0 %collective-permute-done.19.refs_2_ = f32[144,128]{1,0:T(8,128)S(1)} collective-permute-done((f32[144,128]{1,0:T(8,128)S(1)}, f32[144,128]{1,0:T(8,128)S(1)}, u32[]{:S(2)}, u32[]{:S(2)}) %collective-permute-start.19) | collective-permute-done | bytes 73760 | tf_op jit(solution)/shard_map/ppermute | solution.py:68
  74.2 1.1 %collective-permute-done.18.refs_1_ = f32[144,128]{1,0:T(8,128)S(1)} collective-permute-done((f32[144,128]{1,0:T(8,128)S(1)}, f32[144,128]{1,0:T(8,128)S(1)}, u32[]{:S(2)}, u32[]{:S(2)}) %collective-permute-start.18) | collective-permute-done | bytes 73760 | tf_op jit(solution)/shard_map/ppermute | solution.py:68
  75.3 0.1 collective-permute-done.17.refs_0_
  75.4 0.6 collective-permute-start.20
  76.0 3.3 %collective-permute-start.21 = (f32[48,128]{1,0:T(8,128)S(1)}, f32[48,128]{1,0:T(8,128)S(1)}, u32[]{:S(2)}, u32[]{:S(2)}) collective-permute-start(f32[48,128]{1,0:T(8,128)S(1)} %get-tuple-element.83), channel_id=1, source_target_pairs={{0,12},{4,0},{8,4},{12,8},{1,13},{5,1},{9,5},{13,9},{2,14},{6,2},{... | collective-permute-start | bytes 73736 | tf_op jit(solution)/shard_map/ppermute | solution.py:68
  79.3 1.1 %shard_map.81 = f32[1536,128]{1,0:T(8,128)} custom-call(f32[4,6,8,8,128]{4,3,2,1,0:T(8,128)S(1)} %get-tuple-element.52.source_ref, f32[4,6,8,8,128]{4,3,2,1,0:T(8,128)S(1)} %get-tuple-element.74.residual_ref, f32[8,128]{1,0:T(8,128)S(1)} %get-tuple-element.79.scales_ref), custom_call_target="tpu_custom_call" | custom-call | tf_op jit(solution)/shard_map/pallas_call | solution.py:32
  80.4 1.0 %collective-permute-done.20.before_ref = f32[48,128]{1,0:T(8,128)S(1)} collective-permute-done((f32[48,128]{1,0:T(8,128)S(1)}, f32[48,128]{1,0:T(8,128)S(1)}, u32[]{:S(2)}, u32[]{:S(2)}) %collective-permute-start.20) | collective-permute-done | bytes 24608 | tf_op jit(solution)/shard_map/ppermute | solution.py:68
  81.4 0.0 collective-permute-done.21.after_ref
  81.4 0.9 %shard_map.83 = f32[6,2048]{1,0:T(8,128)} custom-call(f32[144,128]{1,0:T(8,128)S(1)} %get-tuple-element.81.dense_ref, f32[48,128]{1,0:T(8,128)S(1)} %collective-permute-done.20.before_ref, f32[48,128]{1,0:T(8,128)S(1)} %collective-permute-done.21.after_ref), custom_call_target="tpu_custom_call" | custom-call | tf_op jit(solution)/shard_map/pallas_call | solution.py:32
  (7 shorter events, 0.0 us)
Async XLA Ops:
  0.6 10.0 %copy-start.1 = (f32[6,8192]{1,0:T(8,128)S(1)}, f32[6,8192]{1,0:T(8,128)}, u32[]{:S(2)}) copy-start(f32[6,8192]{1,0:T(8,128)} %far_perturb_ref.1) | copy-start | bytes 589828
  0.6 10.0 %copy-start = (f32[16,6,8192]{2,0,1:T(8,128)S(1)}, f32[16,6,8192]{2,0,1:T(8,128)}, u32[]{:S(2)}) copy-start(f32[16,6,8192]{2,0,1:T(8,128)} %param.5) | copy-start | bytes 9437188
  5.0 7.9 %collective-permute-start.1 = (f32[24,16]{1,0:T(8,128)}, f32[24,16]{1,0:T(8,128)S(1)}, u32[]{:S(2)}, u32[]{:S(2)}) collective-permute-start(f32[24,16]{1,0:T(8,128)} %get-tuple-element.47), channel_id=1, source_target_pairs={{0,8},{4,12},{8,0},{12,4},{1,9},{5,13},{9,1},{13,5},{2,10},{6,14},... | collective-permute-start | bytes 4616 | tf_op jit(solution)/shard_map/ppermute | solution.py:53
  9.1 5.7 %collective-permute-start.2 = (f32[24,16]{1,0:T(8,128)}, f32[24,16]{1,0:T(8,128)S(1)}, u32[]{:S(2)}, u32[]{:S(2)}) collective-permute-start(f32[24,16]{1,0:T(8,128)} %get-tuple-element.48), channel_id=1, source_target_pairs={{0,12},{4,8},{8,4},{12,0},{1,13},{5,9},{9,5},{13,1},{2,14},{6,10},... | collective-permute-start | bytes 4616 | tf_op jit(solution)/shard_map/ppermute | solution.py:53
  10.4 4.4 %collective-permute-start = (f32[24,16]{1,0:T(8,128)}, f32[24,16]{1,0:T(8,128)S(1)}, u32[]{:S(2)}, u32[]{:S(2)}) collective-permute-start(f32[24,16]{1,0:T(8,128)} %get-tuple-element.46.refs_0_), channel_id=1, source_target_pairs={{0,4},{4,0},{8,12},{12,8},{1,5},{5,1},{9,13},{13,9},{2,6},{6,2},{1... | collective-permute-start | bytes 4616 | tf_op jit(solution)/shard_map/ppermute | solution.py:53
  10.6 1.0 %copy-start.2 = (f32[6,8192]{1,0:T(8,128)S(1)}, f32[6,8192]{1,0:T(8,128)}, u32[]{:S(2)}) copy-start(f32[6,8192]{1,0:T(8,128)} %potential_ref.1) | copy-start | bytes 589828
  11.6 3.2 %copy-start.3 = (f32[24,16]{1,0:T(8,128)S(1)}, f32[24,16]{1,0:T(8,128)}, u32[]{:S(2)}) copy-start(f32[24,16]{1,0:T(8,128)} %get-tuple-element.46.refs_0_) | copy-start | bytes 4612
  11.6 10.6 %copy-start.4 = (f32[4]{0:T(128)S(1)}, f32[4]{0:T(128)}, u32[]{:S(2)}) copy-start(f32[4]{0:T(128)} %energies_ref.3) | copy-start | bytes 52
  15.6 18.8 %collective-permute-start.4 = (f32[4,6,3,8,128]{4,3,2,1,0:T(8,128)S(1)}, f32[4,6,3,8,128]{4,3,2,1,0:T(8,128)S(1)}, u32[]{:S(2)}, u32[]{:S(2)}) collective-permute-start(f32[4,6,3,8,128]{4,3,2,1,0:T(8,128)S(1)} %get-tuple-element.49.shared_ref), channel_id=1, source_target_pairs={{0,12},{4,0},{8,4},{12,8},{1,13},{5,1},{9,5},{13,9},{2,14},{6,2},{... | collective-permute-start | bytes 884744 | tf_op jit(solution)/shard_map/ppermute | solution.py:68
  17.7 16.7 %collective-permute-start.3 = (f32[4,6,3,8,128]{4,3,2,1,0:T(8,128)S(1)}, f32[4,6,3,8,128]{4,3,2,1,0:T(8,128)S(1)}, u32[]{:S(2)}, u32[]{:S(2)}) collective-permute-start(f32[4,6,3,8,128]{4,3,2,1,0:T(8,128)S(1)} %get-tuple-element.49.shared_ref), channel_id=1, source_target_pairs={{0,4},{4,8},{8,12},{12,0},{1,5},{5,9},{9,13},{13,1},{2,6},{6,10},{... | collective-permute-start | bytes 884744 | tf_op jit(solution)/shard_map/ppermute | solution.py:68
  17.7 24.1 %collective-permute-start.8 = (f32[4,6,2,8,128]{4,3,2,1,0:T(8,128)S(1)}, f32[4,6,2,8,128]{4,3,2,1,0:T(8,128)S(1)}, u32[]{:S(2)}, u32[]{:S(2)}) collective-permute-start(f32[4,6,2,8,128]{4,3,2,1,0:T(8,128)S(1)} %get-tuple-element.50.rest_ref), channel_id=1, source_target_pairs={{0,4},{4,8},{8,12},{12,0},{1,5},{5,9},{9,13},{13,1},{2,6},{6,10},{... | collective-permute-start | bytes 589832 | tf_op jit(solution)/shard_map/ppermute | solution.py:68
  17.7 24.1 %collective-permute-start.7 = (f32[4,6,2,8,128]{4,3,2,1,0:T(8,128)S(1)}, f32[4,6,2,8,128]{4,3,2,1,0:T(8,128)S(1)}, u32[]{:S(2)}, u32[]{:S(2)}) collective-permute-start(f32[4,6,2,8,128]{4,3,2,1,0:T(8,128)S(1)} %get-tuple-element.50.rest_ref), channel_id=1, source_target_pairs={{0,12},{4,0},{8,4},{12,8},{1,13},{5,1},{9,5},{13,9},{2,14},{6,2},{... | collective-permute-start | bytes 589832 | tf_op jit(solution)/shard_map/ppermute | solution.py:68
  34.5 5.2 %collective-permute-start.5 = (f32[2,6,3,8,128]{4,3,2,1,0:T(8,128)S(1)}, f32[2,6,3,8,128]{4,3,2,1,0:T(8,128)S(1)}, u32[]{:S(2)}, u32[]{:S(2)}) collective-permute-start(f32[2,6,3,8,128]{4,3,2,1,0:T(8,128)S(1)} %get-tuple-element.56.refs_0_), channel_id=1, source_target_pairs={{0,16},{16,0},{1,17},{17,1},{2,18},{18,2},{3,19},{19,3},{4,20},{20... | collective-permute-start | bytes 442376 | tf_op jit(solution)/shard_map/ppermute | solution.py:689
  36.1 5.2 %collective-permute-start.6 = (f32[2,6,3,8,128]{4,3,2,1,0:T(8,128)S(1)}, f32[2,6,3,8,128]{4,3,2,1,0:T(8,128)S(1)}, u32[]{:S(2)}, u32[]{:S(2)}) collective-permute-start(f32[2,6,3,8,128]{4,3,2,1,0:T(8,128)S(1)} %get-tuple-element.57.refs_1_), channel_id=1, source_target_pairs={{0,16},{16,0},{1,17},{17,1},{2,18},{18,2},{3,19},{19,3},{4,20},{20... | collective-permute-start | bytes 442376 | tf_op jit(solution)/shard_map/ppermute | solution.py:689
  42.4 4.7 %collective-permute-start.10 = (f32[8,128]{1,0:T(8,128)S(1)}, f32[8,128]{1,0:T(8,128)S(1)}, u32[]{:S(2)}, u32[]{:S(2)}) collective-permute-start(f32[8,128]{1,0:T(8,128)S(1)} %get-tuple-element.66), channel_id=1, source_target_pairs={{0,8},{4,12},{8,0},{12,4},{1,9},{5,13},{9,1},{13,5},{2,10},{6,14},... | collective-permute-start | bytes 12296 | tf_op jit(solution)/shard_map/ppermute | solution.py:53
  42.4 5.6 %collective-permute-start.11 = (f32[8,128]{1,0:T(8,128)S(1)}, f32[8,128]{1,0:T(8,128)S(1)}, u32[]{:S(2)}, u32[]{:S(2)}) collective-permute-start(f32[8,128]{1,0:T(8,128)S(1)} %get-tuple-element.67), channel_id=1, source_target_pairs={{0,12},{4,8},{8,4},{12,0},{1,13},{5,9},{9,5},{13,1},{2,14},{6,10},... | collective-permute-start | bytes 12296 | tf_op jit(solution)/shard_map/ppermute | solution.py:53
  45.1 3.7 %collective-permute-start.9 = (f32[8,128]{1,0:T(8,128)S(1)}, f32[8,128]{1,0:T(8,128)S(1)}, u32[]{:S(2)}, u32[]{:S(2)}) collective-permute-start(f32[8,128]{1,0:T(8,128)S(1)} %get-tuple-element.65.refs_0_), channel_id=1, source_target_pairs={{0,4},{4,0},{8,12},{12,8},{1,5},{5,1},{9,13},{13,9},{2,6},{6,2},{1... | collective-permute-start | bytes 12296 | tf_op jit(solution)/shard_map/ppermute | solution.py:53
  49.5 8.1 %collective-permute-start.12 = (f32[2,6,8,8,128]{4,3,2,1,0:T(8,128)S(1)}, f32[2,6,8,8,128]{4,3,2,1,0:T(8,128)S(1)}, u32[]{:S(2)}, u32[]{:S(2)}) collective-permute-start(f32[2,6,8,8,128]{4,3,2,1,0:T(8,128)S(1)} %get-tuple-element.68.refs_0_), channel_id=1, source_target_pairs={{0,12},{4,0},{8,4},{12,8},{1,13},{5,1},{9,5},{13,9},{2,14},{6,2},{... | collective-permute-start | bytes 1179656 | tf_op jit(solution)/shard_map/ppermute | solution.py:68
  52.1 9.8 %collective-permute-start.13 = (f32[2,6,8,8,128]{4,3,2,1,0:T(8,128)S(1)}, f32[2,6,8,8,128]{4,3,2,1,0:T(8,128)S(1)}, u32[]{:S(2)}, u32[]{:S(2)}) collective-permute-start(f32[2,6,8,8,128]{4,3,2,1,0:T(8,128)S(1)} %get-tuple-element.69.refs_1_), channel_id=1, source_target_pairs={{0,12},{4,0},{8,4},{12,8},{1,13},{5,1},{9,5},{13,9},{2,14},{6,2},{... | collective-permute-start | bytes 1179656 | tf_op jit(solution)/shard_map/ppermute | solution.py:68
  62.3 4.5 %collective-permute-start.15 = (f32[8,128]{1,0:T(8,128)S(1)}, f32[8,128]{1,0:T(8,128)S(1)}, u32[]{:S(2)}, u32[]{:S(2)}) collective-permute-start(f32[8,128]{1,0:T(8,128)S(1)} %get-tuple-element.77), channel_id=1, source_target_pairs={{0,8},{4,12},{8,0},{12,4},{1,9},{5,13},{9,1},{13,5},{2,10},{6,14},... | collective-permute-start | bytes 12296 | tf_op jit(solution)/shard_map/ppermute | solution.py:53
  63.9 5.4 %collective-permute-start.16 = (f32[8,128]{1,0:T(8,128)S(1)}, f32[8,128]{1,0:T(8,128)S(1)}, u32[]{:S(2)}, u32[]{:S(2)}) collective-permute-start(f32[8,128]{1,0:T(8,128)S(1)} %get-tuple-element.78), channel_id=1, source_target_pairs={{0,12},{4,8},{8,4},{12,0},{1,13},{5,9},{9,5},{13,1},{2,14},{6,10},... | collective-permute-start | bytes 12296 | tf_op jit(solution)/shard_map/ppermute | solution.py:53
  66.2 3.6 %collective-permute-start.14 = (f32[8,128]{1,0:T(8,128)S(1)}, f32[8,128]{1,0:T(8,128)S(1)}, u32[]{:S(2)}, u32[]{:S(2)}) collective-permute-start(f32[8,128]{1,0:T(8,128)S(1)} %get-tuple-element.76.refs_0_), channel_id=1, source_target_pairs={{0,4},{4,0},{8,12},{12,8},{1,5},{5,1},{9,13},{13,9},{2,6},{6,2},{1... | collective-permute-start | bytes 12296 | tf_op jit(solution)/shard_map/ppermute | solution.py:53
  70.2 4.0 %collective-permute-start.19 = (f32[144,128]{1,0:T(8,128)S(1)}, f32[144,128]{1,0:T(8,128)S(1)}, u32[]{:S(2)}, u32[]{:S(2)}) collective-permute-start(f32[144,128]{1,0:T(8,128)S(1)} %get-tuple-element.84), channel_id=1, source_target_pairs={{0,1},{1,2},{2,3},{3,0},{4,5},{5,6},{6,7},{7,4},{8,9},{9,10},{10,1... | collective-permute-start | bytes 221192 | tf_op jit(solution)/shard_map/ppermute | solution.py:68
  70.3 5.0 %collective-permute-start.18 = (f32[144,128]{1,0:T(8,128)S(1)}, f32[144,128]{1,0:T(8,128)S(1)}, u32[]{:S(2)}, u32[]{:S(2)}) collective-permute-start(f32[144,128]{1,0:T(8,128)S(1)} %get-tuple-element.85), channel_id=1, source_target_pairs={{0,2},{1,3},{2,0},{3,1},{4,6},{5,7},{6,4},{7,5},{8,10},{9,11},{10,... | collective-permute-start | bytes 221192 | tf_op jit(solution)/shard_map/ppermute | solution.py:68
  71.8 3.6 %collective-permute-start.17 = (f32[144,128]{1,0:T(8,128)S(1)}, f32[144,128]{1,0:T(8,128)S(1)}, u32[]{:S(2)}, u32[]{:S(2)}) collective-permute-start(f32[144,128]{1,0:T(8,128)S(1)} %get-tuple-element.86), channel_id=1, source_target_pairs={{0,3},{1,0},{2,1},{3,2},{4,7},{5,4},{6,5},{7,6},{8,11},{9,8},{10,9... | collective-permute-start | bytes 221192 | tf_op jit(solution)/shard_map/ppermute | solution.py:68
  75.4 5.9 %collective-permute-start.20 = (f32[48,128]{1,0:T(8,128)S(1)}, f32[48,128]{1,0:T(8,128)S(1)}, u32[]{:S(2)}, u32[]{:S(2)}) collective-permute-start(f32[48,128]{1,0:T(8,128)S(1)} %get-tuple-element.82), channel_id=1, source_target_pairs={{0,4},{4,8},{8,12},{12,0},{1,5},{5,9},{9,13},{13,1},{2,6},{6,10},{... | collective-permute-start | bytes 73736 | tf_op jit(solution)/shard_map/ppermute | solution.py:68
  76.0 5.4 %collective-permute-start.21 = (f32[48,128]{1,0:T(8,128)S(1)}, f32[48,128]{1,0:T(8,128)S(1)}, u32[]{:S(2)}, u32[]{:S(2)}) collective-permute-start(f32[48,128]{1,0:T(8,128)S(1)} %get-tuple-element.83), channel_id=1, source_target_pairs={{0,12},{4,0},{8,4},{12,8},{1,13},{5,1},{9,5},{13,9},{2,14},{6,2},{... | collective-permute-start | bytes 73736 | tf_op jit(solution)/shard_map/ppermute | solution.py:68

commit v6 on v5

--- a/solution.py
+++ b/solution.py
@@ -210,7 +210,7 @@
 def inner_kernel(shape, ncell, planes_ref, perturb_ref, *refs):
     norb, layers, group, parts, share = shape
     gram_refs = refs[:parts]
-    shared_ref, rest_ref, coef_ref, lines_ref = refs[parts:]
+    shared_ref, coef_ref, lines_ref = refs[parts:]
     first = lax.axis_index("orb") * group
     overlap, rows = small_matrices((norb, group), ncell, gram_refs, lines_ref)
     for n, (line, again) in enumerate(rows):
@@ -219,15 +219,29 @@
     mine = pl.ds(lax.axis_index("freq") * share, share)
 
     def pick(ref, n, z):
-        return jnp.concatenate([ref[n, z, mine], ref[n, z, 2 * share :]], axis=0)
+        return ref[n, z, mine]
 
     def start(n, z):
-        weight = jnp.concatenate([perturb_ref[z, mine], perturb_ref[z, 2 * share :]], axis=0)
-        return -(weight * pick(planes_ref, first + n, z))
+        return -(perturb_ref[z, mine] * pick(planes_ref, first + n, z))
 
     def finish(n, z, value):
-        shared_ref[n, z] = value[:share]
-        rest_ref[n, z] = value[share:]
+        shared_ref[n, z] = value
+
+    combine(layers, group, norb, planes_ref, coef_ref, start, finish, pick)
+
+
+def alone_kernel(shape, planes_ref, perturb_ref, coef_ref, rest_ref):
+    norb, layers, group, share = shape
+    first = lax.axis_index("orb") * group
+
+    def pick(ref, n, z):
+        return ref[n, z, 2 * share :]
+
+    def start(n, z):
+        return -(perturb_ref[z, 2 * share :] * pick(planes_ref, first + n, z))
+
+    def finish(n, z, value):
+        rest_ref[n, z] = value
 
     combine(layers, group, norb, planes_ref, coef_ref, start, finish, pick)
 
@@ -363,6 +377,7 @@
 
 def other_kernel(shape, share, planes_ref, inner_ref, partial_ref, earlier_ref, *refs):
     norb, layers, group = shape
+    refs = refs[:-3][::-1] + refs[-3:]
     field_ref, sums_ref, acc_ref = refs[-3:]
     each = group // (len(refs) - 3)
     spots = pl.ds(share - lax.axis_index("freq") * share, share)
@@ -650,14 +665,23 @@
     )
     share = 3 * spots // 8
     cells = (SUB, LANES)
-    shared, rest, coefs = call(
+    shared, coefs = call(
         functools.partial(inner_kernel, (norb, layers, group, len(grams), share), ncell),
-        [(group, layers, share) + cells, (group, layers, spots - 2 * share) + cells, flat],
+        [(group, layers, share) + cells, flat],
         [(SUB, norb)],
         0,
         planes,
         perturb_planes,
         *grams,
+    )
+    (rest,) = call(
+        functools.partial(alone_kernel, (norb, layers, group, share)),
+        [(group, layers, spots - 2 * share) + cells],
+        [],
+        0,
+        planes,
+        perturb_planes,
+        coefs,
     )
     inner, source, partial, overlap, along, square = call(
         functools.partial(local_kernel, (norb, layers, group, len(grams), halves, share), ncell),
@@ -708,7 +732,7 @@
         inner,
         partial,
         earlier,
-        *partner,
+        *partner[::-1],
     )
     applied, *sums = call(
         functools.partial(rest_kernel, (norb, layers, group), share),
@@ -726,7 +750,7 @@
         before_rest,
     )
     sums = parts_of(sums, "brick")
-    runs = 1 if group % 2 else 2
+    runs = group
     part = group // runs
     steps = [
         call(

time: 82.4 us -> 81.9 us (level)
  waiting for transfers between devices: 25.1 us -> 21 us
  starting transfers between devices: 30.7 us -> 33.6 us
    ppermute x11 -> x13, waiting for transfers between devices: 13 us -> 8.81 us  [shifted(): lax.ppermute(array, axis, [(i, (i + step) % size) for i in range(size)])]
    ppermute x11 -> x13, starting transfers between devices: 14.9 us -> 18 us  [shifted(): lax.ppermute(array, axis, [(i, (i + step) % size) for i in range(size)])]
    pallas_call x16 -> x19, Pallas kernels: 24 us -> 24.7 us  [call(): pl.pallas_call(kernel, out_shape=[jax.ShapeDtypeStruct(s, f32) for s in o...]
  transfers between devices with their start and end apart: 22 -> 24, of which waited for: 16 -> 15; matrix products, arithmetic and copies ran while one was open for 0% -> 0% of each run, Pallas kernels for 20% -> 21%
where the time goes in v6:
time: 81.9 us; the launch traced here: 81.7 us
  starting transfers between devices  33.6 us (41%)
  Pallas kernels  24.7 us (30%)
  waiting for transfers between devices  21 us (26%)
  between operations  1.49 us (2%)
  local copies, waits for them, and re-layouts  0.98 us (1%)
    pallas_call x19, Pallas kernels, call(): pl.pallas_call(kernel, out_shape=[jax.ShapeDtypeStruct(s, f32) for s in o...  24.7 us
    ppermute x13, starting transfers between devices, shifted(): lax.ppermute(array, axis, [(i, (i + step) % size) for i in range(size)])  18 us
    ppermute x9, starting transfers between devices, parts_of(): lax.ppermute(array, axis, [(i, i ^ k + 1) for i in range(size)])  13.5 us
    ppermute x13, waiting for transfers between devices, shifted(): lax.ppermute(array, axis, [(i, (i + step) % size) for i in range(size)])  8.81 us
    ppermute x9, waiting for transfers between devices, parts_of(): lax.ppermute(array, axis, [(i, i ^ k + 1) for i in range(size)])  7.95 us
    ppermute x2, waiting for transfers between devices, per_device(): partner = [lax.ppermute(halo, 'freq', [(0, 1), (1, 0)]) for halo in halos]  4.22 us
    ppermute x2, starting transfers between devices, per_device(): partner = [lax.ppermute(halo, 'freq', [(0, 1), (1, 0)]) for halo in halos]  2.09 us
  transfers between devices with their start and end apart: 24, of which 15 were waited for; matrix products, arithmetic and copies ran while one was open for 0% of the time, Pallas kernels for 21%

profile of v6, /device:TPU:0, one launch (start us, length us, event | category | flops | bytes accessed | tf_op | source)
XLA Modules:
  0.0 81.7 jit_solution(3700293438601027202)
XLA Ops:
  0.6 4.3 %shard_map.69 = (f32[24,16]{1,0:T(8,128)}, f32[24,16]{1,0:T(8,128)}, f32[24,16]{1,0:T(8,128)}) custom-call(f32[6144,128]{1,0:T(8,128)} %bitcast.18, f32[6,8192]{1,0:T(8,128)} %far_perturb_ref.1), custom_call_target="tpu_custom_call" | custom-call | tf_op jit(solution)/shard_map/pallas_call | solution.py:32
  5.0 4.1 %collective-permute-start.1 = (f32[24,16]{1,0:T(8,128)}, f32[24,16]{1,0:T(8,128)S(1)}, u32[]{:S(2)}, u32[]{:S(2)}) collective-permute-start(f32[24,16]{1,0:T(8,128)} %get-tuple-element.52), channel_id=1, source_target_pairs={{0,8},{4,12},{8,0},{12,4},{1,9},{5,13},{9,1},{13,5},{2,10},{6,14},... | collective-permute-start | bytes 4616 | tf_op jit(solution)/shard_map/ppermute | solution.py:53
  9.1 1.3 %collective-permute-start.2 = (f32[24,16]{1,0:T(8,128)}, f32[24,16]{1,0:T(8,128)S(1)}, u32[]{:S(2)}, u32[]{:S(2)}) collective-permute-start(f32[24,16]{1,0:T(8,128)} %get-tuple-element.53), channel_id=1, source_target_pairs={{0,12},{4,8},{8,4},{12,0},{1,13},{5,9},{9,5},{13,1},{2,14},{6,10},... | collective-permute-start | bytes 4616 | tf_op jit(solution)/shard_map/ppermute | solution.py:53
  10.4 0.2 collective-permute-start
  10.6 0.9 %copy-done.2 = f32[6,8192]{1,0:T(8,128)S(1)} copy-done((f32[6,8192]{1,0:T(8,128)S(1)}, f32[6,8192]{1,0:T(8,128)}, u32[]{:S(2)}) %copy-start.2) | copy-done | bytes 196632
  11.6 1.2 %shard_map.68 = (f32[16,6,8,8,128]{4,3,2,1,0:T(8,128)S(1)}, f32[6,8,8,128]{3,2,1,0:T(8,128)S(1)}, f32[6,8,8,128]{3,2,1,0:T(8,128)S(1)}) custom-call(f32[6144,128]{1,0:T(8,128)S(1)} %bitcast.19, f32[6,8192]{1,0:T(8,128)S(1)} %copy-done.1, f32[6,8192]{1,0:T(8,128)S(1)} %copy-done.2), custom_call_target="tpu_custom_call" | custom-call | tf_op jit(solution)/shard_map/pallas_call | solution.py:32
  12.8 0.0 collective-permute-done.1.refs_2_
  12.9 1.9 %collective-permute-done.2.refs_3_ = f32[24,16]{1,0:T(8,128)S(1)} collective-permute-done((f32[24,16]{1,0:T(8,128)}, f32[24,16]{1,0:T(8,128)S(1)}, u32[]{:S(2)}, u32[]{:S(2)}) %collective-permute-start.2) | collective-permute-done | bytes 1568 | tf_op jit(solution)/shard_map/ppermute | solution.py:53
  14.8 0.0 collective-permute-done.refs_1_
  14.8 0.6 shard_map.70
  15.4 2.1 %collective-permute-start.4 = (f32[4,6,3,8,128]{4,3,2,1,0:T(8,128)S(1)}, f32[4,6,3,8,128]{4,3,2,1,0:T(8,128)S(1)}, u32[]{:S(2)}, u32[]{:S(2)}) collective-permute-start(f32[4,6,3,8,128]{4,3,2,1,0:T(8,128)S(1)} %get-tuple-element.54.shared_ref), channel_id=1, source_target_pairs={{0,12},{4,0},{8,4},{12,8},{1,13},{5,1},{9,5},{13,9},{2,14},{6,2},{... | collective-permute-start | bytes 884744 | tf_op jit(solution)/shard_map/ppermute | solution.py:68
  17.5 0.0 collective-permute-start.3
  17.5 0.3 shard_map.71.rest_ref
  17.8 0.1 collective-permute-start.8
  17.8 3.9 %collective-permute-start.7 = (f32[4,6,2,8,128]{4,3,2,1,0:T(8,128)S(1)}, f32[4,6,2,8,128]{4,3,2,1,0:T(8,128)S(1)}, u32[]{:S(2)}, u32[]{:S(2)}) collective-permute-start(f32[4,6,2,8,128]{4,3,2,1,0:T(8,128)S(1)} %shard_map.71.rest_ref), channel_id=1, source_target_pairs={{0,12},{4,0},{8,4},{12,8},{1,13},{5,1},{9,5},{13,9},{2,14},{6,2},{... | collective-permute-start | bytes 589832 | tf_op jit(solution)/shard_map/ppermute | solution.py:68
  22.4 6.9 %shard_map.72 = (f32[4,6,8,8,128]{4,3,2,1,0:T(8,128)S(1)}, f32[4,6,8,8,128]{4,3,2,1,0:T(8,128)S(1)}, f32[4,6,8,8,128]{4,3,2,1,0:T(8,128)S(1)}, f32[16,16,128]{2,...) custom-call(f32[1]{0:T(128)S(6)} %copy.8.omega_ref, f32[4]{0:T(128)S(1)} %copy-done.4, ...), custom_call_target="tpu_custom_call" | custom-call | tf_op jit(solution)/shard_map/pallas_call | solution.py:32
  29.3 4.9 %collective-permute-done.4.after_ref = f32[4,6,3,8,128]{4,3,2,1,0:T(8,128)S(1)} collective-permute-done((f32[4,6,3,8,128]{4,3,2,1,0:T(8,128)S(1)}, f32[4,6,3,8,128]{4,3,2,1,0:T(8,128)S(1)}, u32[]{:S(2)}, u32[]{:S(2)}) %collective-permute-start.4) | collective-permute-done | bytes 294944 | tf_op jit(solution)/shard_map/ppermute | solution.py:68
  34.1 0.1 shard_map.73
  34.3 1.6 %collective-permute-start.6 = (f32[2,6,3,8,128]{4,3,2,1,0:T(8,128)S(1)}, f32[2,6,3,8,128]{4,3,2,1,0:T(8,128)S(1)}, u32[]{:S(2)}, u32[]{:S(2)}) collective-permute-start(f32[2,6,3,8,128]{4,3,2,1,0:T(8,128)S(1)} %get-tuple-element.60.refs_0_), channel_id=1, source_target_pairs={{0,16},{16,0},{1,17},{17,1},{2,18},{18,2},{3,19},{19,3},{4,20},{20... | collective-permute-start | bytes 442376 | tf_op jit(solution)/shard_map/ppermute | solution.py:713
  35.9 0.5 collective-permute-start.5
  36.4 0.5 shard_map.74
  36.8 2.6 %collective-permute-done.6.refs_1_ = f32[2,6,3,8,128]{4,3,2,1,0:T(8,128)S(1)} collective-permute-done((f32[2,6,3,8,128]{4,3,2,1,0:T(8,128)S(1)}, f32[2,6,3,8,128]{4,3,2,1,0:T(8,128)S(1)}, u32[]{:S(2)}, u32[]{:S(2)}) %collective-permute-start.6) | collective-permute-done | bytes 147488 | tf_op jit(solution)/shard_map/ppermute | solution.py:713
  39.5 1.6 %collective-permute-done.5.refs_0_ = f32[2,6,3,8,128]{4,3,2,1,0:T(8,128)S(1)} collective-permute-done((f32[2,6,3,8,128]{4,3,2,1,0:T(8,128)S(1)}, f32[2,6,3,8,128]{4,3,2,1,0:T(8,128)S(1)}, u32[]{:S(2)}, u32[]{:S(2)}) %collective-permute-start.5) | collective-permute-done | bytes 147488 | tf_op jit(solution)/shard_map/ppermute | solution.py:713
  41.1 0.5 shard_map.75
  41.6 0.0 collective-permute-done.8.before_ref
  41.6 0.5 shard_map.76
  42.2 0.1 collective-permute-start.10
  42.2 2.7 %collective-permute-start.11 = (f32[8,128]{1,0:T(8,128)S(1)}, f32[8,128]{1,0:T(8,128)S(1)}, u32[]{:S(2)}, u32[]{:S(2)}) collective-permute-start(f32[8,128]{1,0:T(8,128)S(1)} %get-tuple-element.71), channel_id=1, source_target_pairs={{0,12},{4,8},{8,4},{12,0},{1,13},{5,9},{9,5},{13,1},{2,14},{6,10},... | collective-permute-start | bytes 12296 | tf_op jit(solution)/shard_map/ppermute | solution.py:53
  44.9 0.8 collective-permute-start.9
  45.7 1.1 %collective-permute-done.10.refs_2_ = f32[8,128]{1,0:T(8,128)S(1)} collective-permute-done((f32[8,128]{1,0:T(8,128)S(1)}, f32[8,128]{1,0:T(8,128)S(1)}, u32[]{:S(2)}, u32[]{:S(2)}) %collective-permute-start.10) | collective-permute-done | bytes 4128 | tf_op jit(solution)/shard_map/ppermute | solution.py:53
  46.8 1.0 %collective-permute-done.11.refs_3_ = f32[8,128]{1,0:T(8,128)S(1)} collective-permute-done((f32[8,128]{1,0:T(8,128)S(1)}, f32[8,128]{1,0:T(8,128)S(1)}, u32[]{:S(2)}, u32[]{:S(2)}) %collective-permute-start.11) | collective-permute-done | bytes 4128 | tf_op jit(solution)/shard_map/ppermute | solution.py:53
  47.8 0.8 %collective-permute-done.9.refs_1_ = f32[8,128]{1,0:T(8,128)S(1)} collective-permute-done((f32[8,128]{1,0:T(8,128)S(1)}, f32[8,128]{1,0:T(8,128)S(1)}, u32[]{:S(2)}, u32[]{:S(2)}) %collective-permute-start.9) | collective-permute-done | bytes 4128 | tf_op jit(solution)/shard_map/ppermute | solution.py:53
  48.6 0.4 shard_map.80
  49.1 1.9 %collective-permute-start.15 = (f32[1,6,8,8,128]{4,3,2,1,0:T(8,128)S(1)}, f32[1,6,8,8,128]{4,3,2,1,0:T(8,128)S(1)}, u32[]{:S(2)}, u32[]{:S(2)}) collective-permute-start(f32[1,6,8,8,128]{4,3,2,1,0:T(8,128)S(1)} %get-tuple-element.75.refs_3_), channel_id=1, source_target_pairs={{0,12},{4,0},{8,4},{12,8},{1,13},{5,1},{9,5},{13,9},{2,14},{6,2},{... | collective-permute-start | bytes 589832 | tf_op jit(solution)/shard_map/ppermute | solution.py:68
  50.9 0.4 shard_map.79
  51.4 0.2 collective-permute-start.14
  51.6 0.4 shard_map.77
  52.0 1.8 %collective-permute-start.12 = (f32[1,6,8,8,128]{4,3,2,1,0:T(8,128)S(1)}, f32[1,6,8,8,128]{4,3,2,1,0:T(8,128)S(1)}, u32[]{:S(2)}, u32[]{:S(2)}) collective-permute-start(f32[1,6,8,8,128]{4,3,2,1,0:T(8,128)S(1)} %get-tuple-element.72.refs_0_), channel_id=1, source_target_pairs={{0,12},{4,0},{8,4},{12,8},{1,13},{5,1},{9,5},{13,9},{2,14},{6,2},{... | collective-permute-start | bytes 589832 | tf_op jit(solution)/shard_map/ppermute | solution.py:68
  53.8 0.4 shard_map.78
  54.2 1.3 %collective-permute-start.13 = (f32[1,6,8,8,128]{4,3,2,1,0:T(8,128)S(1)}, f32[1,6,8,8,128]{4,3,2,1,0:T(8,128)S(1)}, u32[]{:S(2)}, u32[]{:S(2)}) collective-permute-start(f32[1,6,8,8,128]{4,3,2,1,0:T(8,128)S(1)} %get-tuple-element.73.refs_1_), channel_id=1, source_target_pairs={{0,12},{4,0},{8,4},{12,8},{1,13},{5,1},{9,5},{13,9},{2,14},{6,2},{... | collective-permute-start | bytes 589832 | tf_op jit(solution)/shard_map/ppermute | solution.py:68
  55.5 5.3 %shard_map.81 = (f32[4,6,8,8,128]{4,3,2,1,0:T(8,128)S(1)}, f32[12,8,128]{2,1,0:T(8,128)S(1)}) custom-call(f32[1]{0:T(128)S(6)} %copy.8.omega_ref, f32[4]{0:T(128)S(1)} %copy-done.4, f32[16,6,8,8,128]{4,3,2,1,0:T(8,128)S(1)} %get-tuple-element.48.planes_ref, f32[6,8,8,128]{3,2,1,0:T(8,128)S(1)} %get-tuple-element.50.potential_ref, ...), custom_call_target="tpu_custom_call" | custom-call | tf_op jit(solution)/shard_map/pallas_call | solution.py:32
  60.9 0.0 collective-permute-done.15.refs_7_
  60.9 0.0 collective-permute-done.14.refs_6_
  60.9 0.7 collective-permute-done.13.refs_5_
  61.6 0.3 shard_map.82
  61.9 1.5 %collective-permute-start.17 = (f32[8,128]{1,0:T(8,128)S(1)}, f32[8,128]{1,0:T(8,128)S(1)}, u32[]{:S(2)}, u32[]{:S(2)}) collective-permute-start(f32[8,128]{1,0:T(8,128)S(1)} %get-tuple-element.87), channel_id=1, source_target_pairs={{0,8},{4,12},{8,0},{12,4},{1,9},{5,13},{9,1},{13,5},{2,10},{6,14},... | collective-permute-start | bytes 12296 | tf_op jit(solution)/shard_map/ppermute | solution.py:53
  63.4 2.3 %collective-permute-start.18 = (f32[8,128]{1,0:T(8,128)S(1)}, f32[8,128]{1,0:T(8,128)S(1)}, u32[]{:S(2)}, u32[]{:S(2)}) collective-permute-start(f32[8,128]{1,0:T(8,128)S(1)} %get-tuple-element.88), channel_id=1, source_target_pairs={{0,12},{4,8},{8,4},{12,0},{1,13},{5,9},{9,5},{13,1},{2,14},{6,10},... | collective-permute-start | bytes 12296 | tf_op jit(solution)/shard_map/ppermute | solution.py:53
  65.7 0.5 collective-permute-start.16
  66.2 0.2 collective-permute-done.17.refs_2_
  66.5 2.4 %collective-permute-done.18.refs_3_ = f32[8,128]{1,0:T(8,128)S(1)} collective-permute-done((f32[8,128]{1,0:T(8,128)S(1)}, f32[8,128]{1,0:T(8,128)S(1)}, u32[]{:S(2)}, u32[]{:S(2)}) %collective-permute-start.18) | collective-permute-done | bytes 4128 | tf_op jit(solution)/shard_map/ppermute | solution.py:53
  68.8 0.5 collective-permute-done.16.refs_1_
  69.3 0.3 shard_map.83
  69.7 0.1 collective-permute-start.21
  69.8 1.5 %collective-permute-start.20 = (f32[144,128]{1,0:T(8,128)S(1)}, f32[144,128]{1,0:T(8,128)S(1)}, u32[]{:S(2)}, u32[]{:S(2)}) collective-permute-start(f32[144,128]{1,0:T(8,128)S(1)} %get-tuple-element.95), channel_id=1, source_target_pairs={{0,2},{1,3},{2,0},{3,1},{4,6},{5,7},{6,4},{7,5},{8,10},{9,11},{10,... | collective-permute-start | bytes 221192 | tf_op jit(solution)/shard_map/ppermute | solution.py:68
  71.3 1.4 %collective-permute-start.19 = (f32[144,128]{1,0:T(8,128)S(1)}, f32[144,128]{1,0:T(8,128)S(1)}, u32[]{:S(2)}, u32[]{:S(2)}) collective-permute-start(f32[144,128]{1,0:T(8,128)S(1)} %get-tuple-element.96), channel_id=1, source_target_pairs={{0,3},{1,0},{2,1},{3,2},{4,7},{5,4},{6,5},{7,6},{8,11},{9,8},{10,9... | collective-permute-start | bytes 221192 | tf_op jit(solution)/shard_map/ppermute | solution.py:68
  72.7 1.0 %collective-permute-done.21.refs_2_ = f32[144,128]{1,0:T(8,128)S(1)} collective-permute-done((f32[144,128]{1,0:T(8,128)S(1)}, f32[144,128]{1,0:T(8,128)S(1)}, u32[]{:S(2)}, u32[]{:S(2)}) %collective-permute-start.21) | collective-permute-done | bytes 73760 | tf_op jit(solution)/shard_map/ppermute | solution.py:68
  73.7 1.1 %collective-permute-done.20.refs_1_ = f32[144,128]{1,0:T(8,128)S(1)} collective-permute-done((f32[144,128]{1,0:T(8,128)S(1)}, f32[144,128]{1,0:T(8,128)S(1)}, u32[]{:S(2)}, u32[]{:S(2)}) %collective-permute-start.20) | collective-permute-done | bytes 73760 | tf_op jit(solution)/shard_map/ppermute | solution.py:68
  74.8 0.1 collective-permute-done.19.refs_0_
  74.9 0.6 collective-permute-start.22
  75.5 3.3 %collective-permute-start.23 = (f32[48,128]{1,0:T(8,128)S(1)}, f32[48,128]{1,0:T(8,128)S(1)}, u32[]{:S(2)}, u32[]{:S(2)}) collective-permute-start(f32[48,128]{1,0:T(8,128)S(1)} %get-tuple-element.93), channel_id=1, source_target_pairs={{0,12},{4,0},{8,4},{12,8},{1,13},{5,1},{9,5},{13,9},{2,14},{6,2},{... | collective-permute-start | bytes 73736 | tf_op jit(solution)/shard_map/ppermute | solution.py:68
  78.8 1.1 %shard_map.84 = f32[1536,128]{1,0:T(8,128)} custom-call(f32[4,6,8,8,128]{4,3,2,1,0:T(8,128)S(1)} %get-tuple-element.56.source_ref, f32[4,6,8,8,128]{4,3,2,1,0:T(8,128)S(1)} %get-tuple-element.84.residual_ref, f32[8,128]{1,0:T(8,128)S(1)} %get-tuple-element.89.scales_ref), custom_call_target="tpu_custom_call" | custom-call | tf_op jit(solution)/shard_map/pallas_call | solution.py:32
  79.9 1.0 %collective-permute-done.22.before_ref = f32[48,128]{1,0:T(8,128)S(1)} collective-permute-done((f32[48,128]{1,0:T(8,128)S(1)}, f32[48,128]{1,0:T(8,128)S(1)}, u32[]{:S(2)}, u32[]{:S(2)}) %collective-permute-start.22) | collective-permute-done | bytes 24608 | tf_op jit(solution)/shard_map/ppermute | solution.py:68
  80.9 0.0 collective-permute-done.23.after_ref
  80.9 0.9 %shard_map.86 = f32[6,2048]{1,0:T(8,128)} custom-call(f32[144,128]{1,0:T(8,128)S(1)} %get-tuple-element.91.dense_ref, f32[48,128]{1,0:T(8,128)S(1)} %collective-permute-done.22.before_ref, f32[48,128]{1,0:T(8,128)S(1)} %collective-permute-done.23.after_ref), custom_call_target="tpu_custom_call" | custom-call | tf_op jit(solution)/shard_map/pallas_call | solution.py:32
  (14 shorter events, 0.1 us)
Async XLA Ops:
  0.6 10.0 %copy-start.1 = (f32[6,8192]{1,0:T(8,128)S(1)}, f32[6,8192]{1,0:T(8,128)}, u32[]{:S(2)}) copy-start(f32[6,8192]{1,0:T(8,128)} %far_perturb_ref.1) | copy-start | bytes 589828
  0.6 10.0 %copy-start = (f32[16,6,8192]{2,0,1:T(8,128)S(1)}, f32[16,6,8192]{2,0,1:T(8,128)}, u32[]{:S(2)}) copy-start(f32[16,6,8192]{2,0,1:T(8,128)} %param.5) | copy-start | bytes 9437188
  5.0 7.9 %collective-permute-start.1 = (f32[24,16]{1,0:T(8,128)}, f32[24,16]{1,0:T(8,128)S(1)}, u32[]{:S(2)}, u32[]{:S(2)}) collective-permute-start(f32[24,16]{1,0:T(8,128)} %get-tuple-element.52), channel_id=1, source_target_pairs={{0,8},{4,12},{8,0},{12,4},{1,9},{5,13},{9,1},{13,5},{2,10},{6,14},... | collective-permute-start | bytes 4616 | tf_op jit(solution)/shard_map/ppermute | solution.py:53
  9.1 5.7 %collective-permute-start.2 = (f32[24,16]{1,0:T(8,128)}, f32[24,16]{1,0:T(8,128)S(1)}, u32[]{:S(2)}, u32[]{:S(2)}) collective-permute-start(f32[24,16]{1,0:T(8,128)} %get-tuple-element.53), channel_id=1, source_target_pairs={{0,12},{4,8},{8,4},{12,0},{1,13},{5,9},{9,5},{13,1},{2,14},{6,10},... | collective-permute-start | bytes 4616 | tf_op jit(solution)/shard_map/ppermute | solution.py:53
  10.4 4.4 %collective-permute-start = (f32[24,16]{1,0:T(8,128)}, f32[24,16]{1,0:T(8,128)S(1)}, u32[]{:S(2)}, u32[]{:S(2)}) collective-permute-start(f32[24,16]{1,0:T(8,128)} %get-tuple-element.51.refs_0_), channel_id=1, source_target_pairs={{0,4},{4,0},{8,12},{12,8},{1,5},{5,1},{9,13},{13,9},{2,6},{6,2},{1... | collective-permute-start | bytes 4616 | tf_op jit(solution)/shard_map/ppermute | solution.py:53
  10.6 1.0 %copy-start.2 = (f32[6,8192]{1,0:T(8,128)S(1)}, f32[6,8192]{1,0:T(8,128)}, u32[]{:S(2)}) copy-start(f32[6,8192]{1,0:T(8,128)} %potential_ref.1) | copy-start | bytes 589828
  11.6 3.2 %copy-start.3 = (f32[24,16]{1,0:T(8,128)S(1)}, f32[24,16]{1,0:T(8,128)}, u32[]{:S(2)}) copy-start(f32[24,16]{1,0:T(8,128)} %get-tuple-element.51.refs_0_) | copy-start | bytes 4612
  14.8 7.6 %copy-start.4 = (f32[4]{0:T(128)S(1)}, f32[4]{0:T(128)}, u32[]{:S(2)}) copy-start(f32[4]{0:T(128)} %energies_ref.3) | copy-start | bytes 52
  15.4 18.8 %collective-permute-start.4 = (f32[4,6,3,8,128]{4,3,2,1,0:T(8,128)S(1)}, f32[4,6,3,8,128]{4,3,2,1,0:T(8,128)S(1)}, u32[]{:S(2)}, u32[]{:S(2)}) collective-permute-start(f32[4,6,3,8,128]{4,3,2,1,0:T(8,128)S(1)} %get-tuple-element.54.shared_ref), channel_id=1, source_target_pairs={{0,12},{4,0},{8,4},{12,8},{1,13},{5,1},{9,5},{13,9},{2,14},{6,2},{... | collective-permute-start | bytes 884744 | tf_op jit(solution)/shard_map/ppermute | solution.py:68
  17.5 16.7 %collective-permute-start.3 = (f32[4,6,3,8,128]{4,3,2,1,0:T(8,128)S(1)}, f32[4,6,3,8,128]{4,3,2,1,0:T(8,128)S(1)}, u32[]{:S(2)}, u32[]{:S(2)}) collective-permute-start(f32[4,6,3,8,128]{4,3,2,1,0:T(8,128)S(1)} %get-tuple-element.54.shared_ref), channel_id=1, source_target_pairs={{0,4},{4,8},{8,12},{12,0},{1,5},{5,9},{9,13},{13,1},{2,6},{6,10},{... | collective-permute-start | bytes 884744 | tf_op jit(solution)/shard_map/ppermute | solution.py:68
  17.8 23.8 %collective-permute-start.8 = (f32[4,6,2,8,128]{4,3,2,1,0:T(8,128)S(1)}, f32[4,6,2,8,128]{4,3,2,1,0:T(8,128)S(1)}, u32[]{:S(2)}, u32[]{:S(2)}) collective-permute-start(f32[4,6,2,8,128]{4,3,2,1,0:T(8,128)S(1)} %shard_map.71.rest_ref), channel_id=1, source_target_pairs={{0,4},{4,8},{8,12},{12,0},{1,5},{5,9},{9,13},{13,1},{2,6},{6,10},{... | collective-permute-start | bytes 589832 | tf_op jit(solution)/shard_map/ppermute | solution.py:68
  17.8 23.8 %collective-permute-start.7 = (f32[4,6,2,8,128]{4,3,2,1,0:T(8,128)S(1)}, f32[4,6,2,8,128]{4,3,2,1,0:T(8,128)S(1)}, u32[]{:S(2)}, u32[]{:S(2)}) collective-permute-start(f32[4,6,2,8,128]{4,3,2,1,0:T(8,128)S(1)} %shard_map.71.rest_ref), channel_id=1, source_target_pairs={{0,12},{4,0},{8,4},{12,8},{1,13},{5,1},{9,5},{13,9},{2,14},{6,2},{... | collective-permute-start | bytes 589832 | tf_op jit(solution)/shard_map/ppermute | solution.py:68
  34.3 5.2 %collective-permute-start.6 = (f32[2,6,3,8,128]{4,3,2,1,0:T(8,128)S(1)}, f32[2,6,3,8,128]{4,3,2,1,0:T(8,128)S(1)}, u32[]{:S(2)}, u32[]{:S(2)}) collective-permute-start(f32[2,6,3,8,128]{4,3,2,1,0:T(8,128)S(1)} %get-tuple-element.60.refs_0_), channel_id=1, source_target_pairs={{0,16},{16,0},{1,17},{17,1},{2,18},{18,2},{3,19},{19,3},{4,20},{20... | collective-permute-start | bytes 442376 | tf_op jit(solution)/shard_map/ppermute | solution.py:713
  35.9 5.2 %collective-permute-start.5 = (f32[2,6,3,8,128]{4,3,2,1,0:T(8,128)S(1)}, f32[2,6,3,8,128]{4,3,2,1,0:T(8,128)S(1)}, u32[]{:S(2)}, u32[]{:S(2)}) collective-permute-start(f32[2,6,3,8,128]{4,3,2,1,0:T(8,128)S(1)} %get-tuple-element.61.refs_1_), channel_id=1, source_target_pairs={{0,16},{16,0},{1,17},{17,1},{2,18},{18,2},{3,19},{19,3},{4,20},{20... | collective-permute-start | bytes 442376 | tf_op jit(solution)/shard_map/ppermute | solution.py:713
  42.2 4.7 %collective-permute-start.10 = (f32[8,128]{1,0:T(8,128)S(1)}, f32[8,128]{1,0:T(8,128)S(1)}, u32[]{:S(2)}, u32[]{:S(2)}) collective-permute-start(f32[8,128]{1,0:T(8,128)S(1)} %get-tuple-element.70), channel_id=1, source_target_pairs={{0,8},{4,12},{8,0},{12,4},{1,9},{5,13},{9,1},{13,5},{2,10},{6,14},... | collective-permute-start | bytes 12296 | tf_op jit(solution)/shard_map/ppermute | solution.py:53
  42.2 5.6 %collective-permute-start.11 = (f32[8,128]{1,0:T(8,128)S(1)}, f32[8,128]{1,0:T(8,128)S(1)}, u32[]{:S(2)}, u32[]{:S(2)}) collective-permute-start(f32[8,128]{1,0:T(8,128)S(1)} %get-tuple-element.71), channel_id=1, source_target_pairs={{0,12},{4,8},{8,4},{12,0},{1,13},{5,9},{9,5},{13,1},{2,14},{6,10},... | collective-permute-start | bytes 12296 | tf_op jit(solution)/shard_map/ppermute | solution.py:53
  44.9 3.7 %collective-permute-start.9 = (f32[8,128]{1,0:T(8,128)S(1)}, f32[8,128]{1,0:T(8,128)S(1)}, u32[]{:S(2)}, u32[]{:S(2)}) collective-permute-start(f32[8,128]{1,0:T(8,128)S(1)} %get-tuple-element.69.refs_0_), channel_id=1, source_target_pairs={{0,4},{4,0},{8,12},{12,8},{1,5},{5,1},{9,13},{13,9},{2,6},{6,2},{1... | collective-permute-start | bytes 12296 | tf_op jit(solution)/shard_map/ppermute | solution.py:53
  49.1 11.8 %collective-permute-start.15 = (f32[1,6,8,8,128]{4,3,2,1,0:T(8,128)S(1)}, f32[1,6,8,8,128]{4,3,2,1,0:T(8,128)S(1)}, u32[]{:S(2)}, u32[]{:S(2)}) collective-permute-start(f32[1,6,8,8,128]{4,3,2,1,0:T(8,128)S(1)} %get-tuple-element.75.refs_3_), channel_id=1, source_target_pairs={{0,12},{4,0},{8,4},{12,8},{1,13},{5,1},{9,5},{13,9},{2,14},{6,2},{... | collective-permute-start | bytes 589832 | tf_op jit(solution)/shard_map/ppermute | solution.py:68
  51.4 9.5 %collective-permute-start.14 = (f32[1,6,8,8,128]{4,3,2,1,0:T(8,128)S(1)}, f32[1,6,8,8,128]{4,3,2,1,0:T(8,128)S(1)}, u32[]{:S(2)}, u32[]{:S(2)}) collective-permute-start(f32[1,6,8,8,128]{4,3,2,1,0:T(8,128)S(1)} %get-tuple-element.74.refs_2_), channel_id=1, source_target_pairs={{0,12},{4,0},{8,4},{12,8},{1,13},{5,1},{9,5},{13,9},{2,14},{6,2},{... | collective-permute-start | bytes 589832 | tf_op jit(solution)/shard_map/ppermute | solution.py:68
  52.0 8.9 %collective-permute-start.12 = (f32[1,6,8,8,128]{4,3,2,1,0:T(8,128)S(1)}, f32[1,6,8,8,128]{4,3,2,1,0:T(8,128)S(1)}, u32[]{:S(2)}, u32[]{:S(2)}) collective-permute-start(f32[1,6,8,8,128]{4,3,2,1,0:T(8,128)S(1)} %get-tuple-element.72.refs_0_), channel_id=1, source_target_pairs={{0,12},{4,0},{8,4},{12,8},{1,13},{5,1},{9,5},{13,9},{2,14},{6,2},{... | collective-permute-start | bytes 589832 | tf_op jit(solution)/shard_map/ppermute | solution.py:68
  54.2 7.4 %collective-permute-start.13 = (f32[1,6,8,8,128]{4,3,2,1,0:T(8,128)S(1)}, f32[1,6,8,8,128]{4,3,2,1,0:T(8,128)S(1)}, u32[]{:S(2)}, u32[]{:S(2)}) collective-permute-start(f32[1,6,8,8,128]{4,3,2,1,0:T(8,128)S(1)} %get-tuple-element.73.refs_1_), channel_id=1, source_target_pairs={{0,12},{4,0},{8,4},{12,8},{1,13},{5,1},{9,5},{13,9},{2,14},{6,2},{... | collective-permute-start | bytes 589832 | tf_op jit(solution)/shard_map/ppermute | solution.py:68
  61.9 4.5 %collective-permute-start.17 = (f32[8,128]{1,0:T(8,128)S(1)}, f32[8,128]{1,0:T(8,128)S(1)}, u32[]{:S(2)}, u32[]{:S(2)}) collective-permute-start(f32[8,128]{1,0:T(8,128)S(1)} %get-tuple-element.87), channel_id=1, source_target_pairs={{0,8},{4,12},{8,0},{12,4},{1,9},{5,13},{9,1},{13,5},{2,10},{6,14},... | collective-permute-start | bytes 12296 | tf_op jit(solution)/shard_map/ppermute | solution.py:53
  63.4 5.4 %collective-permute-start.18 = (f32[8,128]{1,0:T(8,128)S(1)}, f32[8,128]{1,0:T(8,128)S(1)}, u32[]{:S(2)}, u32[]{:S(2)}) collective-permute-start(f32[8,128]{1,0:T(8,128)S(1)} %get-tuple-element.88), channel_id=1, source_target_pairs={{0,12},{4,8},{8,4},{12,0},{1,13},{5,9},{9,5},{13,1},{2,14},{6,10},... | collective-permute-start | bytes 12296 | tf_op jit(solution)/shard_map/ppermute | solution.py:53
  65.7 3.6 %collective-permute-start.16 = (f32[8,128]{1,0:T(8,128)S(1)}, f32[8,128]{1,0:T(8,128)S(1)}, u32[]{:S(2)}, u32[]{:S(2)}) collective-permute-start(f32[8,128]{1,0:T(8,128)S(1)} %get-tuple-element.86.refs_0_), channel_id=1, source_target_pairs={{0,4},{4,0},{8,12},{12,8},{1,5},{5,1},{9,13},{13,9},{2,6},{6,2},{1... | collective-permute-start | bytes 12296 | tf_op jit(solution)/shard_map/ppermute | solution.py:53
  69.7 4.0 %collective-permute-start.21 = (f32[144,128]{1,0:T(8,128)S(1)}, f32[144,128]{1,0:T(8,128)S(1)}, u32[]{:S(2)}, u32[]{:S(2)}) collective-permute-start(f32[144,128]{1,0:T(8,128)S(1)} %get-tuple-element.94), channel_id=1, source_target_pairs={{0,1},{1,2},{2,3},{3,0},{4,5},{5,6},{6,7},{7,4},{8,9},{9,10},{10,1... | collective-permute-start | bytes 221192 | tf_op jit(solution)/shard_map/ppermute | solution.py:68
  69.8 5.0 %collective-permute-start.20 = (f32[144,128]{1,0:T(8,128)S(1)}, f32[144,128]{1,0:T(8,128)S(1)}, u32[]{:S(2)}, u32[]{:S(2)}) collective-permute-start(f32[144,128]{1,0:T(8,128)S(1)} %get-tuple-element.95), channel_id=1, source_target_pairs={{0,2},{1,3},{2,0},{3,1},{4,6},{5,7},{6,4},{7,5},{8,10},{9,11},{10,... | collective-permute-start | bytes 221192 | tf_op jit(solution)/shard_map/ppermute | solution.py:68
  71.3 3.6 %collective-permute-start.19 = (f32[144,128]{1,0:T(8,128)S(1)}, f32[144,128]{1,0:T(8,128)S(1)}, u32[]{:S(2)}, u32[]{:S(2)}) collective-permute-start(f32[144,128]{1,0:T(8,128)S(1)} %get-tuple-element.96), channel_id=1, source_target_pairs={{0,3},{1,0},{2,1},{3,2},{4,7},{5,4},{6,5},{7,6},{8,11},{9,8},{10,9... | collective-permute-start | bytes 221192 | tf_op jit(solution)/shard_map/ppermute | solution.py:68
  74.9 5.9 %collective-permute-start.22 = (f32[48,128]{1,0:T(8,128)S(1)}, f32[48,128]{1,0:T(8,128)S(1)}, u32[]{:S(2)}, u32[]{:S(2)}) collective-permute-start(f32[48,128]{1,0:T(8,128)S(1)} %get-tuple-element.92), channel_id=1, source_target_pairs={{0,4},{4,8},{8,12},{12,0},{1,5},{5,9},{9,13},{13,1},{2,6},{6,10},{... | collective-permute-start | bytes 73736 | tf_op jit(solution)/shard_map/ppermute | solution.py:68
  75.5 5.4 %collective-permute-start.23 = (f32[48,128]{1,0:T(8,128)S(1)}, f32[48,128]{1,0:T(8,128)S(1)}, u32[]{:S(2)}, u32[]{:S(2)}) collective-permute-start(f32[48,128]{1,0:T(8,128)S(1)} %get-tuple-element.93), channel_id=1, source_target_pairs={{0,12},{4,0},{8,4},{12,8},{1,13},{5,1},{9,5},{13,9},{2,14},{6,2},{... | collective-permute-start | bytes 73736 | tf_op jit(solution)/shard_map/ppermute | solution.py:68

commit v7 on v6

--- a/solution.py
+++ b/solution.py
@@ -101,7 +101,7 @@
     norb, layers, halves, group = shape
     groups = norb // SUB
     tiles = NY * halves
-    step = 16
+    step = 32
     ahead = 3
     size = norb * tiles
     own = lax.axis_index("orb") * group // SUB

time: 81.9 us -> 81.9 us (level)
  no operation moved by 1% of the time
where the time goes in v7:
time: 81.9 us; the launch traced here: 81.7 us
  starting transfers between devices  33.6 us (41%)
  Pallas kernels  24.7 us (30%)
  waiting for transfers between devices  21 us (26%)
  between operations  1.49 us (2%)
  local copies, waits for them, and re-layouts  0.98 us (1%)
    pallas_call x19, Pallas kernels, call(): pl.pallas_call(kernel, out_shape=[jax.ShapeDtypeStruct(s, f32) for s in o...  24.7 us
    ppermute x13, starting transfers between devices, shifted(): lax.ppermute(array, axis, [(i, (i + step) % size) for i in range(size)])  18 us
    ppermute x9, starting transfers between devices, parts_of(): lax.ppermute(array, axis, [(i, i ^ k + 1) for i in range(size)])  13.5 us
    ppermute x13, waiting for transfers between devices, shifted(): lax.ppermute(array, axis, [(i, (i + step) % size) for i in range(size)])  8.81 us
    ppermute x9, waiting for transfers between devices, parts_of(): lax.ppermute(array, axis, [(i, i ^ k + 1) for i in range(size)])  7.95 us
    ppermute x2, waiting for transfers between devices, per_device(): partner = [lax.ppermute(halo, 'freq', [(0, 1), (1, 0)]) for halo in halos]  4.22 us
    ppermute x2, starting transfers between devices, per_device(): partner = [lax.ppermute(halo, 'freq', [(0, 1), (1, 0)]) for halo in halos]  2.09 us
  transfers between devices with their start and end apart: 24, of which 15 were waited for; matrix products, arithmetic and copies ran while one was open for 0% of the time, Pallas kernels for 21%

profile of v7, /device:TPU:0, one launch (start us, length us, event | category | flops | bytes accessed | tf_op | source)
XLA Modules:
  0.0 81.7 jit_solution(3700293438601027202)
XLA Ops:
  0.6 4.3 %shard_map.69 = (f32[24,16]{1,0:T(8,128)}, f32[24,16]{1,0:T(8,128)}, f32[24,16]{1,0:T(8,128)}) custom-call(f32[6144,128]{1,0:T(8,128)} %bitcast.18, f32[6,8192]{1,0:T(8,128)} %far_perturb_ref.1), custom_call_target="tpu_custom_call" | custom-call | tf_op jit(solution)/shard_map/pallas_call | solution.py:32
  5.0 4.1 %collective-permute-start.1 = (f32[24,16]{1,0:T(8,128)}, f32[24,16]{1,0:T(8,128)S(1)}, u32[]{:S(2)}, u32[]{:S(2)}) collective-permute-start(f32[24,16]{1,0:T(8,128)} %get-tuple-element.52), channel_id=1, source_target_pairs={{0,8},{4,12},{8,0},{12,4},{1,9},{5,13},{9,1},{13,5},{2,10},{6,14},... | collective-permute-start | bytes 4616 | tf_op jit(solution)/shard_map/ppermute | solution.py:53
  9.1 1.3 %collective-permute-start.2 = (f32[24,16]{1,0:T(8,128)}, f32[24,16]{1,0:T(8,128)S(1)}, u32[]{:S(2)}, u32[]{:S(2)}) collective-permute-start(f32[24,16]{1,0:T(8,128)} %get-tuple-element.53), channel_id=1, source_target_pairs={{0,12},{4,8},{8,4},{12,0},{1,13},{5,9},{9,5},{13,1},{2,14},{6,10},... | collective-permute-start | bytes 4616 | tf_op jit(solution)/shard_map/ppermute | solution.py:53
  10.4 0.2 collective-permute-start
  10.6 0.9 %copy-done.2 = f32[6,8192]{1,0:T(8,128)S(1)} copy-done((f32[6,8192]{1,0:T(8,128)S(1)}, f32[6,8192]{1,0:T(8,128)}, u32[]{:S(2)}) %copy-start.2) | copy-done | bytes 196632
  11.6 1.2 %shard_map.68 = (f32[16,6,8,8,128]{4,3,2,1,0:T(8,128)S(1)}, f32[6,8,8,128]{3,2,1,0:T(8,128)S(1)}, f32[6,8,8,128]{3,2,1,0:T(8,128)S(1)}) custom-call(f32[6144,128]{1,0:T(8,128)S(1)} %bitcast.19, f32[6,8192]{1,0:T(8,128)S(1)} %copy-done.1, f32[6,8192]{1,0:T(8,128)S(1)} %copy-done.2), custom_call_target="tpu_custom_call" | custom-call | tf_op jit(solution)/shard_map/pallas_call | solution.py:32
  12.8 0.0 collective-permute-done.1.refs_2_
  12.9 1.9 %collective-permute-done.2.refs_3_ = f32[24,16]{1,0:T(8,128)S(1)} collective-permute-done((f32[24,16]{1,0:T(8,128)}, f32[24,16]{1,0:T(8,128)S(1)}, u32[]{:S(2)}, u32[]{:S(2)}) %collective-permute-start.2) | collective-permute-done | bytes 1568 | tf_op jit(solution)/shard_map/ppermute | solution.py:53
  14.8 0.0 collective-permute-done.refs_1_
  14.8 0.6 shard_map.70
  15.4 2.1 %collective-permute-start.4 = (f32[4,6,3,8,128]{4,3,2,1,0:T(8,128)S(1)}, f32[4,6,3,8,128]{4,3,2,1,0:T(8,128)S(1)}, u32[]{:S(2)}, u32[]{:S(2)}) collective-permute-start(f32[4,6,3,8,128]{4,3,2,1,0:T(8,128)S(1)} %get-tuple-element.54.shared_ref), channel_id=1, source_target_pairs={{0,12},{4,0},{8,4},{12,8},{1,13},{5,1},{9,5},{13,9},{2,14},{6,2},{... | collective-permute-start | bytes 884744 | tf_op jit(solution)/shard_map/ppermute | solution.py:68
  17.5 0.0 collective-permute-start.3
  17.5 0.3 shard_map.71.rest_ref
  17.8 0.1 collective-permute-start.8
  17.8 3.9 %collective-permute-start.7 = (f32[4,6,2,8,128]{4,3,2,1,0:T(8,128)S(1)}, f32[4,6,2,8,128]{4,3,2,1,0:T(8,128)S(1)}, u32[]{:S(2)}, u32[]{:S(2)}) collective-permute-start(f32[4,6,2,8,128]{4,3,2,1,0:T(8,128)S(1)} %shard_map.71.rest_ref), channel_id=1, source_target_pairs={{0,12},{4,0},{8,4},{12,8},{1,13},{5,1},{9,5},{13,9},{2,14},{6,2},{... | collective-permute-start | bytes 589832 | tf_op jit(solution)/shard_map/ppermute | solution.py:68
  22.4 6.9 %shard_map.72 = (f32[4,6,8,8,128]{4,3,2,1,0:T(8,128)S(1)}, f32[4,6,8,8,128]{4,3,2,1,0:T(8,128)S(1)}, f32[4,6,8,8,128]{4,3,2,1,0:T(8,128)S(1)}, f32[16,16,128]{2,...) custom-call(f32[1]{0:T(128)S(6)} %copy.8.omega_ref, f32[4]{0:T(128)S(1)} %copy-done.4, ...), custom_call_target="tpu_custom_call" | custom-call | tf_op jit(solution)/shard_map/pallas_call | solution.py:32
  29.3 4.9 %collective-permute-done.4.after_ref = f32[4,6,3,8,128]{4,3,2,1,0:T(8,128)S(1)} collective-permute-done((f32[4,6,3,8,128]{4,3,2,1,0:T(8,128)S(1)}, f32[4,6,3,8,128]{4,3,2,1,0:T(8,128)S(1)}, u32[]{:S(2)}, u32[]{:S(2)}) %collective-permute-start.4) | collective-permute-done | bytes 294944 | tf_op jit(solution)/shard_map/ppermute | solution.py:68
  34.1 0.1 shard_map.73
  34.3 1.6 %collective-permute-start.6 = (f32[2,6,3,8,128]{4,3,2,1,0:T(8,128)S(1)}, f32[2,6,3,8,128]{4,3,2,1,0:T(8,128)S(1)}, u32[]{:S(2)}, u32[]{:S(2)}) collective-permute-start(f32[2,6,3,8,128]{4,3,2,1,0:T(8,128)S(1)} %get-tuple-element.60.refs_0_), channel_id=1, source_target_pairs={{0,16},{16,0},{1,17},{17,1},{2,18},{18,2},{3,19},{19,3},{4,20},{20... | collective-permute-start | bytes 442376 | tf_op jit(solution)/shard_map/ppermute | solution.py:713
  35.9 0.5 collective-permute-start.5
  36.4 0.5 shard_map.74
  36.8 2.6 %collective-permute-done.6.refs_1_ = f32[2,6,3,8,128]{4,3,2,1,0:T(8,128)S(1)} collective-permute-done((f32[2,6,3,8,128]{4,3,2,1,0:T(8,128)S(1)}, f32[2,6,3,8,128]{4,3,2,1,0:T(8,128)S(1)}, u32[]{:S(2)}, u32[]{:S(2)}) %collective-permute-start.6) | collective-permute-done | bytes 147488 | tf_op jit(solution)/shard_map/ppermute | solution.py:713
  39.5 1.6 %collective-permute-done.5.refs_0_ = f32[2,6,3,8,128]{4,3,2,1,0:T(8,128)S(1)} collective-permute-done((f32[2,6,3,8,128]{4,3,2,1,0:T(8,128)S(1)}, f32[2,6,3,8,128]{4,3,2,1,0:T(8,128)S(1)}, u32[]{:S(2)}, u32[]{:S(2)}) %collective-permute-start.5) | collective-permute-done | bytes 147488 | tf_op jit(solution)/shard_map/ppermute | solution.py:713
  41.1 0.5 shard_map.75
  41.6 0.0 collective-permute-done.8.before_ref
  41.6 0.5 shard_map.76
  42.2 0.1 collective-permute-start.10
  42.2 2.7 %collective-permute-start.11 = (f32[8,128]{1,0:T(8,128)S(1)}, f32[8,128]{1,0:T(8,128)S(1)}, u32[]{:S(2)}, u32[]{:S(2)}) collective-permute-start(f32[8,128]{1,0:T(8,128)S(1)} %get-tuple-element.71), channel_id=1, source_target_pairs={{0,12},{4,8},{8,4},{12,0},{1,13},{5,9},{9,5},{13,1},{2,14},{6,10},... | collective-permute-start | bytes 12296 | tf_op jit(solution)/shard_map/ppermute | solution.py:53
  44.9 0.8 collective-permute-start.9
  45.7 1.1 %collective-permute-done.10.refs_2_ = f32[8,128]{1,0:T(8,128)S(1)} collective-permute-done((f32[8,128]{1,0:T(8,128)S(1)}, f32[8,128]{1,0:T(8,128)S(1)}, u32[]{:S(2)}, u32[]{:S(2)}) %collective-permute-start.10) | collective-permute-done | bytes 4128 | tf_op jit(solution)/shard_map/ppermute | solution.py:53
  46.8 1.0 %collective-permute-done.11.refs_3_ = f32[8,128]{1,0:T(8,128)S(1)} collective-permute-done((f32[8,128]{1,0:T(8,128)S(1)}, f32[8,128]{1,0:T(8,128)S(1)}, u32[]{:S(2)}, u32[]{:S(2)}) %collective-permute-start.11) | collective-permute-done | bytes 4128 | tf_op jit(solution)/shard_map/ppermute | solution.py:53
  47.8 0.8 %collective-permute-done.9.refs_1_ = f32[8,128]{1,0:T(8,128)S(1)} collective-permute-done((f32[8,128]{1,0:T(8,128)S(1)}, f32[8,128]{1,0:T(8,128)S(1)}, u32[]{:S(2)}, u32[]{:S(2)}) %collective-permute-start.9) | collective-permute-done | bytes 4128 | tf_op jit(solution)/shard_map/ppermute | solution.py:53
  48.6 0.4 shard_map.80
  49.1 1.9 %collective-permute-start.15 = (f32[1,6,8,8,128]{4,3,2,1,0:T(8,128)S(1)}, f32[1,6,8,8,128]{4,3,2,1,0:T(8,128)S(1)}, u32[]{:S(2)}, u32[]{:S(2)}) collective-permute-start(f32[1,6,8,8,128]{4,3,2,1,0:T(8,128)S(1)} %get-tuple-element.75.refs_3_), channel_id=1, source_target_pairs={{0,12},{4,0},{8,4},{12,8},{1,13},{5,1},{9,5},{13,9},{2,14},{6,2},{... | collective-permute-start | bytes 589832 | tf_op jit(solution)/shard_map/ppermute | solution.py:68
  50.9 0.4 shard_map.79
  51.4 0.2 collective-permute-start.14
  51.6 0.4 shard_map.77
  52.0 1.8 %collective-permute-start.12 = (f32[1,6,8,8,128]{4,3,2,1,0:T(8,128)S(1)}, f32[1,6,8,8,128]{4,3,2,1,0:T(8,128)S(1)}, u32[]{:S(2)}, u32[]{:S(2)}) collective-permute-start(f32[1,6,8,8,128]{4,3,2,1,0:T(8,128)S(1)} %get-tuple-element.72.refs_0_), channel_id=1, source_target_pairs={{0,12},{4,0},{8,4},{12,8},{1,13},{5,1},{9,5},{13,9},{2,14},{6,2},{... | collective-permute-start | bytes 589832 | tf_op jit(solution)/shard_map/ppermute | solution.py:68
  53.8 0.4 shard_map.78
  54.2 1.3 %collective-permute-start.13 = (f32[1,6,8,8,128]{4,3,2,1,0:T(8,128)S(1)}, f32[1,6,8,8,128]{4,3,2,1,0:T(8,128)S(1)}, u32[]{:S(2)}, u32[]{:S(2)}) collective-permute-start(f32[1,6,8,8,128]{4,3,2,1,0:T(8,128)S(1)} %get-tuple-element.73.refs_1_), channel_id=1, source_target_pairs={{0,12},{4,0},{8,4},{12,8},{1,13},{5,1},{9,5},{13,9},{2,14},{6,2},{... | collective-permute-start | bytes 589832 | tf_op jit(solution)/shard_map/ppermute | solution.py:68
  55.5 5.3 %shard_map.81 = (f32[4,6,8,8,128]{4,3,2,1,0:T(8,128)S(1)}, f32[12,8,128]{2,1,0:T(8,128)S(1)}) custom-call(f32[1]{0:T(128)S(6)} %copy.8.omega_ref, f32[4]{0:T(128)S(1)} %copy-done.4, f32[16,6,8,8,128]{4,3,2,1,0:T(8,128)S(1)} %get-tuple-element.48.planes_ref, f32[6,8,8,128]{3,2,1,0:T(8,128)S(1)} %get-tuple-element.50.potential_ref, ...), custom_call_target="tpu_custom_call" | custom-call | tf_op jit(solution)/shard_map/pallas_call | solution.py:32
  60.9 0.0 collective-permute-done.15.refs_7_
  60.9 0.0 collective-permute-done.14.refs_6_
  60.9 0.7 collective-permute-done.13.refs_5_
  61.6 0.3 shard_map.82
  61.9 1.5 %collective-permute-start.17 = (f32[8,128]{1,0:T(8,128)S(1)}, f32[8,128]{1,0:T(8,128)S(1)}, u32[]{:S(2)}, u32[]{:S(2)}) collective-permute-start(f32[8,128]{1,0:T(8,128)S(1)} %get-tuple-element.87), channel_id=1, source_target_pairs={{0,8},{4,12},{8,0},{12,4},{1,9},{5,13},{9,1},{13,5},{2,10},{6,14},... | collective-permute-start | bytes 12296 | tf_op jit(solution)/shard_map/ppermute | solution.py:53
  63.4 2.3 %collective-permute-start.18 = (f32[8,128]{1,0:T(8,128)S(1)}, f32[8,128]{1,0:T(8,128)S(1)}, u32[]{:S(2)}, u32[]{:S(2)}) collective-permute-start(f32[8,128]{1,0:T(8,128)S(1)} %get-tuple-element.88), channel_id=1, source_target_pairs={{0,12},{4,8},{8,4},{12,0},{1,13},{5,9},{9,5},{13,1},{2,14},{6,10},... | collective-permute-start | bytes 12296 | tf_op jit(solution)/shard_map/ppermute | solution.py:53
  65.7 0.5 collective-permute-start.16
  66.2 0.2 collective-permute-done.17.refs_2_
  66.5 2.4 %collective-permute-done.18.refs_3_ = f32[8,128]{1,0:T(8,128)S(1)} collective-permute-done((f32[8,128]{1,0:T(8,128)S(1)}, f32[8,128]{1,0:T(8,128)S(1)}, u32[]{:S(2)}, u32[]{:S(2)}) %collective-permute-start.18) | collective-permute-done | bytes 4128 | tf_op jit(solution)/shard_map/ppermute | solution.py:53
  68.8 0.5 collective-permute-done.16.refs_1_
  69.3 0.3 shard_map.83
  69.7 0.1 collective-permute-start.21
  69.8 1.5 %collective-permute-start.20 = (f32[144,128]{1,0:T(8,128)S(1)}, f32[144,128]{1,0:T(8,128)S(1)}, u32[]{:S(2)}, u32[]{:S(2)}) collective-permute-start(f32[144,128]{1,0:T(8,128)S(1)} %get-tuple-element.95), channel_id=1, source_target_pairs={{0,2},{1,3},{2,0},{3,1},{4,6},{5,7},{6,4},{7,5},{8,10},{9,11},{10,... | collective-permute-start | bytes 221192 | tf_op jit(solution)/shard_map/ppermute | solution.py:68
  71.3 1.4 %collective-permute-start.19 = (f32[144,128]{1,0:T(8,128)S(1)}, f32[144,128]{1,0:T(8,128)S(1)}, u32[]{:S(2)}, u32[]{:S(2)}) collective-permute-start(f32[144,128]{1,0:T(8,128)S(1)} %get-tuple-element.96), channel_id=1, source_target_pairs={{0,3},{1,0},{2,1},{3,2},{4,7},{5,4},{6,5},{7,6},{8,11},{9,8},{10,9... | collective-permute-start | bytes 221192 | tf_op jit(solution)/shard_map/ppermute | solution.py:68
  72.7 1.0 %collective-permute-done.21.refs_2_ = f32[144,128]{1,0:T(8,128)S(1)} collective-permute-done((f32[144,128]{1,0:T(8,128)S(1)}, f32[144,128]{1,0:T(8,128)S(1)}, u32[]{:S(2)}, u32[]{:S(2)}) %collective-permute-start.21) | collective-permute-done | bytes 73760 | tf_op jit(solution)/shard_map/ppermute | solution.py:68
  73.7 1.1 %collective-permute-done.20.refs_1_ = f32[144,128]{1,0:T(8,128)S(1)} collective-permute-done((f32[144,128]{1,0:T(8,128)S(1)}, f32[144,128]{1,0:T(8,128)S(1)}, u32[]{:S(2)}, u32[]{:S(2)}) %collective-permute-start.20) | collective-permute-done | bytes 73760 | tf_op jit(solution)/shard_map/ppermute | solution.py:68
  74.8 0.1 collective-permute-done.19.refs_0_
  74.9 0.6 collective-permute-start.22
  75.5 3.3 %collective-permute-start.23 = (f32[48,128]{1,0:T(8,128)S(1)}, f32[48,128]{1,0:T(8,128)S(1)}, u32[]{:S(2)}, u32[]{:S(2)}) collective-permute-start(f32[48,128]{1,0:T(8,128)S(1)} %get-tuple-element.93), channel_id=1, source_target_pairs={{0,12},{4,0},{8,4},{12,8},{1,13},{5,1},{9,5},{13,9},{2,14},{6,2},{... | collective-permute-start | bytes 73736 | tf_op jit(solution)/shard_map/ppermute | solution.py:68
  78.8 1.1 %shard_map.84 = f32[1536,128]{1,0:T(8,128)} custom-call(f32[4,6,8,8,128]{4,3,2,1,0:T(8,128)S(1)} %get-tuple-element.56.source_ref, f32[4,6,8,8,128]{4,3,2,1,0:T(8,128)S(1)} %get-tuple-element.84.residual_ref, f32[8,128]{1,0:T(8,128)S(1)} %get-tuple-element.89.scales_ref), custom_call_target="tpu_custom_call" | custom-call | tf_op jit(solution)/shard_map/pallas_call | solution.py:32
  79.9 1.0 %collective-permute-done.22.before_ref = f32[48,128]{1,0:T(8,128)S(1)} collective-permute-done((f32[48,128]{1,0:T(8,128)S(1)}, f32[48,128]{1,0:T(8,128)S(1)}, u32[]{:S(2)}, u32[]{:S(2)}) %collective-permute-start.22) | collective-permute-done | bytes 24608 | tf_op jit(solution)/shard_map/ppermute | solution.py:68
  80.9 0.0 collective-permute-done.23.after_ref
  80.9 0.9 %shard_map.86 = f32[6,2048]{1,0:T(8,128)} custom-call(f32[144,128]{1,0:T(8,128)S(1)} %get-tuple-element.91.dense_ref, f32[48,128]{1,0:T(8,128)S(1)} %collective-permute-done.22.before_ref, f32[48,128]{1,0:T(8,128)S(1)} %collective-permute-done.23.after_ref), custom_call_target="tpu_custom_call" | custom-call | tf_op jit(solution)/shard_map/pallas_call | solution.py:32
  (14 shorter events, 0.1 us)
Async XLA Ops:
  0.6 10.0 %copy-start.1 = (f32[6,8192]{1,0:T(8,128)S(1)}, f32[6,8192]{1,0:T(8,128)}, u32[]{:S(2)}) copy-start(f32[6,8192]{1,0:T(8,128)} %far_perturb_ref.1) | copy-start | bytes 589828
  0.6 10.0 %copy-start = (f32[16,6,8192]{2,0,1:T(8,128)S(1)}, f32[16,6,8192]{2,0,1:T(8,128)}, u32[]{:S(2)}) copy-start(f32[16,6,8192]{2,0,1:T(8,128)} %param.5) | copy-start | bytes 9437188
  5.0 7.9 %collective-permute-start.1 = (f32[24,16]{1,0:T(8,128)}, f32[24,16]{1,0:T(8,128)S(1)}, u32[]{:S(2)}, u32[]{:S(2)}) collective-permute-start(f32[24,16]{1,0:T(8,128)} %get-tuple-element.52), channel_id=1, source_target_pairs={{0,8},{4,12},{8,0},{12,4},{1,9},{5,13},{9,1},{13,5},{2,10},{6,14},... | collective-permute-start | bytes 4616 | tf_op jit(solution)/shard_map/ppermute | solution.py:53
  9.1 5.7 %collective-permute-start.2 = (f32[24,16]{1,0:T(8,128)}, f32[24,16]{1,0:T(8,128)S(1)}, u32[]{:S(2)}, u32[]{:S(2)}) collective-permute-start(f32[24,16]{1,0:T(8,128)} %get-tuple-element.53), channel_id=1, source_target_pairs={{0,12},{4,8},{8,4},{12,0},{1,13},{5,9},{9,5},{13,1},{2,14},{6,10},... | collective-permute-start | bytes 4616 | tf_op jit(solution)/shard_map/ppermute | solution.py:53
  10.4 4.4 %collective-permute-start = (f32[24,16]{1,0:T(8,128)}, f32[24,16]{1,0:T(8,128)S(1)}, u32[]{:S(2)}, u32[]{:S(2)}) collective-permute-start(f32[24,16]{1,0:T(8,128)} %get-tuple-element.51.refs_0_), channel_id=1, source_target_pairs={{0,4},{4,0},{8,12},{12,8},{1,5},{5,1},{9,13},{13,9},{2,6},{6,2},{1... | collective-permute-start | bytes 4616 | tf_op jit(solution)/shard_map/ppermute | solution.py:53
  10.6 1.0 %copy-start.2 = (f32[6,8192]{1,0:T(8,128)S(1)}, f32[6,8192]{1,0:T(8,128)}, u32[]{:S(2)}) copy-start(f32[6,8192]{1,0:T(8,128)} %potential_ref.1) | copy-start | bytes 589828
  11.6 3.2 %copy-start.3 = (f32[24,16]{1,0:T(8,128)S(1)}, f32[24,16]{1,0:T(8,128)}, u32[]{:S(2)}) copy-start(f32[24,16]{1,0:T(8,128)} %get-tuple-element.51.refs_0_) | copy-start | bytes 4612
  14.8 7.6 %copy-start.4 = (f32[4]{0:T(128)S(1)}, f32[4]{0:T(128)}, u32[]{:S(2)}) copy-start(f32[4]{0:T(128)} %energies_ref.3) | copy-start | bytes 52
  15.4 18.8 %collective-permute-start.4 = (f32[4,6,3,8,128]{4,3,2,1,0:T(8,128)S(1)}, f32[4,6,3,8,128]{4,3,2,1,0:T(8,128)S(1)}, u32[]{:S(2)}, u32[]{:S(2)}) collective-permute-start(f32[4,6,3,8,128]{4,3,2,1,0:T(8,128)S(1)} %get-tuple-element.54.shared_ref), channel_id=1, source_target_pairs={{0,12},{4,0},{8,4},{12,8},{1,13},{5,1},{9,5},{13,9},{2,14},{6,2},{... | collective-permute-start | bytes 884744 | tf_op jit(solution)/shard_map/ppermute | solution.py:68
  17.5 16.7 %collective-permute-start.3 = (f32[4,6,3,8,128]{4,3,2,1,0:T(8,128)S(1)}, f32[4,6,3,8,128]{4,3,2,1,0:T(8,128)S(1)}, u32[]{:S(2)}, u32[]{:S(2)}) collective-permute-start(f32[4,6,3,8,128]{4,3,2,1,0:T(8,128)S(1)} %get-tuple-element.54.shared_ref), channel_id=1, source_target_pairs={{0,4},{4,8},{8,12},{12,0},{1,5},{5,9},{9,13},{13,1},{2,6},{6,10},{... | collective-permute-start | bytes 884744 | tf_op jit(solution)/shard_map/ppermute | solution.py:68
  17.8 23.8 %collective-permute-start.8 = (f32[4,6,2,8,128]{4,3,2,1,0:T(8,128)S(1)}, f32[4,6,2,8,128]{4,3,2,1,0:T(8,128)S(1)}, u32[]{:S(2)}, u32[]{:S(2)}) collective-permute-start(f32[4,6,2,8,128]{4,3,2,1,0:T(8,128)S(1)} %shard_map.71.rest_ref), channel_id=1, source_target_pairs={{0,4},{4,8},{8,12},{12,0},{1,5},{5,9},{9,13},{13,1},{2,6},{6,10},{... | collective-permute-start | bytes 589832 | tf_op jit(solution)/shard_map/ppermute | solution.py:68
  17.8 23.8 %collective-permute-start.7 = (f32[4,6,2,8,128]{4,3,2,1,0:T(8,128)S(1)}, f32[4,6,2,8,128]{4,3,2,1,0:T(8,128)S(1)}, u32[]{:S(2)}, u32[]{:S(2)}) collective-permute-start(f32[4,6,2,8,128]{4,3,2,1,0:T(8,128)S(1)} %shard_map.71.rest_ref), channel_id=1, source_target_pairs={{0,12},{4,0},{8,4},{12,8},{1,13},{5,1},{9,5},{13,9},{2,14},{6,2},{... | collective-permute-start | bytes 589832 | tf_op jit(solution)/shard_map/ppermute | solution.py:68
  34.3 5.2 %collective-permute-start.6 = (f32[2,6,3,8,128]{4,3,2,1,0:T(8,128)S(1)}, f32[2,6,3,8,128]{4,3,2,1,0:T(8,128)S(1)}, u32[]{:S(2)}, u32[]{:S(2)}) collective-permute-start(f32[2,6,3,8,128]{4,3,2,1,0:T(8,128)S(1)} %get-tuple-element.60.refs_0_), channel_id=1, source_target_pairs={{0,16},{16,0},{1,17},{17,1},{2,18},{18,2},{3,19},{19,3},{4,20},{20... | collective-permute-start | bytes 442376 | tf_op jit(solution)/shard_map/ppermute | solution.py:713
  35.9 5.2 %collective-permute-start.5 = (f32[2,6,3,8,128]{4,3,2,1,0:T(8,128)S(1)}, f32[2,6,3,8,128]{4,3,2,1,0:T(8,128)S(1)}, u32[]{:S(2)}, u32[]{:S(2)}) collective-permute-start(f32[2,6,3,8,128]{4,3,2,1,0:T(8,128)S(1)} %get-tuple-element.61.refs_1_), channel_id=1, source_target_pairs={{0,16},{16,0},{1,17},{17,1},{2,18},{18,2},{3,19},{19,3},{4,20},{20... | collective-permute-start | bytes 442376 | tf_op jit(solution)/shard_map/ppermute | solution.py:713
  42.2 4.7 %collective-permute-start.10 = (f32[8,128]{1,0:T(8,128)S(1)}, f32[8,128]{1,0:T(8,128)S(1)}, u32[]{:S(2)}, u32[]{:S(2)}) collective-permute-start(f32[8,128]{1,0:T(8,128)S(1)} %get-tuple-element.70), channel_id=1, source_target_pairs={{0,8},{4,12},{8,0},{12,4},{1,9},{5,13},{9,1},{13,5},{2,10},{6,14},... | collective-permute-start | bytes 12296 | tf_op jit(solution)/shard_map/ppermute | solution.py:53
  42.2 5.6 %collective-permute-start.11 = (f32[8,128]{1,0:T(8,128)S(1)}, f32[8,128]{1,0:T(8,128)S(1)}, u32[]{:S(2)}, u32[]{:S(2)}) collective-permute-start(f32[8,128]{1,0:T(8,128)S(1)} %get-tuple-element.71), channel_id=1, source_target_pairs={{0,12},{4,8},{8,4},{12,0},{1,13},{5,9},{9,5},{13,1},{2,14},{6,10},... | collective-permute-start | bytes 12296 | tf_op jit(solution)/shard_map/ppermute | solution.py:53
  44.9 3.7 %collective-permute-start.9 = (f32[8,128]{1,0:T(8,128)S(1)}, f32[8,128]{1,0:T(8,128)S(1)}, u32[]{:S(2)}, u32[]{:S(2)}) collective-permute-start(f32[8,128]{1,0:T(8,128)S(1)} %get-tuple-element.69.refs_0_), channel_id=1, source_target_pairs={{0,4},{4,0},{8,12},{12,8},{1,5},{5,1},{9,13},{13,9},{2,6},{6,2},{1... | collective-permute-start | bytes 12296 | tf_op jit(solution)/shard_map/ppermute | solution.py:53
  49.1 11.8 %collective-permute-start.15 = (f32[1,6,8,8,128]{4,3,2,1,0:T(8,128)S(1)}, f32[1,6,8,8,128]{4,3,2,1,0:T(8,128)S(1)}, u32[]{:S(2)}, u32[]{:S(2)}) collective-permute-start(f32[1,6,8,8,128]{4,3,2,1,0:T(8,128)S(1)} %get-tuple-element.75.refs_3_), channel_id=1, source_target_pairs={{0,12},{4,0},{8,4},{12,8},{1,13},{5,1},{9,5},{13,9},{2,14},{6,2},{... | collective-permute-start | bytes 589832 | tf_op jit(solution)/shard_map/ppermute | solution.py:68
  51.4 9.5 %collective-permute-start.14 = (f32[1,6,8,8,128]{4,3,2,1,0:T(8,128)S(1)}, f32[1,6,8,8,128]{4,3,2,1,0:T(8,128)S(1)}, u32[]{:S(2)}, u32[]{:S(2)}) collective-permute-start(f32[1,6,8,8,128]{4,3,2,1,0:T(8,128)S(1)} %get-tuple-element.74.refs_2_), channel_id=1, source_target_pairs={{0,12},{4,0},{8,4},{12,8},{1,13},{5,1},{9,5},{13,9},{2,14},{6,2},{... | collective-permute-start | bytes 589832 | tf_op jit(solution)/shard_map/ppermute | solution.py:68
  52.0 8.9 %collective-permute-start.12 = (f32[1,6,8,8,128]{4,3,2,1,0:T(8,128)S(1)}, f32[1,6,8,8,128]{4,3,2,1,0:T(8,128)S(1)}, u32[]{:S(2)}, u32[]{:S(2)}) collective-permute-start(f32[1,6,8,8,128]{4,3,2,1,0:T(8,128)S(1)} %get-tuple-element.72.refs_0_), channel_id=1, source_target_pairs={{0,12},{4,0},{8,4},{12,8},{1,13},{5,1},{9,5},{13,9},{2,14},{6,2},{... | collective-permute-start | bytes 589832 | tf_op jit(solution)/shard_map/ppermute | solution.py:68
  54.2 7.4 %collective-permute-start.13 = (f32[1,6,8,8,128]{4,3,2,1,0:T(8,128)S(1)}, f32[1,6,8,8,128]{4,3,2,1,0:T(8,128)S(1)}, u32[]{:S(2)}, u32[]{:S(2)}) collective-permute-start(f32[1,6,8,8,128]{4,3,2,1,0:T(8,128)S(1)} %get-tuple-element.73.refs_1_), channel_id=1, source_target_pairs={{0,12},{4,0},{8,4},{12,8},{1,13},{5,1},{9,5},{13,9},{2,14},{6,2},{... | collective-permute-start | bytes 589832 | tf_op jit(solution)/shard_map/ppermute | solution.py:68
  61.9 4.5 %collective-permute-start.17 = (f32[8,128]{1,0:T(8,128)S(1)}, f32[8,128]{1,0:T(8,128)S(1)}, u32[]{:S(2)}, u32[]{:S(2)}) collective-permute-start(f32[8,128]{1,0:T(8,128)S(1)} %get-tuple-element.87), channel_id=1, source_target_pairs={{0,8},{4,12},{8,0},{12,4},{1,9},{5,13},{9,1},{13,5},{2,10},{6,14},... | collective-permute-start | bytes 12296 | tf_op jit(solution)/shard_map/ppermute | solution.py:53
  63.4 5.4 %collective-permute-start.18 = (f32[8,128]{1,0:T(8,128)S(1)}, f32[8,128]{1,0:T(8,128)S(1)}, u32[]{:S(2)}, u32[]{:S(2)}) collective-permute-start(f32[8,128]{1,0:T(8,128)S(1)} %get-tuple-element.88), channel_id=1, source_target_pairs={{0,12},{4,8},{8,4},{12,0},{1,13},{5,9},{9,5},{13,1},{2,14},{6,10},... | collective-permute-start | bytes 12296 | tf_op jit(solution)/shard_map/ppermute | solution.py:53
  65.7 3.6 %collective-permute-start.16 = (f32[8,128]{1,0:T(8,128)S(1)}, f32[8,128]{1,0:T(8,128)S(1)}, u32[]{:S(2)}, u32[]{:S(2)}) collective-permute-start(f32[8,128]{1,0:T(8,128)S(1)} %get-tuple-element.86.refs_0_), channel_id=1, source_target_pairs={{0,4},{4,0},{8,12},{12,8},{1,5},{5,1},{9,13},{13,9},{2,6},{6,2},{1... | collective-permute-start | bytes 12296 | tf_op jit(solution)/shard_map/ppermute | solution.py:53
  69.7 4.0 %collective-permute-start.21 = (f32[144,128]{1,0:T(8,128)S(1)}, f32[144,128]{1,0:T(8,128)S(1)}, u32[]{:S(2)}, u32[]{:S(2)}) collective-permute-start(f32[144,128]{1,0:T(8,128)S(1)} %get-tuple-element.94), channel_id=1, source_target_pairs={{0,1},{1,2},{2,3},{3,0},{4,5},{5,6},{6,7},{7,4},{8,9},{9,10},{10,1... | collective-permute-start | bytes 221192 | tf_op jit(solution)/shard_map/ppermute | solution.py:68
  69.8 5.0 %collective-permute-start.20 = (f32[144,128]{1,0:T(8,128)S(1)}, f32[144,128]{1,0:T(8,128)S(1)}, u32[]{:S(2)}, u32[]{:S(2)}) collective-permute-start(f32[144,128]{1,0:T(8,128)S(1)} %get-tuple-element.95), channel_id=1, source_target_pairs={{0,2},{1,3},{2,0},{3,1},{4,6},{5,7},{6,4},{7,5},{8,10},{9,11},{10,... | collective-permute-start | bytes 221192 | tf_op jit(solution)/shard_map/ppermute | solution.py:68
  71.3 3.6 %collective-permute-start.19 = (f32[144,128]{1,0:T(8,128)S(1)}, f32[144,128]{1,0:T(8,128)S(1)}, u32[]{:S(2)}, u32[]{:S(2)}) collective-permute-start(f32[144,128]{1,0:T(8,128)S(1)} %get-tuple-element.96), channel_id=1, source_target_pairs={{0,3},{1,0},{2,1},{3,2},{4,7},{5,4},{6,5},{7,6},{8,11},{9,8},{10,9... | collective-permute-start | bytes 221192 | tf_op jit(solution)/shard_map/ppermute | solution.py:68
  74.9 5.9 %collective-permute-start.22 = (f32[48,128]{1,0:T(8,128)S(1)}, f32[48,128]{1,0:T(8,128)S(1)}, u32[]{:S(2)}, u32[]{:S(2)}) collective-permute-start(f32[48,128]{1,0:T(8,128)S(1)} %get-tuple-element.92), channel_id=1, source_target_pairs={{0,4},{4,8},{8,12},{12,0},{1,5},{5,9},{9,13},{13,1},{2,6},{6,10},{... | collective-permute-start | bytes 73736 | tf_op jit(solution)/shard_map/ppermute | solution.py:68
  75.5 5.4 %collective-permute-start.23 = (f32[48,128]{1,0:T(8,128)S(1)}, f32[48,128]{1,0:T(8,128)S(1)}, u32[]{:S(2)}, u32[]{:S(2)}) collective-permute-start(f32[48,128]{1,0:T(8,128)S(1)} %get-tuple-element.93), channel_id=1, source_target_pairs={{0,12},{4,0},{8,4},{12,8},{1,13},{5,1},{9,5},{13,9},{2,14},{6,2},{... | collective-permute-start | bytes 73736 | tf_op jit(solution)/shard_map/ppermute | solution.py:68
